TPU v7x, 256 devices: a whole 4x4x8 slice. The times are simulated.
256 devices in a mesh: dp: 64 (over z, x, core), expert: 4 (over y).
Axes of the slice: x: 4, y: 4, z: 8, core: 2. Of those that a mesh axis runs over, the one named last changes fastest.
Arguments:
- tokens: bfloat16 [32768, 4096], P(('dp', 'expert')), may hold values from -6 to 6
- grad_out: bfloat16 [32768, 4096], P(('dp', 'expert')), may hold values from -6 to 6
- experts: int32 [32768, 2], P(('dp', 'expert')), may hold values from 0 to 7, all different within a row; in each aligned block of 128 rows (0 to 127, 128 to 255, ...) at most 64 rows name the same one
- gates: bfloat16 [32768, 2], P(('dp', 'expert')), may hold values from 0 to 1, as said below
- router_weight: bfloat16 [8, 4096], replicated, may hold values from -3 to 3
- saved_outputs: bfloat16 [131072, 4096], P(('dp', 'expert')), may hold values from -0.19921875 to 0.19921875
Outputs:
- input_grad: bfloat16 [32768, 4096], P(('dp', 'expert'))
- router_grad: float32 [8, 4096], replicated
- expert_grad: bfloat16 [131072, 4096], P(('dp', 'expert'))
Inputs may be any that keep to these rules, and one draw needn't show every extreme that they name: Within each aligned block of 128 tokens (the tokens of one device), no expert is named by more than 64 slots, and in some blocks an expert is named by exactly 64 slots. The two experts of a token differ. The two gates of a token are positive and add up to one, up to rounding to bfloat16.
All inputs are finite; a program needn't handle non-finite values.
Results may differ from a plain program's by a relative error of at most 0.0085.
Values may be sent and summed in bfloat16 or wider, within the bound.
No kernel may reach another device: no remote copies, remote signals or barrier semaphores. Data moves between devices by JAX's collectives and lax.ppermute only.
A program may use at most 64 MiB of HBM per device.

v0:
```python
import jax
import jax.numpy as jnp
from jax import lax
from jax.sharding import Mesh
from jax.sharding import PartitionSpec as P

DP_EXPERT = ("dp_0", "dp_1", "dp_2", "expert")
DP = ("dp_0", "dp_1", "dp_2")


def side_by_side(arrays, axis, split_dim, concat_dim, along):
    columns = [a.reshape(*a.shape[:along], -1) for a in arrays]
    both = jnp.concatenate(columns, axis=along)
    filled, at, gathered = (
        lax.all_to_all(both, axis, split_axis=split_dim, concat_axis=concat_dim, tiled=True),
        0,
        [],
    )
    for a, column in zip(arrays, columns):
        section = filled[..., at : at + column.shape[along]]
        gathered.append(section.reshape(*section.shape[:along], *a.shape[along:]))
        at += column.shape[along]
    return tuple(gathered)


def split_up(shard, dim, length):
    before, after = (shard.shape[:dim], shard.shape[dim + 1 :])
    return jnp.moveaxis(shard.reshape(*before, length, -1, *after), dim, 0)


def sum_at_owner(shard, axis, dim):
    length = lax.axis_size(axis)
    blocks = lax.all_to_all(split_up(shard, dim, length), axis, 0, 0, tiled=True)
    return jnp.sum(blocks, axis=0)


def sum_in_two_steps(shard, axes, dim):
    far, near = axes
    blocks = split_up(shard, dim, lax.axis_size(far))
    nearer = sum_at_owner(blocks, near, dim + 1)
    arrived = lax.all_to_all(nearer, far, split_axis=0, concat_axis=0, tiled=True)
    return arrived.sum(axis=0)


def filled_up(lines, length):
    spare = -len(lines) % length
    return jnp.pad(lines, [(0, spare)] + [(0, 0)] * (lines.ndim - 1))


def copy_for_each(shard, axis):
    copies = jnp.broadcast_to(shard, (lax.axis_size(axis), *shard.shape))
    return lax.all_to_all(copies, axis, split_axis=0, concat_axis=0, tiled=True)


def laid_out(blocks, dim):
    lengths = list(blocks.shape[1:])
    lengths[dim] *= blocks.shape[0]
    return jnp.moveaxis(blocks, 0, dim).reshape(lengths)


def gather_axes(shard, axes, dim):
    far, near = axes
    blocks = copy_for_each(copy_for_each(shard, far), near)
    return laid_out(blocks.swapaxes(0, 1).reshape(-1, *shard.shape), dim)


def nested_sum(shard, axes):
    lines = shard.reshape(-1)
    own = sum_in_two_steps(
        filled_up(lines, lax.axis_size(axes[0]) * lax.axis_size(axes[1])), axes, 0
    )
    whole = gather_axes(own, axes, 0)
    return whole[: len(lines)].reshape(shard.shape)


def slot_positions(experts, count):
    slot_expert = experts.reshape(-1)
    onehot = (slot_expert[:, None] == jnp.arange(count, dtype=jnp.int32)[None, :]).astype(jnp.int32)
    before = jnp.cumsum(onehot, axis=0) - onehot
    return (slot_expert, jnp.sum(before * onehot, axis=1))


def local(tokens, grad_out, experts, gates, router_weight, saved_outputs):
    groups = lax.axis_size("expert")
    chosen_count = experts.shape[1]
    expert_count = router_weight.shape[0]
    held = expert_count // groups
    capacity = tokens.shape[0] // 2
    width = saved_outputs.shape[1]
    slot_expert, position = slot_positions(experts, expert_count)
    target = slot_expert % held * (groups * capacity) + slot_expert // held * capacity + position
    slot_gates = gates.reshape(-1)
    repeated = jnp.repeat(grad_out, chosen_count, axis=0)
    layout = (held, groups * capacity, width)
    outgoing = jnp.zeros(saved_outputs.shape, jnp.bfloat16).at[target].set(repeated)
    gate_rows = jnp.zeros((saved_outputs.shape[0],), jnp.bfloat16).at[target].set(slot_gates)
    arrived, arrived_gates = side_by_side(
        (outgoing.reshape(layout), gate_rows.reshape(held, groups * capacity)), "expert", 1, 1, 2
    )
    arrived = arrived.reshape(-1, width)
    arrived_gates = arrived_gates.reshape(-1)
    local_products = jnp.einsum(
        "sd,sd->s", arrived, saved_outputs, preferred_element_type=jnp.float32
    )
    expert_grad = (arrived_gates.astype(jnp.float32)[:, None] * arrived.astype(jnp.float32)).astype(
        jnp.bfloat16
    )
    homeward = lax.all_to_all(
        local_products.reshape(held, groups * capacity),
        "expert",
        split_axis=1,
        concat_axis=1,
        tiled=True,
    )
    products = homeward.reshape(-1)[target]
    gate_grad = products.reshape(-1, chosen_count)
    gate_values = gates.astype(jnp.float32)
    blended = jnp.sum(gate_values * gate_grad, axis=1, keepdims=True)
    slot_grad = gate_values * (gate_grad - blended)
    onehot = (
        experts[:, :, None] == jnp.arange(expert_count, dtype=jnp.int32)[None, None, :]
    ).astype(jnp.float32)
    logit_grad = jnp.sum(onehot * slot_grad[:, :, None], axis=1).astype(jnp.bfloat16)
    partial_value = lax.dot_general(
        logit_grad, tokens, (((0,), (0,)), ((), ())), preferred_element_type=jnp.float32
    )
    summed = nested_sum(partial_value, (("dp_0", "dp_1"), ("dp_2", "expert")))
    scale_factor = float(lax.axis_size(DP) * groups * tokens.shape[0]) ** (-0.5)
    router_grad = summed * scale_factor
    input_grad = jnp.dot(logit_grad, router_weight, preferred_element_type=jnp.float32).astype(
        jnp.bfloat16
    )
    return (input_grad, router_grad, expert_grad)


def solution(mesh):
    finer = Mesh(
        mesh.devices.reshape(8, 4, 2, mesh.shape["expert"]), ("dp_0", "dp_1", "dp_2", "expert")
    )
    return jax.shard_map(
        local,
        mesh=finer,
        in_specs=(
            P(DP_EXPERT, None),
            P(DP_EXPERT, None),
            P(DP_EXPERT, None),
            P(DP_EXPERT, None),
            P(),
            P(DP_EXPERT, None),
        ),
        out_specs=(P(DP_EXPERT, None), P(), P(DP_EXPERT, None)),
        check_vma=False,
    )
```

profile of v0, /device:TPU:1, one launch (start us, length us, event | category | flops | bytes accessed | tf_op | source)
XLA Modules:
  0.0 173.3 jit_solution(6757993480702342395)
XLA Ops:
  0.6 0.0 copy-start
  0.6 0.9 copy.85
  1.5 0.1 eq.47
  1.7 0.1 eq.43
  1.8 0.1 reshape.189
  1.9 0.8 copy.88
  2.7 0.1 reshape.218
  2.9 0.6 reduce-window.6
  3.5 0.2 slice_reduce_fusion
  3.7 0.1 fusion.5
  3.9 2.2 %scatter_custom_fusion.1 = bf16[512]{0:T(512)(128)(2,1)S(1)} fusion(s32[256]{0:T(256)S(1)} %bitcast.42, bf16[256]{0:T(256)(128)(2,1)S(1)} %reshape.218, bf16[]{:T(256)} %constant.36.clone.1), kind=kCustom, calls=%fused_computation.39 | custom fusion | bytes 1026 | tf_op jit(solution)/shard_map/scatter | solution.py:96
  6.0 0.2 copy.90
  6.2 3.3 %broadcast_in_dim.11 = bf16[128,2,4096]{2,1,0:T(2,128)(2,1)S(1)} broadcast(bf16[128,4096]{1,0:T(8,128)(2,1)} %param.7), dimensions={0,2} | broadcast | bytes 3145728 | tf_op jit(solution)/shard_map/broadcast_in_dim | solution.py:93
  9.6 2.2 %reshape.210 = bf16[256,4096]{1,0:T(8,128)(2,1)} reshape(bf16[128,2,4096]{2,1,0:T(2,128)(2,1)S(1)} %broadcast_in_dim.11) | data formatting | bytes 4194304 | tf_op jit(solution)/shard_map/reshape | solution.py:93
  11.8 7.1 %scatter_custom_fusion = bf16[512,4096]{1,0:T(8,128)(2,1)} fusion(s32[256]{0:T(256)S(1)} %bitcast.43, bf16[256,4096]{1,0:T(8,128)(2,1)} %reshape.210, bf16[]{:T(256)} %constant.36.clone.1), kind=kCustom, calls=%fused_computation.9 | custom fusion | bytes 4194816 | tf_op jit(solution)/shard_map/scatter | solution.py:95
  18.9 8.6 %copy.89 = bf16[2,256,4096]{2,0,1:T(2,128)(2,1)} copy(bf16[2,256,4096]{2,1,0:T(8,128)(2,1)} %bitcast.35) | data formatting | bytes 8388608 | tf_op jit(solution)/shard_map/reshape | solution.py:98
  27.5 8.6 %pad_maximum_fusion = bf16[2,256,4097]{2,0,1:T(2,128)(2,1)} fusion(bf16[2,256,1]{2,0,1:T(2,128)(2,1)S(1)} %copy.90, bf16[2,256,4096]{2,0,1:T(2,128)(2,1)} %copy.89), kind=kLoop, calls=%fused_computation.8 | loop fusion | flops 8390656 | bytes 8390656 | tf_op jit(solution)/shard_map/concatenate | solution.py:13
  36.1 53.0 %all_to_all.42 = bf16[2,256,4097]{2,0,1:T(2,128)(2,1)S(1)} all-to-all(bf16[2,256,4097]{2,0,1:T(2,128)(2,1)} %pad_maximum_fusion), channel_id=1, replica_groups=mesh['dp_0'=8,'dp_1'=4,'dp_2'=2,'expert'=4] {'expert'}, dimensions={1} | all-to-all | bytes 8390656 | tf_op jit(solution)/shard_map/all_to_all | solution.py:15
  89.1 2.0 %copy-done.1 = bf16[2,256,4097]{2,0,1:T(2,128)(2,1)} copy-done((bf16[2,256,4097]{2,0,1:T(2,128)(2,1)}, bf16[2,256,4097]{2,0,1:T(2,128)(2,1)S(1)}, u32[]{:S(2)}) %copy-start.1) | copy-done | bytes 4195352
  91.1 0.1 slice.20
  91.2 0.1 copy.105
  91.3 6.3 %slice.19 = bf16[2,256,4096]{2,0,1:T(2,128)(2,1)S(1)} slice(bf16[2,256,4097]{2,0,1:T(2,128)(2,1)} %copy-done.1), slice={[0:2], [0:256], [0:4096]} | slice | bytes 8388608 | tf_op jit(solution)/shard_map/slice | solution.py:20
  97.6 0.0 copy-start.2
  97.6 3.0 %copy.104 = bf16[2,256,4096]{2,1,0:T(8,128)(2,1)S(1)} copy(bf16[2,256,4096]{2,0,1:T(2,128)(2,1)S(1)} %slice.19) | data formatting | bytes 8388608
  100.6 0.0 copy-start.4
  100.6 4.9 %fusion.1 = (bf16[512,4096]{1,0:T(8,128)(2,1)}, f32[512]{0:T(512)S(1)}) fusion(bf16[2,256,4096]{2,1,0:T(8,128)(2,1)S(1)} %copy.104, f32[512]{0:T(512)S(1)} %bitcast.41, bf16[512,4096]{1,0:T(8,128)(2,1)S(1)} %copy-done.2), kind=kLoop, calls=%fused_computation.6 | loop fusion | flops 12582400 | bytes 12587008 | tf_op jit(solution)/shard_map/convert_element_type | solution.py:105
  105.6 0.1 all_to_all.28
  105.7 0.7 reshape.230
  106.3 3.2 %all-to-all-start.1 = ((f32[4,1,128]{2,1,0:T(1,128)}), f32[4,1,128]{2,1,0:T(1,128)S(1)}, u32[]{:S(2)}, u32[]{:S(2)}) async-start(f32[4,1,128]{2,1,0:T(1,128)} %reshape.230), calls=%async_computation.1 | async-start | bytes 4096 | tf_op jit(solution)/shard_map/all_to_all | solution.py:108
  109.6 4.0 %all-to-all-done.1 = f32[4,1,128]{2,1,0:T(1,128)S(1)} async-done(((f32[4,1,128]{2,1,0:T(1,128)}), f32[4,1,128]{2,1,0:T(1,128)S(1)}, u32[]{:S(2)}, u32[]{:S(2)}) %all-to-all-start.1) | async-done | bytes 2080 | tf_op jit(solution)/shard_map/all_to_all | solution.py:108
  113.5 0.5 broadcast.150
  114.1 0.7 reduce.5
  114.7 0.1 reshape.231
  114.8 0.1 reshape.195
  114.9 1.9 %gather_fusion = f32[256]{0:T(256)S(1)} fusion(f32[512]{0:T(512)S(1)} %reshape.195, s32[1024]{0:T(1024)S(1)} %pad_clamp_fusion), kind=kCustom, calls=%fused_computation | custom fusion | bytes 3072 | tf_op jit(solution)/shard_map/gather | solution.py:115
  116.8 0.1 reshape.196
  117.0 0.1 copy.95
  117.1 0.2 fusion.16
  117.5 11.9 %all_to_all.43 = f32[8,32,128]{2,1,0:T(8,128)S(1)} all-to-all(f32[8,32,128]{2,1,0:T(8,128)S(1)} %bitcast.36), channel_id=1, replica_groups=mesh['dp_0'=8,'dp_1'=4,'dp_2'=2,'expert'=4] {'dp_2','expert'}, dimensions={0} | all-to-all | bytes 262144 | tf_op jit(solution)/shard_map/all_to_all | solution.py:33
  129.4 19.4 %all_to_all.44 = f32[32,1,128]{2,1,0:T(1,128)S(1)} all-to-all(f32[32,1,128]{2,1,0:T(1,128)S(1)} %bitcast.37), channel_id=1, replica_groups=mesh['dp_0'=8,'dp_1'=4,'dp_2'=2,'expert'=4] {'dp_0','dp_1'}, dimensions={0} | all-to-all | bytes 32768 | tf_op jit(solution)/shard_map/all_to_all | solution.py:41
  148.8 0.1 reduce_sum.52
  148.9 11.6 %all_to_all.45 = f32[32,1,128]{2,1,0:T(1,128)S(1)} all-to-all(f32[32,1,128]{2,1,0:T(1,128)S(1)} %broadcast_in_dim.13), channel_id=1, replica_groups=mesh['dp_0'=8,'dp_1'=4,'dp_2'=2,'expert'=4] {'dp_0','dp_1'}, dimensions={0} | all-to-all | bytes 32768 | tf_op jit(solution)/shard_map/all_to_all | solution.py:52
  160.4 0.7 broadcast_in_dim.28
  161.1 6.3 %all-to-all-start.5 = ((f32[8,32,128]{2,1,0:T(8,128)}), f32[8,32,128]{2,1,0:T(8,128)S(1)}, u32[]{:S(2)}, u32[]{:S(2)}) async-start(f32[8,32,128]{2,1,0:T(8,128)} %broadcast_in_dim.28), calls=%async_computation.5 | async-start | bytes 262144 | tf_op jit(solution)/shard_map/all_to_all | solution.py:52
  167.3 1.4 convolution_convert_fusion
  168.8 3.7 %all-to-all-done.5 = f32[8,32,128]{2,1,0:T(8,128)S(1)} async-done(((f32[8,32,128]{2,1,0:T(8,128)}), f32[8,32,128]{2,1,0:T(8,128)S(1)}, u32[]{:S(2)}, u32[]{:S(2)}) %all-to-all-start.5) | async-done | bytes 131104 | tf_op jit(solution)/shard_map/all_to_all | solution.py:52
  172.5 0.1 copy.97
  172.6 0.7 mul.75
  (26 shorter events, 0.3 us)
Async XLA Ops:
  0.6 116.5 %copy-start = (bf16[128,4096]{1,0:T(8,128)(2,1)S(1)}, bf16[128,4096]{1,0:T(8,128)(2,1)}, u32[]{:S(2)}) copy-start(bf16[128,4096]{1,0:T(8,128)(2,1)} %param.6) | copy-start | bytes 3145732
  89.1 2.0 %copy-start.1 = (bf16[2,256,4097]{2,0,1:T(2,128)(2,1)}, bf16[2,256,4097]{2,0,1:T(2,128)(2,1)S(1)}, u32[]{:S(2)}) copy-start(bf16[2,256,4097]{2,0,1:T(2,128)(2,1)S(1)} %all_to_all.42) | copy-start | bytes 12585988
  97.6 3.0 %copy-start.2 = (bf16[512,4096]{1,0:T(8,128)(2,1)S(1)}, bf16[512,4096]{1,0:T(8,128)(2,1)}, u32[]{:S(2)}) copy-start(bf16[512,4096]{1,0:T(8,128)(2,1)} %param.11) | copy-start | bytes 12582916
  100.6 16.4 %copy-start.4 = (bf16[128,2]{0,1:T(2,128)(2,1)S(1)}, bf16[128,2]{0,1:T(2,128)(2,1)}, u32[]{:S(2)}) copy-start(bf16[128,2]{0,1:T(2,128)(2,1)} %param.9) | copy-start | bytes 1540
  100.6 16.5 %copy-start.5 = (s32[128,2]{0,1:T(2,128)S(1)}, s32[128,2]{0,1:T(2,128)}, u32[]{:S(2)}) copy-start(s32[128,2]{0,1:T(2,128)} %param.8) | copy-start | bytes 3076
  100.6 66.7 %copy-start.3 = (bf16[8,4096]{1,0:T(8,128)(2,1)S(1)}, bf16[8,4096]{1,0:T(8,128)(2,1)}, u32[]{:S(2)}) copy-start(bf16[8,4096]{1,0:T(8,128)(2,1)} %param.10) | copy-start | bytes 196612
  106.3 7.2 %all-to-all-start.1 = ((f32[4,1,128]{2,1,0:T(1,128)}), f32[4,1,128]{2,1,0:T(1,128)S(1)}, u32[]{:S(2)}, u32[]{:S(2)}) async-start(f32[4,1,128]{2,1,0:T(1,128)} %reshape.230), calls=%async_computation.1 | async-start | bytes 4096 | tf_op jit(solution)/shard_map/all_to_all | solution.py:108
  161.1 11.4 %all-to-all-start.5 = ((f32[8,32,128]{2,1,0:T(8,128)}), f32[8,32,128]{2,1,0:T(8,128)S(1)}, u32[]{:S(2)}, u32[]{:S(2)}) async-start(f32[8,32,128]{2,1,0:T(8,128)} %broadcast_in_dim.28), calls=%async_computation.5 | async-start | bytes 262144 | tf_op jit(solution)/shard_map/all_to_all | solution.py:52
where the time goes:
time: 174 us; the launch traced here: 173 us
  blocking collectives  95.8 us (55%)
  local copies, waits for them, and re-layouts  42.6 us (24%)
  other arithmetic  15.1 us (9%)
  starting transfers between devices  9.49 us (5%)
  waiting for transfers between devices  7.69 us (4%)
    all_to_all x1, blocking collectives, side_by_side(): lax.all_to_all(both, axis, split_axis=split_dim, concat_axis=concat_dim,...  53 us
    all_to_all x1, blocking collectives, sum_in_two_steps(): lax.all_to_all(nearer, far, split_axis=0, concat_axis=0, tiled=True)  19.4 us
    all_to_all x1, blocking collectives, sum_at_owner(): lax.all_to_all(split_up(shard, dim, length), axis, 0, 0, tiled=True)  11.9 us
    all_to_all x1, blocking collectives, copy_for_each(): return lax.all_to_all(copies, axis, split_axis=0, concat_axis=0, tiled=True)  11.6 us
    concatenate x1, other arithmetic, side_by_side(): both = jnp.concatenate(columns, axis=along)  8.62 us
    reshape x1, local copies, waits for them, and re-layouts, local(): outgoing.reshape(layout)  8.58 us
    unnamed x19, local copies, waits for them, and re-layouts  7.5 us
    scatter x1, local copies, waits for them, and re-layouts, local(): jnp.zeros(saved_outputs.shape, jnp.bfloat16).at[target].set(repeated)  7.13 us
  transfers between devices with their start and end apart: 2, of which 2 were waited for; matrix products, arithmetic and copies ran while one was open for 1% of the time, Pallas kernels for 0%

commit v1 on v0

v1 whole, which is shorter than its diff:
```python
import functools

import jax
import jax.numpy as jnp
from jax import lax
from jax.experimental import pallas as pl
from jax.experimental.pallas import tpu as pltpu
from jax.sharding import Mesh
from jax.sharding import PartitionSpec as P

DP_EXPERT = ("dp_0", "dp_1", "dp_2", "expert")
CHUNK = 1024
BF16 = jnp.bfloat16
F32 = jnp.float32


def shift(a, step):
    n = lax.axis_size("expert")
    return lax.ppermute(a, "expert", [(i, (i + step) % n) for i in range(n)])


def prepare_kernel(me_ref, meta_ref, info_ref):
    first = 2 * me_ref[0]
    row = lax.broadcasted_iota(jnp.int32, (8, 128), 0)
    held = (first + row).astype(F32)
    earlier = lax.broadcasted_iota(jnp.int32, (128, 128), 0)
    later = lax.broadcasted_iota(jnp.int32, (128, 128), 1)
    before = jnp.where(earlier < later, 1.0, 0.0).astype(BF16)
    for s in range(meta_ref.shape[0]):
        meta = meta_ref[s]
        is0 = jnp.broadcast_to(meta[0:1], (8, 128)) == held
        is1 = jnp.broadcast_to(meta[1:2], (8, 128)) == held
        named = jnp.logical_or(is0, is1)
        count = jnp.dot(
            jnp.where(named, 1.0, 0.0).astype(BF16), before, preferred_element_type=F32
        )
        gate = jnp.where(is0, jnp.broadcast_to(meta[2:3], (8, 128)), jnp.broadcast_to(meta[3:4], (8, 128)))
        position = jnp.where(named, count, -1.0)
        info_ref[s, 0:2, :] = position[0:2]
        info_ref[s, 2:4, :] = gate[0:2]


def prepare(me, meta):
    return pl.pallas_call(
        prepare_kernel,
        out_shape=jax.ShapeDtypeStruct(meta.shape, F32),
        in_specs=[
            pl.BlockSpec(memory_space=pltpu.SMEM),
            pl.BlockSpec(memory_space=pltpu.VMEM),
        ],
        out_specs=pl.BlockSpec(memory_space=pltpu.VMEM),
    )(me, meta)


def chosen(info, h):
    slot = lax.broadcasted_iota(jnp.int32, (64, 128), 0).astype(F32)
    return slot == jnp.broadcast_to(info[h : h + 1], (64, 128))


def source_kernel(with_products, with_grad, aliased, *refs):
    refs = list(refs)
    source_ref, info_ref = refs[0], refs[1]
    at = 2
    if with_products:
        saved_ref = refs[at]
        at += 1
    upper_ref, lower_ref = refs[at], refs[at + 1]
    at += 2 + aliased
    if with_products:
        products_ref = refs[at]
        at += 1
    if with_grad:
        grad_ref = refs[at]
        at += 1
    if with_products:
        total_ref = refs[at]
        at += 1
    if with_grad:
        pick_ref = refs[at]
    step = pl.program_id(0)
    rows = jnp.concatenate([upper_ref[...], lower_ref[...]], axis=0)

    if with_grad:

        @pl.when(step == 0)
        def _():
            info = info_ref[0]
            for h in range(2):
                gate = jnp.broadcast_to(info[2 + h : 3 + h], (64, 128))
                pick_ref[64 * h : 64 * h + 64, :] = jnp.where(chosen(info, h), gate, 0.0).astype(BF16)

        scaled = jnp.dot(pick_ref[...], rows, preferred_element_type=F32).astype(BF16)
        grad_ref[0, 0] = scaled[0:64]
        grad_ref[1, 0] = scaled[64:128]

    if with_products:

        @pl.when(step == 0)
        def _():
            total_ref[...] = jnp.zeros_like(total_ref)

        stored = jnp.concatenate([saved_ref[0, 0], saved_ref[1, 0]], axis=0)
        total_ref[...] += lax.dot_general(
            stored, rows, (((1,), (1,)), ((), ())), preferred_element_type=F32
        )

        @pl.when(step == pl.num_programs(0) - 1)
        def _():
            info = info_ref[0]
            products_ref[...] = jnp.zeros_like(products_ref)
            for h in range(2):
                z = total_ref[64 * h : 64 * h + 64, :]
                products_ref[h : h + 1, :] = jnp.sum(
                    jnp.where(chosen(info, h), z, 0.0), axis=0, keepdims=True
                )


def from_source(source, info, saved, upper, lower, grad, with_products, with_grad):
    width = saved.shape[-1]
    upper, up = upper
    lower, low = lower
    grid = (width // CHUNK,)
    half = (64, CHUNK)
    in_specs = [pl.BlockSpec((1, 8, 128), lambda i, s: (s[0], 0, 0))]
    operands = [info]
    block = pl.BlockSpec((2, 1, 64, CHUNK), lambda i, s: (0, s[0], 0, i))
    if with_products:
        in_specs.append(block)
        operands.append(saved)
    in_specs += [
        pl.BlockSpec(half, lambda i, s: (up, i)),
        pl.BlockSpec(half, lambda i, s: (low, i)),
    ]
    operands += [upper, lower]
    aliased = grad is not None
    aliases = {}
    out_specs, out_shape, scratch = [], [], []
    if with_products:
        out_specs.append(pl.BlockSpec((8, 128), lambda i, s: (0, 0)))
        out_shape.append(jax.ShapeDtypeStruct((8, 128), F32))
        scratch.append(pltpu.VMEM((128, 128), F32))
    if aliased:
        in_specs.append(pl.BlockSpec(memory_space=pl.ANY))
        operands.append(grad)
        aliases = {len(operands): len(out_shape)}
    if with_grad:
        out_specs.append(block)
        out_shape.append(jax.ShapeDtypeStruct(saved.shape, BF16))
        scratch.append(pltpu.VMEM((128, 128), BF16))
    return pl.pallas_call(
        functools.partial(source_kernel, with_products, with_grad, aliased),
        grid_spec=pltpu.PrefetchScalarGridSpec(
            num_scalar_prefetch=1,
            grid=grid,
            in_specs=in_specs,
            out_specs=out_specs,
            scratch_shapes=scratch,
        ),
        out_shape=out_shape,
        input_output_aliases=aliases,
        cost_estimate=pl.CostEstimate(
            flops=4 * 128 * 128 * width, bytes_accessed=6 * 128 * width, transcendentals=0
        ),
    )(source, *operands)


def logit_kernel(me_ref, meta_ref, p0_ref, p1_ref, p2_ref, p3_ref, tokens_ref, logit_ref, part_ref):
    first = 2 * me_ref[0]
    meta = meta_ref[...]
    e0, e1, g0, g1 = meta[0:1], meta[1:2], meta[2:3], meta[3:4]
    gg0 = jnp.zeros((1, 128), F32)
    gg1 = jnp.zeros((1, 128), F32)
    for d, p_ref in enumerate((p0_ref, p1_ref, p2_ref, p3_ref)):
        for h in range(2):
            expert = lax.rem(first + 2 * d + h, 8).astype(F32)
            line = p_ref[h : h + 1, :]
            gg0 = gg0 + jnp.where(e0 == expert, line, 0.0)
            gg1 = gg1 + jnp.where(e1 == expert, line, 0.0)
    blended = g0 * gg0 + g1 * gg1
    s0 = g0 * (gg0 - blended)
    s1 = g1 * (gg1 - blended)
    row = lax.broadcasted_iota(jnp.int32, (8, 128), 0).astype(F32)
    wide = lambda v: jnp.broadcast_to(v, (8, 128))
    logit = jnp.where(wide(e0) == row, wide(s0), 0.0) + jnp.where(wide(e1) == row, wide(s1), 0.0)
    logit = logit.astype(BF16)
    logit_ref[...] = logit
    parts = part_ref.shape[0]
    piece = part_ref.shape[2]
    for j in range(parts):
        part_ref[j] = jnp.dot(
            logit, tokens_ref[:, j * piece : (j + 1) * piece], preferred_element_type=F32
        )


def logits(me, meta, products, tokens, parts):
    width = tokens.shape[1]
    vmem = pl.BlockSpec(memory_space=pltpu.VMEM)
    return pl.pallas_call(
        logit_kernel,
        out_shape=[
            jax.ShapeDtypeStruct((8, 128), BF16),
            jax.ShapeDtypeStruct((parts, 8, width // parts), F32),
        ],
        in_specs=[pl.BlockSpec(memory_space=pltpu.SMEM)] + [vmem] * 6,
        out_specs=[vmem, vmem],
    )(me, meta, *products, tokens)


def local(tokens, grad_out, experts, gates, router_weight, saved_outputs):
    width = tokens.shape[1]
    place = lax.axis_index("expert")
    groups = lax.axis_size("expert")
    me = jnp.reshape(place, (1,)).astype(jnp.int32)
    at = [lax.rem(me + d, groups) for d in range(groups)]
    saved = saved_outputs.reshape(2, groups, 64, width)
    upper, lower = grad_out[:64], grad_out[64:]

    from_left_upper = shift(upper, 1)
    from_right_lower = shift(lower, -1)
    meta = jnp.concatenate(
        [experts.astype(F32).T, gates.astype(F32).T, jnp.zeros((4, 128), F32)], axis=0
    )
    copies = jnp.broadcast_to(meta, (groups, 8, 128))
    everyone = lax.all_to_all(copies, "expert", 0, 0, tiled=True)
    info = prepare(me, everyone)
    lower_next, upper_next, info = lax.optimization_barrier((lower, upper, info))
    from_left_lower = shift(lower_next, 1)
    from_right_upper = shift(upper_next, -1)
    p_own, expert_grad = from_source(
        at[0], info, saved, (grad_out, 0), (grad_out, 1), None, True, True
    )
    far_in, near_in, p_own = lax.optimization_barrier((from_left_upper, from_right_lower, p_own))
    far_upper = shift(far_in, 1)
    far_lower = shift(near_in, -1)
    p_left, expert_grad = from_source(
        at[3], info, saved, (from_left_upper, 0), (from_left_lower, 0), expert_grad, True, True
    )
    p_right, expert_grad = from_source(
        at[1], info, saved, (from_right_upper, 0), (from_right_lower, 0), expert_grad, True, True
    )
    home_right = shift(p_left, -1)
    home_left = shift(p_right, 1)
    (p_far,) = from_source(at[2], info, saved, (far_upper, 0), (far_lower, 0), None, True, False)
    home_far = shift(p_far, 2)
    (expert_grad,) = from_source(
        at[2], info, saved, (far_upper, 0), (far_lower, 0), expert_grad, False, True
    )

    parts = lax.axis_size(("dp_2", "expert"))
    logit, partial = logits(me, meta, (p_own, home_right, home_far, home_left), tokens, parts)
    near = lax.all_to_all(partial, ("dp_2", "expert"), 0, 0, tiled=True).sum(axis=0)
    far_count = lax.axis_size(("dp_0", "dp_1"))
    copies = jnp.broadcast_to(near.astype(BF16), (far_count, *near.shape))
    total = lax.all_to_all(copies, ("dp_0", "dp_1"), 0, 0, tiled=True).astype(F32).sum(axis=0)
    scale = float(lax.axis_size(DP_EXPERT) * tokens.shape[0]) ** (-0.5)
    total = total * scale
    whole = lax.all_to_all(
        jnp.broadcast_to(total, (parts, *total.shape)), ("dp_2", "expert"), 0, 0, tiled=True
    )
    router_grad = whole.swapaxes(0, 1).reshape(8, width)
    input_grad = lax.dot_general(
        logit, router_weight, (((0,), (0,)), ((), ())), preferred_element_type=F32
    ).astype(BF16)
    return input_grad, router_grad, expert_grad.reshape(saved_outputs.shape)


def solution(mesh):
    finer = Mesh(
        mesh.devices.reshape(8, 4, 2, mesh.shape["expert"]), ("dp_0", "dp_1", "dp_2", "expert")
    )
    rows = P(DP_EXPERT, None)
    return jax.shard_map(
        local,
        mesh=finer,
        in_specs=(rows, rows, rows, rows, P(), rows),
        out_specs=(rows, P(), rows),
        check_vma=False,
    )
```

time: 174 us -> 111 us (0.64)
  blocking collectives: 95.8 us -> 15.3 us
  local copies, waits for them, and re-layouts: 42.6 us -> 9.46 us
  Pallas kernels: 0 us -> 24.5 us
  starting transfers between devices: 9.49 us -> 31.6 us
  waiting for transfers between devices: 7.69 us -> 25.8 us
  other arithmetic: 15.1 us -> 1.48 us
    all_to_all x4 -> x1, blocking collectives: 95.8 us -> 15.3 us  [local(): lax.all_to_all(partial, ('dp_2', 'expert'), 0, 0, tiled=True).sum(axis=0)]
    pallas_call x0 -> x7, Pallas kernels: none -> 24.5 us  [the longest x5 20.8 us: from_source(): pl.pallas_call(functools.partial(source_kernel, with_products, with_grad,...]
    ppermute x0 -> x9, starting transfers between devices: none -> 11.7 us  [shift(): return lax.ppermute(a, 'expert', [(i, (i + step) % n) for i in range(n)])]
    reshape x7 -> x0, local copies, waits for them, and re-layouts: 11.4 us -> none  [the longest x1 8.58 us: local(): outgoing.reshape(layout)]
    all_to_all x2 -> x3, waiting for transfers between devices: 7.69 us -> 18.6 us  [the longest x1 7.68 us: local(): lax.all_to_all(copies, ('dp_0', 'dp_1'), 0, 0, tiled=True).astype(F32)]
    all_to_all x2 -> x3, starting transfers between devices: 9.49 us -> 19.9 us  [the longest x1 11 us: local(): lax.all_to_all(copies, ('dp_0', 'dp_1'), 0, 0, tiled=True).astype(F32)]
    scatter x2 -> x0, local copies, waits for them, and re-layouts: 9.29 us -> none  [the longest x1 7.13 us: local(): jnp.zeros(saved_outputs.shape, jnp.bfloat16).at[target].set(repeated)]
    concatenate x1, other arithmetic: 8.62 us -> 0.07 us  [local(): jnp.concatenate([experts.astype(F32).T, gates.astype(F32).T, jnp.zeros((4...]
  transfers between devices with their start and end apart: 2 -> 12, of which waited for: 2 -> 5; matrix products, arithmetic and copies ran while one was open for 1% -> 3% of each run, Pallas kernels for 0% -> 20%
where the time goes in v1:
time: 111 us; the launch traced here: 110 us
  starting transfers between devices  31.6 us (28%)
  waiting for transfers between devices  25.8 us (23%)
  Pallas kernels  24.5 us (22%)
  blocking collectives  15.3 us (14%)
  local copies, waits for them, and re-layouts  9.46 us (9%)
  other arithmetic  1.48 us (1%)
  matrix products  1.44 us (1%)
    pallas_call x5, Pallas kernels, from_source(): pl.pallas_call(functools.partial(source_kernel, with_products, with_grad,...  20.8 us
    all_to_all x1, blocking collectives, local(): lax.all_to_all(partial, ('dp_2', 'expert'), 0, 0, tiled=True).sum(axis=0)  15.3 us
    ppermute x9, starting transfers between devices, shift(): return lax.ppermute(a, 'expert', [(i, (i + step) % n) for i in range(n)])  11.7 us
    all_to_all x1, starting transfers between devices, local(): lax.all_to_all(copies, ('dp_0', 'dp_1'), 0, 0, tiled=True).astype(F32)  11 us
    all_to_all x1, waiting for transfers between devices, local(): lax.all_to_all(copies, ('dp_0', 'dp_1'), 0, 0, tiled=True).astype(F32)  7.68 us
    all_to_all x1, waiting for transfers between devices, local(): everyone = lax.all_to_all(copies, 'expert', 0, 0, tiled=True)  7.23 us
    ppermute x9, waiting for transfers between devices, shift(): return lax.ppermute(a, 'expert', [(i, (i + step) % n) for i in range(n)])  7.21 us
    all_to_all x1, starting transfers between devices, local(): lax.all_to_all(jnp.broadcast_to(total, (parts, *total.shape)), ('dp_2', '...  5.62 us
  transfers between devices with their start and end apart: 12, of which 5 were waited for; matrix products, arithmetic and copies ran while one was open for 3% of the time, Pallas kernels for 20%

profile of v1, /device:TPU:1, one launch (start us, length us, event | category | flops | bytes accessed | tf_op | source)
XLA Modules:
  0.0 110.3 jit_solution(1318446061164491306)
XLA Ops:
  0.6 0.0 copy-start
  0.6 2.3 %fusion = (bf16[64,4096]{1,0:T(8,128)(2,1)}, bf16[64,4096]{1,0:T(8,128)(2,1)}) fusion(bf16[128,4096]{1,0:T(8,128)(2,1)} %refs_4_.1), kind=kLoop, calls=%fused_computation.6 | loop fusion | bytes 2097152 | tf_op jit(solution)/shard_map/slice | solution.py:216
  3.0 2.1 %collective-permute-start = (bf16[64,4096]{1,0:T(8,128)(2,1)}, bf16[64,4096]{1,0:T(8,128)(2,1)S(1)}, u32[]{:S(2)}, u32[]{:S(2)}) collective-permute-start(bf16[64,4096]{1,0:T(8,128)(2,1)} %get-tuple-element.25), channel_id=1, source_target_pairs={{0,1},{1,2},{2,3},{3,0},{4,5},{5,6},{6,7},{7,4},{8,9},{9,10},{10,1... | collective-permute-start | bytes 1572872 | tf_op jit(solution)/shard_map/ppermute | solution.py:19
  5.1 1.4 %collective-permute-start.1 = (bf16[64,4096]{1,0:T(8,128)(2,1)}, bf16[64,4096]{1,0:T(8,128)(2,1)S(1)}, u32[]{:S(2)}, u32[]{:S(2)}) collective-permute-start(bf16[64,4096]{1,0:T(8,128)(2,1)} %get-tuple-element.20), channel_id=1, source_target_pairs={{0,3},{1,0},{2,1},{3,2},{4,7},{5,4},{6,5},{7,6},{8,11},{9,8},{10,9... | collective-permute-start | bytes 1572872 | tf_op jit(solution)/shard_map/ppermute | solution.py:19
  6.5 0.7 convert_bitcast_fusion
  7.2 0.1 pad.2.clone
  7.3 0.7 convert_bitcast_fusion.1
  7.9 0.1 maximum_maximum_fusion.meta_ref
  8.0 0.6 broadcast_in_dim.13
  8.6 3.3 %all-to-all-start = ((f32[4,8,128]{2,1,0:T(8,128)}), f32[4,8,128]{2,1,0:T(8,128)S(1)}, u32[]{:S(2)}, u32[]{:S(2)}) async-start(f32[4,8,128]{2,1,0:T(8,128)} %broadcast_in_dim.13), calls=%async_computation | async-start | bytes 32768 | tf_op jit(solution)/shard_map/all_to_all | solution.py:224
  11.9 7.2 %all-to-all-done.meta_ref = f32[4,8,128]{2,1,0:T(8,128)S(1)} async-done(((f32[4,8,128]{2,1,0:T(8,128)}), f32[4,8,128]{2,1,0:T(8,128)S(1)}, u32[]{:S(2)}, u32[]{:S(2)}) %all-to-all-start) | async-done | bytes 16416 | tf_op jit(solution)/shard_map/all_to_all | solution.py:224
  19.1 0.6 copy-done.7
  19.7 1.5 %shard_map.85.refs_1_ = f32[4,8,128]{2,1,0:T(8,128)} custom-call(s32[1]{0:T(128)} %bitcast.me_ref, f32[4,8,128]{2,1,0:T(8,128)} %copy-done.7), custom_call_target="tpu_custom_call" | custom-call | tf_op jit(solution)/shard_map/pallas_call | solution.py:44
  21.2 0.5 collective-permute-start.2
  21.7 2.1 %collective-permute-start.7 = (bf16[64,4096]{1,0:T(8,128)(2,1)}, bf16[64,4096]{1,0:T(8,128)(2,1)S(1)}, u32[]{:S(2)}, u32[]{:S(2)}) collective-permute-start(bf16[64,4096]{1,0:T(8,128)(2,1)} %get-tuple-element.25), channel_id=1, source_target_pairs={{0,3},{1,0},{2,1},{3,2},{4,7},{5,4},{6,5},{7,6},{8,11},{9,8},{10,9... | collective-permute-start | bytes 1572872 | tf_op jit(solution)/shard_map/ppermute | solution.py:19
  23.9 4.5 %shard_map.86 = (f32[8,128]{1,0:T(8,128)}, bf16[2,4,64,4096]{3,2,1,0:T(8,128)(2,1)}) custom-call(s32[1]{0:T(128)S(6)} %rem.57.refs_0_, f32[4,8,128]{2,1,0:T(8,128)} %shard_map.85.refs_1_, bf16[2,4,64,4096]{3,2,1,0:T(8,128)(2,1)} %bitcast.12, bf16[128,4096]{1,0:T(8,128)(2,1)} %refs_4_.1, bf16[128,4096]{1,0:T(8,128)(2,1)} %refs_4_.1), custom_call_target="tpu_custom_call" | custom-call | flops 268435456 | bytes 3145728 | tf_op jit(solution)/shard_map/pallas_call | solution.py:150
  28.3 0.0 collective-permute-done.refs_3_
  28.4 0.0 collective-permute-done.1.refs_4_
  28.4 0.1 collective-permute-start.4
  28.5 2.7 %collective-permute-start.5 = (bf16[64,4096]{1,0:T(8,128)(2,1)S(1)}, bf16[64,4096]{1,0:T(8,128)(2,1)S(1)}, u32[]{:S(2)}, u32[]{:S(2)}) collective-permute-start(bf16[64,4096]{1,0:T(8,128)(2,1)S(1)} %collective-permute-done.1.refs_4_), channel_id=1, source_target_pairs={{0,3},{1,0},{2,1},{3,2},{4,7},{5,4},{6,5},{7,6},{8,11},{9,8},{10,9... | collective-permute-start | bytes 1572872 | tf_op jit(solution)/shard_map/ppermute | solution.py:19
  31.1 3.1 %collective-permute-done.2.refs_4_ = bf16[64,4096]{1,0:T(8,128)(2,1)S(1)} collective-permute-done((bf16[64,4096]{1,0:T(8,128)(2,1)}, bf16[64,4096]{1,0:T(8,128)(2,1)S(1)}, u32[]{:S(2)}, u32[]{:S(2)}) %collective-permute-start.2) | collective-permute-done | bytes 524320 | tf_op jit(solution)/shard_map/ppermute | solution.py:19
  34.2 0.8 copy-done.5
  35.0 4.5 %shard_map.87 = (f32[8,128]{1,0:T(8,128)}, bf16[2,4,64,4096]{3,2,1,0:T(8,128)(2,1)}) custom-call(s32[1]{0:T(128)S(6)} %rem.63.refs_0_, f32[4,8,128]{2,1,0:T(8,128)} %shard_map.85.refs_1_, bf16[2,4,64,4096]{3,2,1,0:T(8,128)(2,1)} %bitcast.13, bf16[64,4096]{1,0:T(8,128)(2,1)} %copy-done.3, ...), custom_call_target="tpu_custom_call", output_to_operand_aliasing={{1}: (5, {})} | custom-call | flops 268435456 | bytes 3145728 | tf_op jit(solution)/shard_map/pallas_call | solution.py:150
  39.5 0.0 collective-permute-done.7.refs_3_
  39.5 0.0 copy-start.6
  39.5 0.8 copy-done.6
  40.3 4.5 %shard_map.89 = (f32[8,128]{1,0:T(8,128)}, bf16[2,4,64,4096]{3,2,1,0:T(8,128)(2,1)}) custom-call(s32[1]{0:T(128)S(6)} %rem.75.refs_0_, f32[4,8,128]{2,1,0:T(8,128)} %shard_map.85.refs_1_, bf16[2,4,64,4096]{3,2,1,0:T(8,128)(2,1)} %bitcast.14, bf16[64,4096]{1,0:T(8,128)(2,1)} %copy-done.6, ...), custom_call_target="tpu_custom_call", output_to_operand_aliasing={{1}: (5, {})} | custom-call | flops 268435456 | bytes 3145728 | tf_op jit(solution)/shard_map/pallas_call | solution.py:150
  44.8 0.0 collective-permute-start.8
  44.8 2.7 %collective-permute-start.3 = (f32[8,128]{1,0:T(8,128)S(1)}, f32[8,128]{1,0:T(8,128)S(1)}, u32[]{:S(2)}, u32[]{:S(2)}) collective-permute-start(f32[8,128]{1,0:T(8,128)S(1)} %copy-done.13), channel_id=1, source_target_pairs={{0,3},{1,0},{2,1},{3,2},{4,7},{5,4},{6,5},{7,6},{8,11},{9,8},{10,9... | collective-permute-start | bytes 12296 | tf_op jit(solution)/shard_map/ppermute | solution.py:19
  47.4 0.0 collective-permute-done.4.refs_3_.refs_2_
  47.5 0.8 copy-done.1
  48.2 0.8 copy-done.2
  49.0 3.5 %shard_map.88 = f32[8,128]{1,0:T(8,128)} custom-call(s32[1]{0:T(128)S(6)} %rem.69.refs_0_, f32[4,8,128]{2,1,0:T(8,128)} %shard_map.85.refs_1_, bf16[2,4,64,4096]{3,2,1,0:T(8,128)(2,1)} %bitcast.15, bf16[64,4096]{1,0:T(8,128)(2,1)} %copy-done.1, bf16[64,4096]{1,0:T(8,128)(2,1)} %copy-done.2), custom_call_target="tpu_custom_call" | custom-call | flops 268435456 | bytes 3145728 | tf_op jit(solution)/shard_map/pallas_call | solution.py:150
  52.6 0.0 collective-permute-start.6
  52.6 0.0 collective-permute-done.3.p1_ref
  52.6 4.1 %collective-permute-done.6.p2_ref = f32[8,128]{1,0:T(8,128)S(1)} collective-permute-done((f32[8,128]{1,0:T(8,128)}, f32[8,128]{1,0:T(8,128)S(1)}, u32[]{:S(2)}, u32[]{:S(2)}) %collective-permute-start.6) | collective-permute-done | bytes 4128 | tf_op jit(solution)/shard_map/ppermute | solution.py:19
  56.8 0.6 copy-done.11
  57.4 2.2 %shard_map.90 = (bf16[8,128]{1,0:T(8,128)(2,1)}, f32[8,8,512]{2,1,0:T(8,128)}) custom-call(s32[1]{0:T(128)} %bitcast.me_ref, f32[8,128]{1,0:T(8,128)} %copy-done.8, f32[8,128]{1,0:T(8,128)} %get-tuple-element.19.p0_ref, f32[8,128]{1,0:T(8,128)} %copy-done.10, f32[8,128]{1,0:T(8,128)} %copy-done.11, f32[8,128]{1,0:T(8,128)} %copy-done.9, ...), custom_call_target="tpu_custom_call" | custom-call | tf_op jit(solution)/shard_map/pallas_call | solution.py:198
  59.5 15.3 %all_to_all.20 = f32[8,8,512]{2,1,0:T(8,128)S(1)} all-to-all(f32[8,8,512]{2,1,0:T(8,128)} %get-tuple-element.29), channel_id=1, replica_groups=mesh['dp_0'=8,'dp_1'=4,'dp_2'=2,'expert'=4] {'dp_2','expert'}, dimensions={0} | all-to-all | bytes 262144 | tf_op jit(solution)/shard_map/all_to_all | solution.py:251
  74.8 0.7 broadcast_in_dim.14
  75.5 11.0 %all-to-all-start.2 = ((bf16[32,8,512]{2,1,0:T(8,128)(2,1)}), bf16[32,8,512]{2,1,0:T(8,128)(2,1)S(1)}, u32[]{:S(2)}, u32[]{:S(2)}) async-start(bf16[32,8,512]{2,1,0:T(8,128)(2,1)} %broadcast_in_dim.14), calls=%async_computation.2 | async-start | bytes 524288 | tf_op jit(solution)/shard_map/all_to_all | solution.py:254
  86.6 3.9 %shard_map.91 = bf16[2,4,64,4096]{3,2,1,0:T(8,128)(2,1)} custom-call(s32[1]{0:T(128)S(6)} %rem.69.refs_0_, f32[4,8,128]{2,1,0:T(8,128)} %shard_map.85.refs_1_, bf16[64,4096]{1,0:T(8,128)(2,1)} %copy-done.1, bf16[64,4096]{1,0:T(8,128)(2,1)} %copy-done.2, bf16[2,4,64,4096]{3,2,1,0:T(8,128)(2,1)} %get-tuple-element.30.refs_4_), custom_call_target="tpu_custom_call", output_to_operand_aliasing={{}: (4, {})} | custom-call | flops 268435456 | bytes 3145728 | tf_op jit(solution)/shard_map/pallas_call | solution.py:150
  90.5 7.7 %all-to-all-done.2 = bf16[32,8,512]{2,1,0:T(8,128)(2,1)S(1)} async-done(((bf16[32,8,512]{2,1,0:T(8,128)(2,1)}), bf16[32,8,512]{2,1,0:T(8,128)(2,1)S(1)}, u32[]{:S(2)}, u32[]{:S(2)}) %all-to-all-start.2) | async-done | bytes 262176 | tf_op jit(solution)/shard_map/all_to_all | solution.py:254
  98.2 0.7 broadcast_in_dim.15
  98.9 5.6 %all-to-all-start.3 = ((f32[8,8,512]{2,1,0:T(8,128)}), f32[8,8,512]{2,1,0:T(8,128)S(1)}, u32[]{:S(2)}, u32[]{:S(2)}) async-start(f32[8,8,512]{2,1,0:T(8,128)} %broadcast_in_dim.15), calls=%async_computation.3 | async-start | bytes 262144 | tf_op jit(solution)/shard_map/all_to_all | solution.py:257
  104.5 1.4 %convolution_convert_fusion = bf16[128,4096]{1,0:T(8,128)(2,1)} fusion(bf16[8,128]{1,0:T(8,128)(2,1)S(1)} %copy-done.12, bf16[8,4096]{1,0:T(8,128)(2,1)S(1)} %copy-done), kind=kOutput, calls=%fused_computation | convolution fusion | flops 8912896 | bytes 1116160 | tf_op jit(solution)/shard_map/dot_general | solution.py:261
  105.9 3.7 %all-to-all-done.3 = f32[8,8,512]{2,1,0:T(8,128)S(1)} async-done(((f32[8,8,512]{2,1,0:T(8,128)}), f32[8,8,512]{2,1,0:T(8,128)S(1)}, u32[]{:S(2)}, u32[]{:S(2)}) %all-to-all-start.3) | async-done | bytes 131104 | tf_op jit(solution)/shard_map/all_to_all | solution.py:257
  109.6 0.7 copy.16
  (26 shorter events, 0.1 us)
Async XLA Ops:
  0.6 103.9 %copy-start = (bf16[8,4096]{1,0:T(8,128)(2,1)S(1)}, bf16[8,4096]{1,0:T(8,128)(2,1)}, u32[]{:S(2)}) copy-start(bf16[8,4096]{1,0:T(8,128)(2,1)} %param.10) | copy-start | bytes 196612
  3.0 25.4 %collective-permute-start = (bf16[64,4096]{1,0:T(8,128)(2,1)}, bf16[64,4096]{1,0:T(8,128)(2,1)S(1)}, u32[]{:S(2)}, u32[]{:S(2)}) collective-permute-start(bf16[64,4096]{1,0:T(8,128)(2,1)} %get-tuple-element.25), channel_id=1, source_target_pairs={{0,1},{1,2},{2,3},{3,0},{4,5},{5,6},{6,7},{7,4},{8,9},{9,10},{10,1... | collective-permute-start | bytes 1572872 | tf_op jit(solution)/shard_map/ppermute | solution.py:19
  5.1 23.3 %collective-permute-start.1 = (bf16[64,4096]{1,0:T(8,128)(2,1)}, bf16[64,4096]{1,0:T(8,128)(2,1)S(1)}, u32[]{:S(2)}, u32[]{:S(2)}) collective-permute-start(bf16[64,4096]{1,0:T(8,128)(2,1)} %get-tuple-element.20), channel_id=1, source_target_pairs={{0,3},{1,0},{2,1},{3,2},{4,7},{5,4},{6,5},{7,6},{8,11},{9,8},{10,9... | collective-permute-start | bytes 1572872 | tf_op jit(solution)/shard_map/ppermute | solution.py:19
  8.0 31.4 %copy-start.8 = (f32[8,128]{1,0:T(8,128)}, f32[8,128]{1,0:T(8,128)S(1)}, u32[]{:S(2)}) copy-start(f32[8,128]{1,0:T(8,128)S(1)} %maximum_maximum_fusion.meta_ref) | copy-start | bytes 12292
  8.6 10.5 %all-to-all-start = ((f32[4,8,128]{2,1,0:T(8,128)}), f32[4,8,128]{2,1,0:T(8,128)S(1)}, u32[]{:S(2)}, u32[]{:S(2)}) async-start(f32[4,8,128]{2,1,0:T(8,128)} %broadcast_in_dim.13), calls=%async_computation | async-start | bytes 32768 | tf_op jit(solution)/shard_map/all_to_all | solution.py:224
  19.1 0.6 copy-start.7
  21.2 13.0 %collective-permute-start.2 = (bf16[64,4096]{1,0:T(8,128)(2,1)}, bf16[64,4096]{1,0:T(8,128)(2,1)S(1)}, u32[]{:S(2)}, u32[]{:S(2)}) collective-permute-start(bf16[64,4096]{1,0:T(8,128)(2,1)} %get-tuple-element.20), channel_id=1, source_target_pairs={{0,1},{1,2},{2,3},{3,0},{4,5},{5,6},{6,7},{7,4},{8,9},{9,10},{10,1... | collective-permute-start | bytes 1572872 | tf_op jit(solution)/shard_map/ppermute | solution.py:19
  21.7 17.7 %collective-permute-start.7 = (bf16[64,4096]{1,0:T(8,128)(2,1)}, bf16[64,4096]{1,0:T(8,128)(2,1)S(1)}, u32[]{:S(2)}, u32[]{:S(2)}) collective-permute-start(bf16[64,4096]{1,0:T(8,128)(2,1)} %get-tuple-element.25), channel_id=1, source_target_pairs={{0,3},{1,0},{2,1},{3,2},{4,7},{5,4},{6,5},{7,6},{8,11},{9,8},{10,9... | collective-permute-start | bytes 1572872 | tf_op jit(solution)/shard_map/ppermute | solution.py:19
  28.4 5.8 %copy-start.3 = (bf16[64,4096]{1,0:T(8,128)(2,1)}, bf16[64,4096]{1,0:T(8,128)(2,1)S(1)}, u32[]{:S(2)}) copy-start(bf16[64,4096]{1,0:T(8,128)(2,1)S(1)} %collective-permute-done.refs_3_) | copy-start | bytes 1572868
  28.4 11.1 %copy-start.4 = (bf16[64,4096]{1,0:T(8,128)(2,1)}, bf16[64,4096]{1,0:T(8,128)(2,1)S(1)}, u32[]{:S(2)}) copy-start(bf16[64,4096]{1,0:T(8,128)(2,1)S(1)} %collective-permute-done.1.refs_4_) | copy-start | bytes 1572868
  28.4 19.1 %collective-permute-start.4 = (bf16[64,4096]{1,0:T(8,128)(2,1)S(1)}, bf16[64,4096]{1,0:T(8,128)(2,1)S(1)}, u32[]{:S(2)}, u32[]{:S(2)}) collective-permute-start(bf16[64,4096]{1,0:T(8,128)(2,1)S(1)} %collective-permute-done.refs_3_), channel_id=1, source_target_pairs={{0,1},{1,2},{2,3},{3,0},{4,5},{5,6},{6,7},{7,4},{8,9},{9,10},{10,1... | collective-permute-start | bytes 1572872 | tf_op jit(solution)/shard_map/ppermute | solution.py:19
  28.5 19.0 %collective-permute-start.5 = (bf16[64,4096]{1,0:T(8,128)(2,1)S(1)}, bf16[64,4096]{1,0:T(8,128)(2,1)S(1)}, u32[]{:S(2)}, u32[]{:S(2)}) collective-permute-start(bf16[64,4096]{1,0:T(8,128)(2,1)S(1)} %collective-permute-done.1.refs_4_), channel_id=1, source_target_pairs={{0,3},{1,0},{2,1},{3,2},{4,7},{5,4},{6,5},{7,6},{8,11},{9,8},{10,9... | collective-permute-start | bytes 1572872 | tf_op jit(solution)/shard_map/ppermute | solution.py:19
  34.2 0.8 copy-start.5
  39.5 0.8 copy-start.6
  40.3 4.5 %copy-start.13 = (f32[8,128]{1,0:T(8,128)S(1)}, f32[8,128]{1,0:T(8,128)}, u32[]{:S(2)}) copy-start(f32[8,128]{1,0:T(8,128)} %get-tuple-element.22) | copy-start | bytes 12292
  44.8 7.8 %collective-permute-start.8 = (f32[8,128]{1,0:T(8,128)}, f32[8,128]{1,0:T(8,128)S(1)}, u32[]{:S(2)}, u32[]{:S(2)}) collective-permute-start(f32[8,128]{1,0:T(8,128)} %get-tuple-element.27), channel_id=1, source_target_pairs={{0,1},{1,2},{2,3},{3,0},{4,5},{5,6},{6,7},{7,4},{8,9},{9,10},{10,1... | collective-permute-start | bytes 12296 | tf_op jit(solution)/shard_map/ppermute | solution.py:19
  44.8 7.8 %collective-permute-start.3 = (f32[8,128]{1,0:T(8,128)S(1)}, f32[8,128]{1,0:T(8,128)S(1)}, u32[]{:S(2)}, u32[]{:S(2)}) collective-permute-start(f32[8,128]{1,0:T(8,128)S(1)} %copy-done.13), channel_id=1, source_target_pairs={{0,3},{1,0},{2,1},{3,2},{4,7},{5,4},{6,5},{7,6},{8,11},{9,8},{10,9... | collective-permute-start | bytes 12296 | tf_op jit(solution)/shard_map/ppermute | solution.py:19
  47.4 0.8 copy-start.1
  48.2 0.8 copy-start.2
  52.6 4.2 %collective-permute-start.6 = (f32[8,128]{1,0:T(8,128)}, f32[8,128]{1,0:T(8,128)S(1)}, u32[]{:S(2)}, u32[]{:S(2)}) collective-permute-start(f32[8,128]{1,0:T(8,128)} %shard_map.88), channel_id=1, source_target_pairs={{0,2},{1,3},{2,0},{3,1},{4,6},{5,7},{6,4},{7,5},{8,10},{9,11},{10,... | collective-permute-start | bytes 12296 | tf_op jit(solution)/shard_map/ppermute | solution.py:19
  52.6 4.2 %copy-start.9 = (f32[8,128]{1,0:T(8,128)}, f32[8,128]{1,0:T(8,128)S(1)}, u32[]{:S(2)}) copy-start(f32[8,128]{1,0:T(8,128)S(1)} %collective-permute-done.8.p3_ref) | copy-start | bytes 12292
  52.6 4.1 %copy-start.10 = (f32[8,128]{1,0:T(8,128)}, f32[8,128]{1,0:T(8,128)S(1)}, u32[]{:S(2)}) copy-start(f32[8,128]{1,0:T(8,128)S(1)} %collective-permute-done.3.p1_ref) | copy-start | bytes 12292
  56.8 0.6 copy-start.11
  75.5 22.6 %all-to-all-start.2 = ((bf16[32,8,512]{2,1,0:T(8,128)(2,1)}), bf16[32,8,512]{2,1,0:T(8,128)(2,1)S(1)}, u32[]{:S(2)}, u32[]{:S(2)}) async-start(bf16[32,8,512]{2,1,0:T(8,128)(2,1)} %broadcast_in_dim.14), calls=%async_computation.2 | async-start | bytes 524288 | tf_op jit(solution)/shard_map/all_to_all | solution.py:254
  86.6 17.9 %copy-start.12 = (bf16[8,128]{1,0:T(8,128)(2,1)S(1)}, bf16[8,128]{1,0:T(8,128)(2,1)}, u32[]{:S(2)}) copy-start(bf16[8,128]{1,0:T(8,128)(2,1)} %get-tuple-element.28) | copy-start | bytes 6148
  98.9 10.8 %all-to-all-start.3 = ((f32[8,8,512]{2,1,0:T(8,128)}), f32[8,8,512]{2,1,0:T(8,128)S(1)}, u32[]{:S(2)}, u32[]{:S(2)}) async-start(f32[8,8,512]{2,1,0:T(8,128)} %broadcast_in_dim.15), calls=%async_computation.3 | async-start | bytes 262144 | tf_op jit(solution)/shard_map/all_to_all | solution.py:257

commit v2 on v0

v2 whole, which is shorter than its diff:
```python
import functools

import jax
import jax.numpy as jnp
from jax import lax
from jax.experimental import pallas as pl
from jax.experimental.pallas import tpu as pltpu
from jax.sharding import Mesh
from jax.sharding import PartitionSpec as P

DP_EXPERT = ("dp_0", "dp_1", "dp_2", "expert")
PLANE = ("dp_1", "dp_2")
HOUSE = ("dp_1", "dp_2", "expert")
REST = ("dp_0", "expert")
BF16 = jnp.bfloat16
F32 = jnp.float32
SMEM = pl.BlockSpec(memory_space=pltpu.SMEM)
VMEM = pl.BlockSpec(memory_space=pltpu.VMEM)
ANY = pl.BlockSpec(memory_space=pl.ANY)
PARAMS = pltpu.CompilerParams(vmem_limit_bytes=16 * 2**20)


def cost(flops, size):
    return pl.CostEstimate(flops=flops, bytes_accessed=size, transcendentals=0)


def shift(a, step, axis="expert"):
    n = lax.axis_size(axis)
    return lax.ppermute(a, axis, [(i, (i + step) % n) for i in range(n)])


def to_all(a, axes):
    return lax.all_to_all(a, axes, 0, 0, tiled=True)


def wide(v, rows=8):
    return jnp.broadcast_to(v, (rows, v.shape[1]))


def prepare_kernel(place_ref, meta_ref, info_ref):
    house, me = place_ref[0], place_ref[1]
    groups = info_ref.shape[0]
    row = lax.broadcasted_iota(jnp.int32, (8, 128), 0)
    held = (2 * me + row).astype(F32)
    earlier = lax.broadcasted_iota(jnp.int32, (128, 128), 0)
    later = lax.broadcasted_iota(jnp.int32, (128, 128), 1)
    before = jnp.where(earlier < later, 1.0, 0.0).astype(BF16)
    for s in range(groups):
        meta = meta_ref[house * groups + s]
        is0 = wide(meta[0:1]) == held
        is1 = wide(meta[1:2]) == held
        named = jnp.logical_or(is0, is1)
        count = jnp.dot(
            jnp.where(named, 1.0, 0.0).astype(BF16), before, preferred_element_type=F32
        )
        info_ref[s, 0:2, :] = jnp.where(named, count, -1.0)[0:2]
        info_ref[s, 2:4, :] = jnp.where(is0, wide(meta[2:3]), wide(meta[3:4]))[0:2]


def prepare(place, meta, groups):
    return pl.pallas_call(
        prepare_kernel,
        out_shape=jax.ShapeDtypeStruct((groups, 8, 128), F32),
        in_specs=[SMEM, VMEM],
        out_specs=VMEM,
        cost_estimate=cost(1 << 21, 1 << 17),
    )(place, meta)


def chosen(info, h):
    slot = lax.broadcasted_iota(jnp.int32, (64, 128), 0).astype(F32)
    return slot == wide(info[h : h + 1], 64)


def stacked(pieces):
    return pieces[0][...] if len(pieces) == 1 else jnp.concatenate([p[...] for p in pieces], axis=0)


def products(info, saved_ref, s, pieces):
    stored = jnp.concatenate([saved_ref[0, s], saved_ref[1, s]], axis=0)
    total = lax.dot_general(
        stored, stacked(pieces), (((1,), (1,)), ((), ())), preferred_element_type=F32
    )
    return [
        jnp.sum(jnp.where(chosen(info, h), total[64 * h : 64 * h + 64], 0.0), axis=0, keepdims=True)
        for h in range(2)
    ]


def near_kernel(place_ref, info_ref, saved_ref, own, lu, ll, ru, rl, out_ref):
    me = place_ref[1]
    groups = info_ref.shape[0]
    for d, pieces in ((0, (own,)), (1, (ru, rl)), (3, (lu, ll))):
        s = lax.rem(me + d, groups)
        for h, line in enumerate(products(info_ref[s], saved_ref, s, pieces)):
            out_ref[d, h : h + 1, :] = line


def near_products(place, info, saved, pieces):
    groups, width = info.shape[0], saved.shape[-1]
    return pl.pallas_call(
        near_kernel,
        out_shape=jax.ShapeDtypeStruct((groups, 2, 128), F32),
        in_specs=[SMEM] + [VMEM] * 7,
        out_specs=VMEM,
        compiler_params=PARAMS,
        cost_estimate=cost(6 * 128 * 128 * width, 12 * 128 * width),
    )(place, info, saved, *pieces)


def far_kernel(place_ref, info_ref, saved_ref, up, low, near_ref, out_ref):
    me = place_ref[1]
    groups = info_ref.shape[0]
    s = lax.rem(me + 2, groups)
    lines = {2: jnp.concatenate(products(info_ref[s], saved_ref, s, (up, low)), axis=0)}
    for d in (0, 1, 3):
        lines[d] = near_ref[d]
    for d in range(groups):
        t = lax.rem(me + d, groups)
        for j in range(out_ref.shape[0]):
            out_ref[j, t] = lines[d]


def far_products(place, info, saved, pieces, near, copies):
    groups, width = info.shape[0], saved.shape[-1]
    return pl.pallas_call(
        far_kernel,
        out_shape=jax.ShapeDtypeStruct((copies, groups, 2, 128), F32),
        in_specs=[SMEM] + [VMEM] * 5,
        out_specs=VMEM,
        compiler_params=PARAMS,
        cost_estimate=cost(2 * 128 * 128 * width, 4 * 128 * width),
    )(place, info, saved, *pieces, near)


def scaled_kernel(place_ref, info_ref, own, lu, ll, ru, rl, fu, fl, out_ref, pick_ref, held_ref, sems):
    me = place_ref[1]
    groups = info_ref.shape[0]
    started = []
    for d, pieces in ((0, (own,)), (1, (ru, rl)), (3, (lu, ll)), (2, (fu, fl))):
        s = lax.rem(me + d, groups)
        info = info_ref[s]
        for h in range(2):
            pick_ref[64 * h : 64 * h + 64, :] = jnp.where(
                chosen(info, h), wide(info[2 + h : 3 + h], 64), 0.0
            ).astype(BF16)
        held_ref[d] = jnp.dot(
            pick_ref[...], stacked(pieces), preferred_element_type=F32
        ).astype(BF16)
        for h in range(2):
            copy = pltpu.make_async_copy(
                held_ref.at[d, 64 * h : 64 * h + 64], out_ref.at[h, s], sems.at[2 * d + h]
            )
            copy.start()
            started.append(copy)
    for copy in started:
        copy.wait()


def scaled_rows(place, info, pieces, shape):
    groups, width = info.shape[0], shape[-1]
    return pl.pallas_call(
        scaled_kernel,
        out_shape=jax.ShapeDtypeStruct(shape, BF16),
        in_specs=[SMEM] + [VMEM] * 8,
        out_specs=ANY,
        scratch_shapes=[
            pltpu.VMEM((128, 128), BF16),
            pltpu.VMEM((groups, 128, width), BF16),
            pltpu.SemaphoreType.DMA((2 * groups,)),
        ],
        compiler_params=PARAMS,
        cost_estimate=cost(8 * 128 * 128 * width, 16 * 128 * width),
    )(place, info, *pieces)


def turn_kernel(place_ref, tokens_ref, kept_ref, sent_ref):
    column, core = place_ref[2], place_ref[3]
    columns, _, piece = kept_ref.shape
    for k in range(columns):
        first = lax.rem(column + k, columns) * 2
        for out_ref, c in ((kept_ref, core), (sent_ref, 1 - core)):
            at = pl.multiple_of((first + c) * piece, piece)
            out_ref[k] = tokens_ref[:, pl.ds(at, piece)]


def turn(place, tokens, columns):
    piece = tokens.shape[1] // (2 * columns)
    shape = jax.ShapeDtypeStruct((columns, 128, piece), BF16)
    return pl.pallas_call(
        turn_kernel,
        out_shape=[shape, shape],
        in_specs=[SMEM, VMEM],
        out_specs=[VMEM, VMEM],
        compiler_params=PARAMS,
        cost_estimate=cost(0, 4 * tokens.size),
    )(place, tokens)


def plane_blocks(kept, sent):
    columns = kept.shape[0]
    got = shift(sent, 1, "dp_2")
    blocks = [jnp.stack([kept[k], got[k]]) for k in range(columns)]
    return blocks[:1] + [shift(blocks[k], k, "dp_1") for k in range(1, columns)]


def logit_kernel(place_ref, meta_ref, home_ref, t0_ref, t1_ref, t2_ref, t3_ref, logit_ref, out_ref):
    me, column, core = place_ref[1], place_ref[2], place_ref[3]
    tokens_refs = (t0_ref, t1_ref, t2_ref, t3_ref)
    columns = len(tokens_refs)
    groups = home_ref.shape[0] // (2 * columns)
    row = lax.broadcasted_iota(jnp.int32, (8, 128), 0).astype(F32)
    part = None
    for k in range(columns):
        found = []
        for r in range(2):
            b = lax.rem(column + columns - k, columns) * 2 + lax.rem(core + r, 2)
            meta = meta_ref[b * groups + me]
            e0, e1, g0, g1 = meta[0:1], meta[1:2], meta[2:3], meta[3:4]
            grads = jnp.concatenate([home_ref[b * groups + y] for y in range(groups)], axis=0)
            is0, is1 = wide(e0) == row, wide(e1) == row
            gg0 = jnp.sum(jnp.where(is0, grads, 0.0), axis=0, keepdims=True)
            gg1 = jnp.sum(jnp.where(is1, grads, 0.0), axis=0, keepdims=True)
            blended = g0 * gg0 + g1 * gg1
            s0 = g0 * (gg0 - blended)
            s1 = g1 * (gg1 - blended)
            logit = jnp.where(is0, wide(s0), 0.0) + jnp.where(is1, wide(s1), 0.0)
            found.append(logit.astype(BF16))
        if k == 0:
            logit_ref[...] = found[0]
        features = jnp.concatenate([tokens_refs[k][0], tokens_refs[k][1]], axis=0)
        term = jnp.dot(jnp.concatenate(found, axis=1), features, preferred_element_type=F32)
        part = term if part is None else part + term
    part = part.astype(BF16)
    for j in range(out_ref.shape[0]):
        out_ref[j] = part


def logits(place, meta, home, tokens, copies):
    piece = tokens[0].shape[2]
    return pl.pallas_call(
        logit_kernel,
        out_shape=[
            jax.ShapeDtypeStruct((8, 128), BF16),
            jax.ShapeDtypeStruct((copies, 8, piece), BF16),
        ],
        in_specs=[SMEM] + [VMEM] * 6,
        out_specs=[VMEM, VMEM],
        compiler_params=PARAMS,
        cost_estimate=cost(64 * tokens[0].size, 16 * tokens[0].size),
    )(place, meta, home, *tokens)


def total_kernel(scale, parts_ref, out_ref):
    total = parts_ref[0].astype(F32)
    for j in range(1, parts_ref.shape[0]):
        total = total + parts_ref[j].astype(F32)
    total = total * scale
    for j in range(out_ref.shape[0]):
        out_ref[j] = total


def totals(scale, parts, copies):
    return pl.pallas_call(
        functools.partial(total_kernel, scale),
        out_shape=jax.ShapeDtypeStruct((copies, *parts.shape[1:]), F32),
        in_specs=[VMEM],
        out_specs=VMEM,
        cost_estimate=cost(parts.size, 4 * parts.size),
    )(parts)


def local(tokens, grad_out, experts, gates, router_weight, saved_outputs):
    width = tokens.shape[1]
    groups = lax.axis_size("expert")
    houses = lax.axis_size(PLANE)
    place = [lax.axis_index(axis) for axis in (PLANE, "expert", "dp_1", "dp_2")]
    place = jnp.stack(place).astype(jnp.int32)
    saved = saved_outputs.reshape(2, groups, 64, width)

    upper = grad_out[:64]
    left_upper = shift(upper, 1)
    again, upper = lax.optimization_barrier((grad_out, upper))
    lower = again[64:]
    right_lower = shift(lower, -1)
    meta = jnp.concatenate(
        [experts.astype(F32).T, gates.astype(F32).T, jnp.zeros((4, 128), F32)], axis=0
    )
    kept, sent = turn(place, tokens, lax.axis_size("dp_1"))
    lower, upper, sent = lax.optimization_barrier((lower, upper, sent))
    left_lower = shift(lower, 1)
    right_upper = shift(upper, -1)
    every_meta = to_all(jnp.broadcast_to(meta, (houses * groups, 8, 128)), HOUSE)
    left_upper, right_lower, every_meta = lax.optimization_barrier(
        (left_upper, right_lower, every_meta)
    )
    far_upper = shift(left_upper, 1)
    far_lower = shift(right_lower, -1)
    turned = plane_blocks(kept, sent)
    every_meta, left_lower, right_upper, turned = lax.optimization_barrier(
        (every_meta, left_lower, right_upper, turned)
    )
    info = prepare(place, every_meta, groups)

    near_pieces = (grad_out, left_upper, left_lower, right_upper, right_lower)
    near = near_products(place, info, saved, near_pieces)
    sent = far_products(place, info, saved, (far_upper, far_lower), near, houses)
    home = to_all(sent.reshape(houses * groups, 2, 128), HOUSE)
    expert_grad = scaled_rows(place, info, (*near_pieces, far_upper, far_lower), saved.shape)

    logit, parts = logits(place, every_meta, home, turned, lax.axis_size(REST))
    scale = float(lax.axis_size(DP_EXPERT) * tokens.shape[0]) ** (-0.5)
    whole = to_all(totals(scale, to_all(parts, REST), houses), PLANE)
    router_grad = whole.swapaxes(0, 1).reshape(8, width)
    input_grad = lax.dot_general(
        logit, router_weight, (((0,), (0,)), ((), ())), preferred_element_type=F32
    ).astype(BF16)
    return input_grad, router_grad, expert_grad.reshape(saved_outputs.shape)


def solution(mesh):
    finer = Mesh(
        mesh.devices.reshape(8, 4, 2, mesh.shape["expert"]), ("dp_0", "dp_1", "dp_2", "expert")
    )
    rows = P(DP_EXPERT, None)
    return jax.shard_map(
        local,
        mesh=finer,
        in_specs=(rows, rows, rows, rows, P(), rows),
        out_specs=(rows, P(), rows),
        check_vma=False,
    )
```

time: 174 us -> 110 us (0.63)
  blocking collectives: 95.8 us -> 12.6 us
  local copies, waits for them, and re-layouts: 42.6 us -> 16.6 us
  starting transfers between devices: 9.49 us -> 35 us
  waiting for transfers between devices: 7.69 us -> 24.8 us
  Pallas kernels: 0 us -> 13.2 us
  other arithmetic: 15.1 us -> 5 us
    all_to_all x4 -> x1, blocking collectives: 95.8 us -> 12.6 us  [to_all(): return lax.all_to_all(a, axes, 0, 0, tiled=True)]
    ppermute x0 -> x10, starting transfers between devices: none -> 16.2 us  [shift(): return lax.ppermute(a, axis, [(i, (i + step) % n) for i in range(n)])]
    pallas_call x0 -> x7, Pallas kernels: none -> 13.2 us  [the longest x1 3.71 us: scaled_rows(): pl.pallas_call(scaled_kernel, out_shape=jax.ShapeDtypeStruct(shape, BF16)...]
    reshape x7 -> x0, local copies, waits for them, and re-layouts: 11.4 us -> none  [the longest x1 8.58 us: local(): outgoing.reshape(layout)]
    ppermute x0 -> x10, waiting for transfers between devices: none -> 10.4 us  [shift(): return lax.ppermute(a, axis, [(i, (i + step) % n) for i in range(n)])]
    all_to_all x2 -> x3, starting transfers between devices: 9.49 us -> 18.8 us  [to_all(): return lax.all_to_all(a, axes, 0, 0, tiled=True)]
    scatter x2 -> x0, local copies, waits for them, and re-layouts: 9.29 us -> none  [the longest x1 7.13 us: local(): jnp.zeros(saved_outputs.shape, jnp.bfloat16).at[target].set(repeated)]
    concatenate x1, other arithmetic: 8.62 us -> 0.07 us  [local(): jnp.concatenate([experts.astype(F32).T, gates.astype(F32).T, jnp.zeros((4...]
  transfers between devices with their start and end apart: 2 -> 13, of which waited for: 2 -> 6; matrix products, arithmetic and copies ran while one was open for 1% -> 11% of each run, Pallas kernels for 0% -> 8%
where the time goes in v2:
time: 110 us; the launch traced here: 109 us
  starting transfers between devices  35 us (32%)
  waiting for transfers between devices  24.8 us (23%)
  local copies, waits for them, and re-layouts  16.6 us (15%)
  Pallas kernels  13.2 us (12%)
  blocking collectives  12.6 us (11%)
  other arithmetic  5 us (5%)
  matrix products  1.45 us (1%)
    all_to_all x3, starting transfers between devices, to_all(): return lax.all_to_all(a, axes, 0, 0, tiled=True)  18.8 us
    ppermute x10, starting transfers between devices, shift(): return lax.ppermute(a, axis, [(i, (i + step) % n) for i in range(n)])  16.2 us
    all_to_all x3, waiting for transfers between devices, to_all(): return lax.all_to_all(a, axes, 0, 0, tiled=True)  14.3 us
    all_to_all x1, blocking collectives, to_all(): return lax.all_to_all(a, axes, 0, 0, tiled=True)  12.6 us
    ppermute x10, waiting for transfers between devices, shift(): return lax.ppermute(a, axis, [(i, (i + step) % n) for i in range(n)])  10.4 us
    unnamed x41, local copies, waits for them, and re-layouts  8.99 us
    pallas_call x1, Pallas kernels, scaled_rows(): pl.pallas_call(scaled_kernel, out_shape=jax.ShapeDtypeStruct(shape, BF16)...  3.71 us
    another operation x4, other arithmetic, plane_blocks(): blocks = [jnp.stack([kept[k], got[k]]) for k in range(columns)]  3.52 us
  transfers between devices with their start and end apart: 13, of which 6 were waited for; matrix products, arithmetic and copies ran while one was open for 11% of the time, Pallas kernels for 8%

profile of v2, /device:TPU:1, one launch (start us, length us, event | category | flops | bytes accessed | tf_op | source)
XLA Modules:
  0.0 109.5 jit_solution(7652979397210981311)
XLA Ops:
  0.7 2.0 %slice.30 = bf16[64,4096]{1,0:T(8,128)(2,1)} slice(bf16[128,4096]{1,0:T(8,128)(2,1)} %own.3), slice={[0:64], [0:4096]} | slice | bytes 1048576 | tf_op jit(solution)/shard_map/slice | solution.py:281
  2.6 2.1 %collective-permute-start = (bf16[64,4096]{1,0:T(8,128)(2,1)}, bf16[64,4096]{1,0:T(8,128)(2,1)S(1)}, u32[]{:S(2)}, u32[]{:S(2)}) collective-permute-start(bf16[64,4096]{1,0:T(8,128)(2,1)} %slice.30), channel_id=1, source_target_pairs={{0,1},{1,2},{2,3},{3,0},{4,5},{5,6},{6,7},{7,4},{8,9},{9,10},{10,1... | collective-permute-start | bytes 1572872 | tf_op jit(solution)/shard_map/ppermute | solution.py:29
  4.7 1.9 %slice.31 = bf16[64,4096]{1,0:T(8,128)(2,1)} slice(bf16[128,4096]{1,0:T(8,128)(2,1)} %own.3), slice={[64:128], [0:4096]} | slice | bytes 1048576 | tf_op jit(solution)/shard_map/slice | solution.py:284
  6.6 1.4 %collective-permute-start.1 = (bf16[64,4096]{1,0:T(8,128)(2,1)}, bf16[64,4096]{1,0:T(8,128)(2,1)S(1)}, u32[]{:S(2)}, u32[]{:S(2)}) collective-permute-start(bf16[64,4096]{1,0:T(8,128)(2,1)} %slice.31), channel_id=1, source_target_pairs={{0,3},{1,0},{2,1},{3,2},{4,7},{5,4},{6,5},{7,6},{8,11},{9,8},{10,9... | collective-permute-start | bytes 1572872 | tf_op jit(solution)/shard_map/ppermute | solution.py:29
  8.1 1.2 %copy-done.5 = bf16[128,4096]{1,0:T(8,128)(2,1)S(1)} copy-done((bf16[128,4096]{1,0:T(8,128)(2,1)S(1)}, bf16[128,4096]{1,0:T(8,128)(2,1)}, u32[]{:S(2)}) %copy-start.5) | copy-done | bytes 1048600
  9.4 1.4 %shard_map.85 = (bf16[4,128,512]{2,1,0:T(8,128)(2,1)S(1)}, bf16[4,128,512]{2,1,0:T(8,128)(2,1)}) custom-call(s32[4]{0:T(128)S(1)} %pad_add_fusion.place_ref, bf16[128,4096]{1,0:T(8,128)(2,1)S(1)} %copy-done.5), custom_call_target="tpu_custom_call" | custom-call | bytes 2097152 | tf_op jit(solution)/shard_map/pallas_call | solution.py:190
  10.8 0.8 copy-done.7
  11.6 2.9 %collective-permute-start.4 = (bf16[4,128,512]{2,1,0:T(8,128)(2,1)}, bf16[4,128,512]{2,1,0:T(8,128)(2,1)}, u32[]{:S(2)}, u32[]{:S(2)}) collective-permute-start(bf16[4,128,512]{2,1,0:T(8,128)(2,1)} %get-tuple-element.29), channel_id=1, source_target_pairs={{0,4},{4,0},{1,5},{5,1},{2,6},{6,2},{3,7},{7,3},{8,12},{12,8},{9,1... | collective-permute-start | bytes 1572872 | tf_op jit(solution)/shard_map/ppermute | solution.py:29
  14.5 0.7 convert_bitcast_fusion.1
  15.2 0.7 convert_bitcast_fusion
  16.0 0.7 broadcast_in_dim.7
  16.6 4.3 %all-to-all-start = ((f32[32,8,128]{2,1,0:T(8,128)}), f32[32,8,128]{2,1,0:T(8,128)S(1)}, u32[]{:S(2)}, u32[]{:S(2)}) async-start(f32[32,8,128]{2,1,0:T(8,128)} %broadcast_in_dim.7), calls=%async_computation | async-start | bytes 262144 | tf_op jit(solution)/shard_map/all_to_all | solution.py:33
  20.9 1.5 %collective-permute-start.2 = (bf16[64,4096]{1,0:T(8,128)(2,1)}, bf16[64,4096]{1,0:T(8,128)(2,1)S(1)}, u32[]{:S(2)}, u32[]{:S(2)}) collective-permute-start(bf16[64,4096]{1,0:T(8,128)(2,1)} %slice.31), channel_id=1, source_target_pairs={{0,1},{1,2},{2,3},{3,0},{4,5},{5,6},{6,7},{7,4},{8,9},{9,10},{10,1... | collective-permute-start | bytes 1572872 | tf_op jit(solution)/shard_map/ppermute | solution.py:29
  22.4 1.3 %collective-permute-start.3 = (bf16[64,4096]{1,0:T(8,128)(2,1)}, bf16[64,4096]{1,0:T(8,128)(2,1)S(1)}, u32[]{:S(2)}, u32[]{:S(2)}) collective-permute-start(bf16[64,4096]{1,0:T(8,128)(2,1)} %slice.30), channel_id=1, source_target_pairs={{0,3},{1,0},{2,1},{3,2},{4,7},{5,4},{6,5},{7,6},{8,11},{9,8},{10,9... | collective-permute-start | bytes 1572872 | tf_op jit(solution)/shard_map/ppermute | solution.py:29
  23.7 1.9 %fusion = (bf16[1,128,512]{2,1,0:T(8,128)(2,1)}, bf16[1,128,512]{2,1,0:T(8,128)(2,1)}, bf16[1,128,512]{2,1,0:T(8,128)(2,1)}, bf16[1,128,512]{2,1,0:T(8,128)(2,1)S(1)}) fusion(bf16[4,128,512]{2,1,0:T(8,128)(2,1)} %copy-done.7), kind=kLoop, calls=%fused_computation.9 | loop fusion | bytes 1048576 | tf_op jit(solution)/shard_map/slice | solution.py:203
  25.5 3.0 %all-to-all-done.meta_ref = f32[32,8,128]{2,1,0:T(8,128)S(1)} async-done(((f32[32,8,128]{2,1,0:T(8,128)}), f32[32,8,128]{2,1,0:T(8,128)S(1)}, u32[]{:S(2)}, u32[]{:S(2)}) %all-to-all-start) | async-done | bytes 131104 | tf_op jit(solution)/shard_map/all_to_all | solution.py:33
  28.9 2.3 %collective-permute-start.9 = (bf16[64,4096]{1,0:T(8,128)(2,1)S(1)}, bf16[64,4096]{1,0:T(8,128)(2,1)}, u32[]{:S(2)}, u32[]{:S(2)}) collective-permute-start(bf16[64,4096]{1,0:T(8,128)(2,1)S(1)} %collective-permute-done.1.rl), channel_id=1, source_target_pairs={{0,3},{1,0},{2,1},{3,2},{4,7},{5,4},{6,5},{7,6},{8,11},{9,8},{10,9... | collective-permute-start | bytes 1572872 | tf_op jit(solution)/shard_map/ppermute | solution.py:29
  31.3 1.1 %fusion.1 = (bf16[1,128,512]{2,1,0:T(8,128)(2,1)S(1)}, bf16[1,128,512]{2,1,0:T(8,128)(2,1)S(1)}, bf16[1,128,512]{2,1,0:T(8,128)(2,1)S(1)}, bf16[1,128,512]{2,1,0:T(8,128)(2,1)S(1)}) fusion(bf16[4,128,512]{2,1,0:T(8,128)(2,1)} %collective-permute-done.4), kind=kLoop, calls=%fused_computation.10 | loop fusion | bytes 1048576 | tf_op jit(solution)/shard_map/slice | solution.py:203
  32.4 0.9 pad_maximum_fusion.1
  33.3 0.5 collective-permute-start.5
  33.8 0.9 pad_maximum_fusion.3
  34.7 0.9 pad_maximum_fusion.2
  35.7 1.6 %collective-permute-done.2.ll = bf16[64,4096]{1,0:T(8,128)(2,1)S(1)} collective-permute-done((bf16[64,4096]{1,0:T(8,128)(2,1)}, bf16[64,4096]{1,0:T(8,128)(2,1)S(1)}, u32[]{:S(2)}, u32[]{:S(2)}) %collective-permute-start.2) | collective-permute-done | bytes 524320 | tf_op jit(solution)/shard_map/ppermute | solution.py:29
  37.3 3.0 %collective-permute-start.6 = (bf16[2,128,512]{2,1,0:T(8,128)(2,1)S(1)}, bf16[2,128,512]{2,1,0:T(8,128)(2,1)S(1)}, u32[]{:S(2)}, u32[]{:S(2)}) collective-permute-start(bf16[2,128,512]{2,1,0:T(8,128)(2,1)S(1)} %pad_maximum_fusion.2), channel_id=1, source_target_pairs={{0,16},{8,24},{16,0},{24,8},{1,17},{9,25},{17,1},{25,9},{2,18},{10... | collective-permute-start | bytes 786440 | tf_op jit(solution)/shard_map/ppermute | solution.py:29
  40.3 0.7 collective-permute-start.7
  41.0 0.7 pad_maximum_fusion.t0_ref
  41.7 0.7 copy-done.10
  42.5 4.8 %collective-permute-done.6.t2_ref = bf16[2,128,512]{2,1,0:T(8,128)(2,1)S(1)} collective-permute-done((bf16[2,128,512]{2,1,0:T(8,128)(2,1)S(1)}, bf16[2,128,512]{2,1,0:T(8,128)(2,1)S(1)}, u32[]{:S(2)}, u32[]{:S(2)}) %collective-permute-start.6) | collective-permute-done | bytes 262176 | tf_op jit(solution)/shard_map/ppermute | solution.py:29
  47.3 0.7 copy-done.12
  47.9 4.0 %collective-permute-done.7.t3_ref = bf16[2,128,512]{2,1,0:T(8,128)(2,1)S(1)} collective-permute-done((bf16[2,128,512]{2,1,0:T(8,128)(2,1)S(1)}, bf16[2,128,512]{2,1,0:T(8,128)(2,1)S(1)}, u32[]{:S(2)}, u32[]{:S(2)}) %collective-permute-start.7) | collective-permute-done | bytes 262176 | tf_op jit(solution)/shard_map/ppermute | solution.py:29
  52.0 0.7 copy-done.14
  52.6 1.7 %shard_map.86.info_ref = f32[4,8,128]{2,1,0:T(8,128)} custom-call(s32[4]{0:T(128)} %copy-done.16, f32[32,8,128]{2,1,0:T(8,128)} %copy-done.3), custom_call_target="tpu_custom_call" | custom-call | flops 2097152 | bytes 131072 | tf_op jit(solution)/shard_map/pallas_call | solution.py:61
  54.3 2.2 %copy-done.1 = bf16[512,4096]{1,0:T(8,128)(2,1)S(1)} copy-done((bf16[512,4096]{1,0:T(8,128)(2,1)S(1)}, bf16[512,4096]{1,0:T(8,128)(2,1)}, u32[]{:S(2)}) %copy-start.1) | copy-done | bytes 4194328
  56.5 0.7 copy-done.8
  57.2 0.6 copy-done.17
  57.8 1.5 %shard_map.87.near_ref = f32[4,2,128]{2,1,0:T(2,128)S(1)} custom-call(s32[4]{0:T(128)S(1)} %copy-done.17, f32[4,8,128]{2,1,0:T(8,128)S(1)} %copy-done.8, bf16[2,4,64,4096]{3,2,1,0:T(8,128)(2,1)S(1)} %bitcast.16, bf16[128,4096]{1,0:T(8,128)(2,1)S(1)} %copy-done.2, bf16[64,4096]{1,0:T(8,128)(2,1)S(1)} %collective-permute-done.lu, ...), custom_call_target="tpu_custom_call" | custom-call | flops 402653184 | bytes 6291456 | tf_op jit(solution)/shard_map/pallas_call | solution.py:101
  59.4 1.7 %shard_map.88 = f32[8,4,2,128]{3,2,1,0:T(2,128)S(1)} custom-call(s32[4]{0:T(128)S(1)} %copy-done.18, f32[4,8,128]{2,1,0:T(8,128)S(1)} %copy-done.9, bf16[2,4,64,4096]{3,2,1,0:T(8,128)(2,1)S(1)} %bitcast.17, bf16[64,4096]{1,0:T(8,128)(2,1)} %collective-permute-done.8.up.fu, bf16[64,4096]{1,0:T(8,128)(2,1)} %collective-permute-done.9.low.fl, ...), custom_call_target="tpu_custom_call" | custom-call | flops 134217728 | bytes 2097152 | tf_op jit(solution)/shard_map/pallas_call | solution.py:126
  61.2 12.6 %all_to_all.20.home_ref = f32[32,2,128]{2,1,0:T(2,128)S(1)} all-to-all(f32[32,2,128]{2,1,0:T(2,128)S(1)} %bitcast.18), channel_id=1, replica_groups=mesh['dp_0'=8,'dp_1'=4,'dp_2'=2,'expert'=4] {'dp_1','dp_2','expert'}, dimensions={0} | all-to-all | bytes 65536 | tf_op jit(solution)/shard_map/all_to_all | solution.py:33
  73.8 1.5 %shard_map.89 = (bf16[8,128]{1,0:T(8,128)(2,1)S(1)}, bf16[32,8,512]{2,1,0:T(8,128)(2,1)}) custom-call(s32[4]{0:T(128)S(1)} %copy-done.18, f32[32,8,128]{2,1,0:T(8,128)S(1)} %copy-done.4, f32[32,2,128]{2,1,0:T(2,128)S(1)} %all_to_all.20.home_ref, bf16[2,128,512]{2,1,0:T(8,128)(2,1)S(1)} %copy-done.6, bf16[2,128,512]{2,1,0:T(8,128)(2,1)S(1)} %copy-done.11, ...), custom_call_target="tpu_custom_call" | custom-call | flops 8388608 | bytes 2097152 | tf_op jit(solution)/shard_map/pallas_call | solution.py:241
  75.3 8.9 %all-to-all-start.2 = ((bf16[32,8,512]{2,1,0:T(8,128)(2,1)}), bf16[32,8,512]{2,1,0:T(8,128)(2,1)S(1)}, u32[]{:S(2)}, u32[]{:S(2)}) async-start(bf16[32,8,512]{2,1,0:T(8,128)(2,1)} %get-tuple-element.40), calls=%async_computation.2 | async-start | bytes 524288 | tf_op jit(solution)/shard_map/all_to_all | solution.py:33
  84.3 3.7 %shard_map.91 = bf16[2,4,64,4096]{3,2,1,0:T(8,128)(2,1)} custom-call(s32[4]{0:T(128)S(1)} %copy-done.18, f32[4,8,128]{2,1,0:T(8,128)S(1)} %copy-done.9, bf16[128,4096]{1,0:T(8,128)(2,1)S(1)} %copy-done.2, bf16[64,4096]{1,0:T(8,128)(2,1)S(1)} %collective-permute-done.lu, bf16[64,4096]{1,0:T(8,128)(2,1)S(1)} %collective-permute-done.2.ll, ...), custom_call_target="tpu_custom_call" | custom-call | flops 536870912 | bytes 8388608 | tf_op jit(solution)/shard_map/pallas_call | solution.py:162
  88.0 7.5 %all-to-all-done.2.parts_ref = bf16[32,8,512]{2,1,0:T(8,128)(2,1)S(1)} async-done(((bf16[32,8,512]{2,1,0:T(8,128)(2,1)}), bf16[32,8,512]{2,1,0:T(8,128)(2,1)S(1)}, u32[]{:S(2)}, u32[]{:S(2)}) %all-to-all-start.2) | async-done | bytes 262176 | tf_op jit(solution)/shard_map/all_to_all | solution.py:33
  95.5 0.7 copy-done.19
  96.2 1.7 %shard_map.90 = f32[8,8,512]{2,1,0:T(8,128)} custom-call(bf16[32,8,512]{2,1,0:T(8,128)(2,1)} %copy-done.19), custom_call_target="tpu_custom_call" | custom-call | flops 131072 | bytes 524288 | tf_op jit(solution)/shard_map/pallas_call | solution.py:264
  97.8 5.7 %all-to-all-start.3 = ((f32[8,8,512]{2,1,0:T(8,128)}), f32[8,8,512]{2,1,0:T(8,128)S(1)}, u32[]{:S(2)}, u32[]{:S(2)}) async-start(f32[8,8,512]{2,1,0:T(8,128)} %shard_map.90), calls=%async_computation.3 | async-start | bytes 262144 | tf_op jit(solution)/shard_map/all_to_all | solution.py:33
  103.5 1.4 %convolution_convert_fusion = bf16[128,4096]{1,0:T(8,128)(2,1)} fusion(bf16[8,128]{1,0:T(8,128)(2,1)S(1)} %get-tuple-element.39, bf16[8,4096]{1,0:T(8,128)(2,1)S(1)} %copy-done), kind=kOutput, calls=%fused_computation | convolution fusion | flops 8912896 | bytes 1116160 | tf_op jit(solution)/shard_map/dot_general | solution.py:315
  105.0 3.8 %all-to-all-done.3 = f32[8,8,512]{2,1,0:T(8,128)S(1)} async-done(((f32[8,8,512]{2,1,0:T(8,128)}), f32[8,8,512]{2,1,0:T(8,128)S(1)}, u32[]{:S(2)}, u32[]{:S(2)}) %all-to-all-start.3) | async-done | bytes 131104 | tf_op jit(solution)/shard_map/all_to_all | solution.py:33
  108.8 0.7 copy.10
  (43 shorter events, 0.7 us)
Async XLA Ops:
  0.6 102.9 %copy-start = (bf16[8,4096]{1,0:T(8,128)(2,1)S(1)}, bf16[8,4096]{1,0:T(8,128)(2,1)}, u32[]{:S(2)}) copy-start(bf16[8,4096]{1,0:T(8,128)(2,1)} %param.10) | copy-start | bytes 196612
  0.6 53.7 %copy-start.2 = (bf16[128,4096]{1,0:T(8,128)(2,1)S(1)}, bf16[128,4096]{1,0:T(8,128)(2,1)}, u32[]{:S(2)}) copy-start(bf16[128,4096]{1,0:T(8,128)(2,1)} %own.3) | copy-start | bytes 3145732
  2.6 25.9 %collective-permute-start = (bf16[64,4096]{1,0:T(8,128)(2,1)}, bf16[64,4096]{1,0:T(8,128)(2,1)S(1)}, u32[]{:S(2)}, u32[]{:S(2)}) collective-permute-start(bf16[64,4096]{1,0:T(8,128)(2,1)} %slice.30), channel_id=1, source_target_pairs={{0,1},{1,2},{2,3},{3,0},{4,5},{5,6},{6,7},{7,4},{8,9},{9,10},{10,1... | collective-permute-start | bytes 1572872 | tf_op jit(solution)/shard_map/ppermute | solution.py:29
  6.6 21.9 %collective-permute-start.1 = (bf16[64,4096]{1,0:T(8,128)(2,1)}, bf16[64,4096]{1,0:T(8,128)(2,1)S(1)}, u32[]{:S(2)}, u32[]{:S(2)}) collective-permute-start(bf16[64,4096]{1,0:T(8,128)(2,1)} %slice.31), channel_id=1, source_target_pairs={{0,3},{1,0},{2,1},{3,2},{4,7},{5,4},{6,5},{7,6},{8,11},{9,8},{10,9... | collective-permute-start | bytes 1572872 | tf_op jit(solution)/shard_map/ppermute | solution.py:29
  8.1 1.2 %copy-start.5 = (bf16[128,4096]{1,0:T(8,128)(2,1)S(1)}, bf16[128,4096]{1,0:T(8,128)(2,1)}, u32[]{:S(2)}) copy-start(bf16[128,4096]{1,0:T(8,128)(2,1)} %tokens_ref.1) | copy-start | bytes 3145732
  9.4 42.6 %copy-start.16 = (s32[4]{0:T(128)}, s32[4]{0:T(128)S(1)}, u32[]{:S(2)}) copy-start(s32[4]{0:T(128)S(1)} %pad_add_fusion.place_ref) | copy-start | bytes 52
  10.8 0.8 copy-start.7
  11.6 19.7 %collective-permute-start.4 = (bf16[4,128,512]{2,1,0:T(8,128)(2,1)}, bf16[4,128,512]{2,1,0:T(8,128)(2,1)}, u32[]{:S(2)}, u32[]{:S(2)}) collective-permute-start(bf16[4,128,512]{2,1,0:T(8,128)(2,1)} %get-tuple-element.29), channel_id=1, source_target_pairs={{0,4},{4,0},{1,5},{5,1},{2,6},{6,2},{3,7},{7,3},{8,12},{12,8},{9,1... | collective-permute-start | bytes 1572872 | tf_op jit(solution)/shard_map/ppermute | solution.py:29
  16.6 11.8 %all-to-all-start = ((f32[32,8,128]{2,1,0:T(8,128)}), f32[32,8,128]{2,1,0:T(8,128)S(1)}, u32[]{:S(2)}, u32[]{:S(2)}) async-start(f32[32,8,128]{2,1,0:T(8,128)} %broadcast_in_dim.7), calls=%async_computation | async-start | bytes 262144 | tf_op jit(solution)/shard_map/all_to_all | solution.py:33
  20.9 16.4 %collective-permute-start.2 = (bf16[64,4096]{1,0:T(8,128)(2,1)}, bf16[64,4096]{1,0:T(8,128)(2,1)S(1)}, u32[]{:S(2)}, u32[]{:S(2)}) collective-permute-start(bf16[64,4096]{1,0:T(8,128)(2,1)} %slice.31), channel_id=1, source_target_pairs={{0,1},{1,2},{2,3},{3,0},{4,5},{5,6},{6,7},{7,4},{8,9},{9,10},{10,1... | collective-permute-start | bytes 1572872 | tf_op jit(solution)/shard_map/ppermute | solution.py:29
  22.4 17.9 %collective-permute-start.3 = (bf16[64,4096]{1,0:T(8,128)(2,1)}, bf16[64,4096]{1,0:T(8,128)(2,1)S(1)}, u32[]{:S(2)}, u32[]{:S(2)}) collective-permute-start(bf16[64,4096]{1,0:T(8,128)(2,1)} %slice.30), channel_id=1, source_target_pairs={{0,3},{1,0},{2,1},{3,2},{4,7},{5,4},{6,5},{7,6},{8,11},{9,8},{10,9... | collective-permute-start | bytes 1572872 | tf_op jit(solution)/shard_map/ppermute | solution.py:29
  28.5 23.5 %copy-start.3 = (f32[32,8,128]{2,1,0:T(8,128)}, f32[32,8,128]{2,1,0:T(8,128)S(1)}, u32[]{:S(2)}) copy-start(f32[32,8,128]{2,1,0:T(8,128)S(1)} %all-to-all-done.meta_ref) | copy-start | bytes 393220
  28.5 30.9 %collective-permute-start.8 = (bf16[64,4096]{1,0:T(8,128)(2,1)S(1)}, bf16[64,4096]{1,0:T(8,128)(2,1)}, u32[]{:S(2)}, u32[]{:S(2)}) collective-permute-start(bf16[64,4096]{1,0:T(8,128)(2,1)S(1)} %collective-permute-done.lu), channel_id=1, source_target_pairs={{0,1},{1,2},{2,3},{3,0},{4,5},{5,6},{6,7},{7,4},{8,9},{9,10},{10,1... | collective-permute-start | bytes 1572872 | tf_op jit(solution)/shard_map/ppermute | solution.py:29
  28.9 30.5 %collective-permute-start.9 = (bf16[64,4096]{1,0:T(8,128)(2,1)S(1)}, bf16[64,4096]{1,0:T(8,128)(2,1)}, u32[]{:S(2)}, u32[]{:S(2)}) collective-permute-start(bf16[64,4096]{1,0:T(8,128)(2,1)S(1)} %collective-permute-done.1.rl), channel_id=1, source_target_pairs={{0,3},{1,0},{2,1},{3,2},{4,7},{5,4},{6,5},{7,6},{8,11},{9,8},{10,9... | collective-permute-start | bytes 1572872 | tf_op jit(solution)/shard_map/ppermute | solution.py:29
  33.3 8.4 %collective-permute-start.5 = (bf16[2,128,512]{2,1,0:T(8,128)(2,1)S(1)}, bf16[2,128,512]{2,1,0:T(8,128)(2,1)S(1)}, u32[]{:S(2)}, u32[]{:S(2)}) collective-permute-start(bf16[2,128,512]{2,1,0:T(8,128)(2,1)S(1)} %pad_maximum_fusion.1), channel_id=1, source_target_pairs={{0,8},{8,16},{16,24},{24,0},{1,9},{9,17},{17,25},{25,1},{2,10},{10... | collective-permute-start | bytes 786440 | tf_op jit(solution)/shard_map/ppermute | solution.py:29
  37.3 10.0 %collective-permute-start.6 = (bf16[2,128,512]{2,1,0:T(8,128)(2,1)S(1)}, bf16[2,128,512]{2,1,0:T(8,128)(2,1)S(1)}, u32[]{:S(2)}, u32[]{:S(2)}) collective-permute-start(bf16[2,128,512]{2,1,0:T(8,128)(2,1)S(1)} %pad_maximum_fusion.2), channel_id=1, source_target_pairs={{0,16},{8,24},{16,0},{24,8},{1,17},{9,25},{17,1},{25,9},{2,18},{10... | collective-permute-start | bytes 786440 | tf_op jit(solution)/shard_map/ppermute | solution.py:29
  40.3 11.6 %collective-permute-start.7 = (bf16[2,128,512]{2,1,0:T(8,128)(2,1)S(1)}, bf16[2,128,512]{2,1,0:T(8,128)(2,1)S(1)}, u32[]{:S(2)}, u32[]{:S(2)}) collective-permute-start(bf16[2,128,512]{2,1,0:T(8,128)(2,1)S(1)} %pad_maximum_fusion.3), channel_id=1, source_target_pairs={{0,24},{8,0},{16,8},{24,16},{1,25},{9,1},{17,9},{25,17},{2,26},{10... | collective-permute-start | bytes 786440 | tf_op jit(solution)/shard_map/ppermute | solution.py:29
  41.7 0.7 copy-start.10
  47.3 0.7 copy-start.12
  51.9 0.7 copy-start.14
  54.3 5.1 %copy-start.18 = (s32[4]{0:T(128)S(1)}, s32[4]{0:T(128)}, u32[]{:S(2)}) copy-start(s32[4]{0:T(128)} %copy-done.16) | copy-start | bytes 52
  54.3 2.2 %copy-start.1 = (bf16[512,4096]{1,0:T(8,128)(2,1)S(1)}, bf16[512,4096]{1,0:T(8,128)(2,1)}, u32[]{:S(2)}) copy-start(bf16[512,4096]{1,0:T(8,128)(2,1)} %param.11) | copy-start | bytes 12582916
  56.5 0.7 copy-start.8
  57.2 0.6 copy-start.17
  57.8 1.6 %copy-start.9 = (f32[4,8,128]{2,1,0:T(8,128)S(1)}, f32[4,8,128]{2,1,0:T(8,128)}, u32[]{:S(2)}) copy-start(f32[4,8,128]{2,1,0:T(8,128)} %shard_map.86.info_ref) | copy-start | bytes 49156
  59.3 14.5 %copy-start.4 = (f32[32,8,128]{2,1,0:T(8,128)S(1)}, f32[32,8,128]{2,1,0:T(8,128)}, u32[]{:S(2)}) copy-start(f32[32,8,128]{2,1,0:T(8,128)} %copy-done.3) | copy-start | bytes 393220
  59.3 14.5 %copy-start.6 = (bf16[2,128,512]{2,1,0:T(8,128)(2,1)S(1)}, bf16[2,128,512]{2,1,0:T(8,128)(2,1)}, u32[]{:S(2)}) copy-start(bf16[2,128,512]{2,1,0:T(8,128)(2,1)} %pad_maximum_fusion.t0_ref) | copy-start | bytes 786436
  59.3 14.5 %copy-start.11 = (bf16[2,128,512]{2,1,0:T(8,128)(2,1)S(1)}, bf16[2,128,512]{2,1,0:T(8,128)(2,1)}, u32[]{:S(2)}) copy-start(bf16[2,128,512]{2,1,0:T(8,128)(2,1)} %copy-done.10) | copy-start | bytes 786436
  59.3 14.5 %copy-start.13 = (bf16[2,128,512]{2,1,0:T(8,128)(2,1)S(1)}, bf16[2,128,512]{2,1,0:T(8,128)(2,1)}, u32[]{:S(2)}) copy-start(bf16[2,128,512]{2,1,0:T(8,128)(2,1)} %copy-done.12) | copy-start | bytes 786436
  59.4 14.5 %copy-start.15 = (bf16[2,128,512]{2,1,0:T(8,128)(2,1)S(1)}, bf16[2,128,512]{2,1,0:T(8,128)(2,1)}, u32[]{:S(2)}) copy-start(bf16[2,128,512]{2,1,0:T(8,128)(2,1)} %copy-done.14) | copy-start | bytes 786436
  75.3 20.1 %all-to-all-start.2 = ((bf16[32,8,512]{2,1,0:T(8,128)(2,1)}), bf16[32,8,512]{2,1,0:T(8,128)(2,1)S(1)}, u32[]{:S(2)}, u32[]{:S(2)}) async-start(bf16[32,8,512]{2,1,0:T(8,128)(2,1)} %get-tuple-element.40), calls=%async_computation.2 | async-start | bytes 524288 | tf_op jit(solution)/shard_map/all_to_all | solution.py:33
  95.5 0.7 copy-start.19
  97.8 11.0 %all-to-all-start.3 = ((f32[8,8,512]{2,1,0:T(8,128)}), f32[8,8,512]{2,1,0:T(8,128)S(1)}, u32[]{:S(2)}, u32[]{:S(2)}) async-start(f32[8,8,512]{2,1,0:T(8,128)} %shard_map.90), calls=%async_computation.3 | async-start | bytes 262144 | tf_op jit(solution)/shard_map/all_to_all | solution.py:33

commit v3 on v2

v3 whole, which is shorter than its diff:
```python
import functools

import jax
import jax.numpy as jnp
from jax import lax
from jax.experimental import pallas as pl
from jax.experimental.pallas import tpu as pltpu
from jax.sharding import Mesh
from jax.sharding import PartitionSpec as P

DP_EXPERT = ("dp_0", "dp_1", "dp_2", "expert")
PLANE = ("dp_1", "dp_2")
HOUSE = ("dp_1", "dp_2", "expert")
REST = ("dp_0", "expert")
BF16 = jnp.bfloat16
F32 = jnp.float32
VMEM = pl.BlockSpec(memory_space=pltpu.VMEM)
ANY = pl.BlockSpec(memory_space=pl.ANY)
PARAMS = pltpu.CompilerParams(vmem_limit_bytes=16 * 2**20)


def cost(flops, size):
    return pl.CostEstimate(flops=flops, bytes_accessed=size, transcendentals=0)


def shift(a, step):
    n = lax.axis_size("expert")
    return lax.ppermute(a, "expert", [(i, (i + step) % n) for i in range(n)])


def to_all(a, axes):
    return lax.all_to_all(a, axes, 0, 0, tiled=True)


def wide(v, rows=8):
    return jnp.broadcast_to(v, (rows, v.shape[1]))


def split_kernel(grad_ref, upper_ref, lower_ref, sems):
    copies = []
    for j in range(8):
        out_ref, at = (upper_ref, 16 * j) if j < 4 else (lower_ref, 16 * (j - 4))
        copies.append(
            pltpu.make_async_copy(
                grad_ref.at[16 * j : 16 * j + 16], out_ref.at[at : at + 16], sems.at[j]
            )
        )
    for copy in copies:
        copy.start()
    for copy in copies:
        copy.wait()


def split(grad):
    half = jax.ShapeDtypeStruct((64, grad.shape[1]), grad.dtype)
    return pl.pallas_call(
        split_kernel,
        out_shape=[half, half],
        in_specs=[ANY],
        out_specs=[ANY, ANY],
        scratch_shapes=[pltpu.SemaphoreType.DMA((8,))],
        cost_estimate=cost(0, 4 * grad.size),
    )(grad)


def columns_kernel(tokens_ref, out_ref, sems):
    count, _, piece = out_ref.shape
    copies = [
        pltpu.make_async_copy(
            tokens_ref.at[:, j * piece : (j + 1) * piece], out_ref.at[j], sems.at[j]
        )
        for j in range(count)
    ]
    for copy in copies:
        copy.start()
    for copy in copies:
        copy.wait()


def columns(tokens, count):
    return pl.pallas_call(
        columns_kernel,
        out_shape=jax.ShapeDtypeStruct((count, 128, tokens.shape[1] // count), tokens.dtype),
        in_specs=[ANY],
        out_specs=ANY,
        scratch_shapes=[pltpu.SemaphoreType.DMA((count,))],
        cost_estimate=cost(0, 4 * tokens.size),
    )(tokens)


def meta_kernel(experts_ref, gates_ref, out_ref):
    meta = jnp.concatenate(
        [experts_ref[...].astype(F32), gates_ref[...].astype(F32), jnp.zeros((4, 128), F32)], axis=0
    )
    for j in range(out_ref.shape[0]):
        out_ref[j] = meta


def meta_copies(experts, gates, count):
    return pl.pallas_call(
        meta_kernel,
        out_shape=jax.ShapeDtypeStruct((count, 8, 128), F32),
        in_specs=[VMEM, VMEM],
        out_specs=VMEM,
        cost_estimate=cost(0, 4096 * count),
    )(experts.T, gates.T)


def house_index():
    return lax.axis_index("dp_1") * 2 + lax.axis_index("dp_2")


def routing(meta, me):
    row = lax.broadcasted_iota(jnp.int32, (8, 128), 0)
    held = (2 * me + row).astype(F32)
    earlier = lax.broadcasted_iota(jnp.int32, (128, 128), 0)
    later = lax.broadcasted_iota(jnp.int32, (128, 128), 1)
    before = jnp.where(earlier < later, 1.0, 0.0).astype(BF16)
    is0 = wide(meta[0:1]) == held
    is1 = wide(meta[1:2]) == held
    named = jnp.logical_or(is0, is1)
    count = jnp.dot(jnp.where(named, 1.0, 0.0).astype(BF16), before, preferred_element_type=F32)
    position = jnp.where(named, count, -1.0)
    gate = jnp.where(is0, wide(meta[2:3]), wide(meta[3:4]))
    return jnp.concatenate([position[0:2], gate[0:2], jnp.zeros((4, 128), F32)], axis=0)


def chosen(info, h):
    slot = lax.broadcasted_iota(jnp.int32, (64, 128), 0).astype(F32)
    return slot == wide(info[h : h + 1], 64)


def stacked(pieces):
    return pieces[0][...] if len(pieces) == 1 else jnp.concatenate([p[...] for p in pieces], axis=0)


def fetch(saved_ref, s, stored_ref, sems, at):
    copies = [
        pltpu.make_async_copy(
            saved_ref.at[h, s], stored_ref.at[64 * h : 64 * h + 64], sems.at[at + h]
        )
        for h in range(2)
    ]
    for copy in copies:
        copy.start()
    return copies


def products(info, stored_ref, pieces):
    total = lax.dot_general(
        stored_ref[...], stacked(pieces), (((1,), (1,)), ((), ())), preferred_element_type=F32
    )
    return [
        jnp.sum(jnp.where(chosen(info, h), total[64 * h : 64 * h + 64], 0.0), axis=0, keepdims=True)
        for h in range(2)
    ]


def near_kernel(meta_ref, saved_ref, own, lu, ll, ru, rl, info_ref, out_ref, stored_ref, sems):
    me = lax.axis_index("expert")
    groups = info_ref.shape[0]
    order = ((0, (own,)), (1, (ru, rl)), (3, (lu, ll)))
    copies = [
        fetch(saved_ref, lax.rem(me + d, groups), stored_ref.at[j], sems, 2 * j)
        for j, (d, _) in enumerate(order)
    ]
    house = house_index()
    for s in range(groups):
        info_ref[s] = routing(meta_ref[house * groups + s], me)
    for j, (d, pieces) in enumerate(order):
        for copy in copies[j]:
            copy.wait()
        info = info_ref[lax.rem(me + d, groups)]
        for h, line in enumerate(products(info, stored_ref.at[j], pieces)):
            out_ref[d, h : h + 1, :] = line
    out_ref[2] = jnp.zeros((2, 128), F32)


def near_products(meta, saved, pieces, groups):
    width = saved.shape[-1]
    return pl.pallas_call(
        near_kernel,
        out_shape=[
            jax.ShapeDtypeStruct((groups, 8, 128), F32),
            jax.ShapeDtypeStruct((groups, 2, 128), F32),
        ],
        in_specs=[VMEM, ANY] + [VMEM] * 5,
        out_specs=[VMEM, VMEM],
        scratch_shapes=[pltpu.VMEM((3, 128, width), BF16), pltpu.SemaphoreType.DMA((6,))],
        compiler_params=PARAMS,
        cost_estimate=cost(6 * 128 * 128 * width, 12 * 128 * width),
    )(meta, saved, *pieces)


def far_kernel(info_ref, saved_ref, up, low, near_ref, out_ref, stored_ref, sems):
    me = lax.axis_index("expert")
    groups = info_ref.shape[0]
    s = lax.rem(me + 2, groups)
    copies = fetch(saved_ref, s, stored_ref, sems, 0)
    for d in (0, 1, 3):
        t = lax.rem(me + d, groups)
        for j in range(out_ref.shape[0]):
            out_ref[j, t] = near_ref[d]
    for copy in copies:
        copy.wait()
    lines = jnp.concatenate(products(info_ref[s], stored_ref, (up, low)), axis=0)
    for j in range(out_ref.shape[0]):
        out_ref[j, s] = lines


def far_products(info, saved, pieces, near, copies):
    groups, width = info.shape[0], saved.shape[-1]
    return pl.pallas_call(
        far_kernel,
        out_shape=jax.ShapeDtypeStruct((copies, groups, 2, 128), F32),
        in_specs=[VMEM, ANY] + [VMEM] * 3,
        out_specs=VMEM,
        scratch_shapes=[pltpu.VMEM((128, width), BF16), pltpu.SemaphoreType.DMA((2,))],
        compiler_params=PARAMS,
        cost_estimate=cost(2 * 128 * 128 * width, 4 * 128 * width),
    )(info, saved, *pieces, near)


def scaled_kernel(info_ref, own, lu, ll, ru, rl, fu, fl, out_ref, pick_ref, held_ref, sems):
    me = lax.axis_index("expert")
    groups = info_ref.shape[0]
    started = []
    for d, pieces in ((0, (own,)), (1, (ru, rl)), (3, (lu, ll)), (2, (fu, fl))):
        s = lax.rem(me + d, groups)
        info = info_ref[s]
        for h in range(2):
            pick_ref[64 * h : 64 * h + 64, :] = jnp.where(
                chosen(info, h), wide(info[2 + h : 3 + h], 64), 0.0
            ).astype(BF16)
        held_ref[d] = jnp.dot(
            pick_ref[...], stacked(pieces), preferred_element_type=F32
        ).astype(BF16)
        for h in range(2):
            copy = pltpu.make_async_copy(
                held_ref.at[d, 64 * h : 64 * h + 64], out_ref.at[h, s], sems.at[2 * d + h]
            )
            copy.start()
            started.append(copy)
    for copy in started:
        copy.wait()


def scaled_rows(info, pieces, shape):
    groups, width = info.shape[0], shape[-1]
    return pl.pallas_call(
        scaled_kernel,
        out_shape=jax.ShapeDtypeStruct(shape, BF16),
        in_specs=[VMEM] * 8,
        out_specs=ANY,
        scratch_shapes=[
            pltpu.VMEM((128, 128), BF16),
            pltpu.VMEM((groups, 128, width), BF16),
            pltpu.SemaphoreType.DMA((2 * groups,)),
        ],
        compiler_params=PARAMS,
        cost_estimate=cost(8 * 128 * 128 * width, 16 * 128 * width),
    )(info, *pieces)


def logit_kernel(meta_ref, home_ref, tokens_ref, logit_ref, out_ref):
    house, me = house_index(), lax.axis_index("expert")
    blocks = tokens_ref.shape[0]
    groups = home_ref.shape[0] // blocks
    row = lax.broadcasted_iota(jnp.int32, (8, 128), 0).astype(F32)
    found = []
    for b in range(blocks):
        meta = meta_ref[b * groups + me]
        e0, e1, g0, g1 = meta[0:1], meta[1:2], meta[2:3], meta[3:4]
        grads = jnp.concatenate([home_ref[b * groups + y] for y in range(groups)], axis=0)
        is0, is1 = wide(e0) == row, wide(e1) == row
        gg0 = jnp.sum(jnp.where(is0, grads, 0.0), axis=0, keepdims=True)
        gg1 = jnp.sum(jnp.where(is1, grads, 0.0), axis=0, keepdims=True)
        blended = g0 * gg0 + g1 * gg1
        s0 = g0 * (gg0 - blended)
        s1 = g1 * (gg1 - blended)
        logit = jnp.where(is0, wide(s0), 0.0) + jnp.where(is1, wide(s1), 0.0)
        found.append(logit.astype(BF16))

        @pl.when(house == b)
        def _():
            logit_ref[...] = logit.astype(BF16)

    every = jnp.concatenate(found, axis=1)
    features = tokens_ref[...].reshape(blocks * 128, tokens_ref.shape[2])
    part = jnp.dot(every, features, preferred_element_type=F32).astype(BF16)
    for j in range(out_ref.shape[0]):
        out_ref[j] = part


def logits(meta, home, tokens, copies):
    piece = tokens.shape[2]
    return pl.pallas_call(
        logit_kernel,
        out_shape=[
            jax.ShapeDtypeStruct((8, 128), BF16),
            jax.ShapeDtypeStruct((copies, 8, piece), BF16),
        ],
        in_specs=[VMEM, VMEM, VMEM],
        out_specs=[VMEM, VMEM],
        compiler_params=PARAMS,
        cost_estimate=cost(16 * tokens.size, 4 * tokens.size),
    )(meta, home, tokens)


def local(tokens, grad_out, experts, gates, router_weight, saved_outputs):
    width = tokens.shape[1]
    groups = lax.axis_size("expert")
    houses = lax.axis_size(PLANE)
    saved = saved_outputs.reshape(2, groups, 64, width)

    upper, lower = split(grad_out)
    left_upper = shift(upper, 1)
    right_lower = shift(lower, -1)
    tokens, upper, lower = lax.optimization_barrier((tokens, upper, lower))
    own_columns = columns(tokens, houses)
    own_columns, upper, lower = lax.optimization_barrier((own_columns, upper, lower))
    turned = to_all(own_columns, PLANE)
    left_lower = shift(lower, 1)
    right_upper = shift(upper, -1)
    meta = meta_copies(experts, gates, houses * groups)
    left_upper, right_lower, turned, meta = lax.optimization_barrier(
        (left_upper, right_lower, turned, meta)
    )
    far_upper = shift(left_upper, 1)
    far_lower = shift(right_lower, -1)
    every_meta = to_all(meta, HOUSE)

    near_pieces = (grad_out, left_upper, left_lower, right_upper, right_lower)
    info, near = near_products(every_meta, saved, near_pieces, groups)
    sent = far_products(info, saved, (far_upper, far_lower), near, houses)
    home = to_all(sent.reshape(houses * groups, 2, 128), HOUSE)
    expert_grad = scaled_rows(info, (*near_pieces, far_upper, far_lower), saved.shape)

    logit, parts = logits(every_meta, home, turned, lax.axis_size(REST))
    scale = float(lax.axis_size(DP_EXPERT) * tokens.shape[0]) ** (-0.5)
    total = to_all(parts, REST).astype(F32).sum(axis=0) * scale
    whole = to_all(jnp.broadcast_to(total, (houses, *total.shape)), PLANE)
    router_grad = whole.swapaxes(0, 1).reshape(8, width)
    input_grad = lax.dot_general(
        logit, router_weight, (((0,), (0,)), ((), ())), preferred_element_type=F32
    ).astype(BF16)
    return input_grad, router_grad, expert_grad.reshape(saved_outputs.shape)


def solution(mesh):
    finer = Mesh(
        mesh.devices.reshape(8, 4, 2, mesh.shape["expert"]), ("dp_0", "dp_1", "dp_2", "expert")
    )
    rows = P(DP_EXPERT, None)
    return jax.shard_map(
        local,
        mesh=finer,
        in_specs=(rows, rows, rows, rows, P(), rows),
        out_specs=(rows, P(), rows),
        check_vma=False,
    )
```

time: 110 us -> 168 us (1.53)
  Pallas kernels: 13.2 us -> 77 us
  local copies, waits for them, and re-layouts: 16.6 us -> 4.22 us
  waiting for transfers between devices: 24.8 us -> 33 us
  other arithmetic: 5 us -> 0.05 us
    pallas_call x4, Pallas kernels: 6.25 us -> 70.8 us  [the longest x1 32.9 us: columns(): pl.pallas_call(columns_kernel, out_shape=jax.ShapeDtypeStruct((count, 128...]
    all_to_all x3 -> x4, waiting for transfers between devices: 14.3 us -> 24.8 us  [to_all(): return lax.all_to_all(a, axes, 0, 0, tiled=True)]
    all_to_all x3 -> x4, starting transfers between devices: 18.8 us -> 28.6 us  [to_all(): return lax.all_to_all(a, axes, 0, 0, tiled=True)]
    ppermute x10 -> x6, starting transfers between devices: 16.2 us -> 8.03 us  [shift(): return lax.ppermute(a, 'expert', [(i, (i + step) % n) for i in range(n)])]
    slice x4 -> x0, local copies, waits for them, and re-layouts: 6.81 us -> none  [the longest x2 2.99 us: plane_blocks(): blocks = [jnp.stack([kept[k], got[k]]) for k in range(columns)]]
    unnamed x41 -> x11, local copies, waits for them, and re-layouts: 8.99 us -> 3.56 us
    another operation x5 -> x0, other arithmetic: 3.59 us -> none  [the longest x4 3.52 us: plane_blocks(): blocks = [jnp.stack([kept[k], got[k]]) for k in range(columns)]]
    ppermute x10 -> x6, waiting for transfers between devices: 10.4 us -> 8.27 us  [shift(): return lax.ppermute(a, 'expert', [(i, (i + step) % n) for i in range(n)])]
  transfers between devices with their start and end apart: 13 -> 10, of which waited for: 6 -> 6; matrix products, arithmetic and copies ran while one was open for 11% -> 1% of each run, Pallas kernels for 8% -> 5%
where the time goes in v3:
time: 168 us; the launch traced here: 167 us
  Pallas kernels  77 us (46%)
  starting transfers between devices  36.6 us (22%)
  waiting for transfers between devices  33 us (20%)
  blocking collectives  14.2 us (8%)
  local copies, waits for them, and re-layouts  4.22 us (3%)
    pallas_call x1, Pallas kernels, columns(): pl.pallas_call(columns_kernel, out_shape=jax.ShapeDtypeStruct((count, 128...  32.9 us
    pallas_call x1, Pallas kernels, split(): pl.pallas_call(split_kernel, out_shape=[half, half], in_specs=[ANY], out_...  32.9 us
    all_to_all x4, starting transfers between devices, to_all(): return lax.all_to_all(a, axes, 0, 0, tiled=True)  28.6 us
    all_to_all x4, waiting for transfers between devices, to_all(): return lax.all_to_all(a, axes, 0, 0, tiled=True)  24.8 us
    all_to_all x1, blocking collectives, to_all(): return lax.all_to_all(a, axes, 0, 0, tiled=True)  14.2 us
    ppermute x6, waiting for transfers between devices, shift(): return lax.ppermute(a, 'expert', [(i, (i + step) % n) for i in range(n)])  8.27 us
    ppermute x6, starting transfers between devices, shift(): return lax.ppermute(a, 'expert', [(i, (i + step) % n) for i in range(n)])  8.03 us
    pallas_call x1, Pallas kernels, scaled_rows(): pl.pallas_call(scaled_kernel, out_shape=jax.ShapeDtypeStruct(shape, BF16)...  4.02 us
  transfers between devices with their start and end apart: 10, of which 6 were waited for; matrix products, arithmetic and copies ran while one was open for 1% of the time, Pallas kernels for 5%

profile of v3, /device:TPU:1, one launch (start us, length us, event | category | flops | bytes accessed | tf_op | source)
XLA Modules:
  0.0 167.3 jit_solution(14754274120747266560)
XLA Ops:
  0.6 0.0 copy-start
  0.6 0.0 copy-start.3
  0.7 32.9 %shard_map.85 = (bf16[64,4096]{1,0:T(8,128)(2,1)}, bf16[64,4096]{1,0:T(8,128)(2,1)}) custom-call(bf16[128,4096]{1,0:T(8,128)(2,1)} %own.3), custom_call_target="tpu_custom_call" | custom-call | bytes 2097152 | tf_op jit(solution)/shard_map/pallas_call | solution.py:56
  33.6 32.9 %shard_map.86 = bf16[8,128,512]{2,1,0:T(8,128)(2,1)} custom-call(bf16[128,4096]{1,0:T(8,128)(2,1)} %tokens_ref), custom_call_target="tpu_custom_call" | custom-call | bytes 2097152 | tf_op jit(solution)/shard_map/pallas_call | solution.py:81
  66.5 6.7 %all-to-all-start = ((bf16[8,128,512]{2,1,0:T(8,128)(2,1)}), bf16[8,128,512]{2,1,0:T(8,128)(2,1)S(1)}, u32[]{:S(2)}, u32[]{:S(2)}) async-start(bf16[8,128,512]{2,1,0:T(8,128)(2,1)} %shard_map.86), calls=%async_computation | async-start | bytes 2097152 | tf_op jit(solution)/shard_map/all_to_all | solution.py:32
  73.3 0.4 collective-permute-start
  73.7 2.3 %collective-permute-start.1 = (bf16[64,4096]{1,0:T(8,128)(2,1)}, bf16[64,4096]{1,0:T(8,128)(2,1)S(1)}, u32[]{:S(2)}, u32[]{:S(2)}) collective-permute-start(bf16[64,4096]{1,0:T(8,128)(2,1)} %get-tuple-element.27), channel_id=1, source_target_pairs={{0,3},{1,0},{2,1},{3,2},{4,7},{5,4},{6,5},{7,6},{8,11},{9,8},{10,9... | collective-permute-start | bytes 1572872 | tf_op jit(solution)/shard_map/ppermute | solution.py:28
  75.9 0.0 collective-permute-start.2
  75.9 2.7 %collective-permute-start.3 = (bf16[64,4096]{1,0:T(8,128)(2,1)}, bf16[64,4096]{1,0:T(8,128)(2,1)}, u32[]{:S(2)}, u32[]{:S(2)}) collective-permute-start(bf16[64,4096]{1,0:T(8,128)(2,1)} %get-tuple-element.28), channel_id=1, source_target_pairs={{0,3},{1,0},{2,1},{3,2},{4,7},{5,4},{6,5},{7,6},{8,11},{9,8},{10,9... | collective-permute-start | bytes 1572872 | tf_op jit(solution)/shard_map/ppermute | solution.py:28
  78.6 1.3 shard_map.87
  80.0 8.1 %collective-permute-done.lu = bf16[64,4096]{1,0:T(8,128)(2,1)S(1)} collective-permute-done((bf16[64,4096]{1,0:T(8,128)(2,1)}, bf16[64,4096]{1,0:T(8,128)(2,1)S(1)}, u32[]{:S(2)}, u32[]{:S(2)}) %collective-permute-start) | collective-permute-done | bytes 524320 | tf_op jit(solution)/shard_map/ppermute | solution.py:28
  88.0 0.0 collective-permute-done.1.rl
  88.0 0.3 all-to-all-done.tokens_ref
  88.4 0.4 collective-permute-start.4
  88.8 2.3 %collective-permute-start.5 = (bf16[64,4096]{1,0:T(8,128)(2,1)S(1)}, bf16[64,4096]{1,0:T(8,128)(2,1)}, u32[]{:S(2)}, u32[]{:S(2)}) collective-permute-start(bf16[64,4096]{1,0:T(8,128)(2,1)S(1)} %collective-permute-done.1.rl), channel_id=1, source_target_pairs={{0,3},{1,0},{2,1},{3,2},{4,7},{5,4},{6,5},{7,6},{8,11},{9,8},{10,9... | collective-permute-start | bytes 1572872 | tf_op jit(solution)/shard_map/ppermute | solution.py:28
  91.1 8.1 %all-to-all-start.1 = ((f32[32,8,128]{2,1,0:T(8,128)}), f32[32,8,128]{2,1,0:T(8,128)S(1)}, u32[]{:S(2)}, u32[]{:S(2)}) async-start(f32[32,8,128]{2,1,0:T(8,128)} %shard_map.87), calls=%async_computation.1 | async-start | bytes 262144 | tf_op jit(solution)/shard_map/all_to_all | solution.py:32
  99.2 0.2 collective-permute-done.2.ll
  99.4 0.0 collective-permute-done.3.ru
  99.4 13.4 %all-to-all-done.1.meta_ref = f32[32,8,128]{2,1,0:T(8,128)S(1)} async-done(((f32[32,8,128]{2,1,0:T(8,128)}), f32[32,8,128]{2,1,0:T(8,128)S(1)}, u32[]{:S(2)}, u32[]{:S(2)}) %all-to-all-start.1) | async-done | bytes 131104 | tf_op jit(solution)/shard_map/all_to_all | solution.py:32
  112.8 0.0 copy-done.3
  112.8 0.0 copy-start.1
  112.8 2.2 %copy-done.1 = bf16[512,4096]{1,0:T(8,128)(2,1)S(1)} copy-done((bf16[512,4096]{1,0:T(8,128)(2,1)S(1)}, bf16[512,4096]{1,0:T(8,128)(2,1)}, u32[]{:S(2)}) %copy-start.1) | copy-done | bytes 4194328
  114.9 0.0 copy-start.2
  114.9 3.6 %shard_map.88 = (f32[4,8,128]{2,1,0:T(8,128)S(1)}, f32[4,2,128]{2,1,0:T(2,128)S(1)}) custom-call(f32[32,8,128]{2,1,0:T(8,128)S(1)} %all-to-all-done.1.meta_ref, bf16[2,4,64,4096]{3,2,1,0:T(8,128)(2,1)S(1)} %bitcast.10, bf16[128,4096]{1,0:T(8,128)(2,1)S(1)} %copy-done.3, bf16[64,4096]{1,0:T(8,128)(2,1)S(1)} %collective-permute-done.lu, ...), custom_call_target="tpu_custom_call" | custom-call | flops 402653184 | bytes 6291456 | tf_op jit(solution)/shard_map/pallas_call | solution.py:181
  118.6 0.0 collective-permute-done.4.up.fu
  118.6 0.0 collective-permute-done.5.low.fl
  118.6 0.0 copy-done.2
  118.6 1.8 %shard_map.89 = f32[8,4,2,128]{3,2,1,0:T(2,128)S(1)} custom-call(f32[4,8,128]{2,1,0:T(8,128)S(1)} %get-tuple-element.30.info_ref, bf16[2,4,64,4096]{3,2,1,0:T(8,128)(2,1)S(1)} %bitcast.11, bf16[64,4096]{1,0:T(8,128)(2,1)} %collective-permute-done.4.up.fu, bf16[64,4096]{1,0:T(8,128)(2,1)} %collective-permute-done.5.low.fl, ...), custom_call_target="tpu_custom_call" | custom-call | flops 134217728 | bytes 2097152 | tf_op jit(solution)/shard_map/pallas_call | solution.py:213
  120.4 14.2 %all_to_all.25.home_ref = f32[32,2,128]{2,1,0:T(2,128)S(1)} all-to-all(f32[32,2,128]{2,1,0:T(2,128)S(1)} %bitcast.12), channel_id=1, replica_groups=mesh['dp_0'=8,'dp_1'=4,'dp_2'=2,'expert'=4] {'dp_1','dp_2','expert'}, dimensions={0} | all-to-all | bytes 65536 | tf_op jit(solution)/shard_map/all_to_all | solution.py:32
  134.6 0.4 shard_map.90
  135.0 0.0 copy-start.4
  135.0 0.7 copy-done.4
  135.7 8.1 %all-to-all-start.3 = ((bf16[32,8,512]{2,1,0:T(8,128)(2,1)}), bf16[32,8,512]{2,1,0:T(8,128)(2,1)S(1)}, u32[]{:S(2)}, u32[]{:S(2)}) async-start(bf16[32,8,512]{2,1,0:T(8,128)(2,1)} %copy-done.4), calls=%async_computation.3 | async-start | bytes 524288 | tf_op jit(solution)/shard_map/all_to_all | solution.py:32
  143.8 4.0 %shard_map.91 = bf16[2,4,64,4096]{3,2,1,0:T(8,128)(2,1)} custom-call(f32[4,8,128]{2,1,0:T(8,128)S(1)} %get-tuple-element.30.info_ref, bf16[128,4096]{1,0:T(8,128)(2,1)S(1)} %copy-done.3, bf16[64,4096]{1,0:T(8,128)(2,1)S(1)} %collective-permute-done.lu, bf16[64,4096]{1,0:T(8,128)(2,1)} %collective-permute-done.2.ll, ...), custom_call_target="tpu_custom_call" | custom-call | flops 536870912 | bytes 8388608 | tf_op jit(solution)/shard_map/pallas_call | solution.py:250
  147.8 7.2 %all-to-all-done.3 = bf16[32,8,512]{2,1,0:T(8,128)(2,1)S(1)} async-done(((bf16[32,8,512]{2,1,0:T(8,128)(2,1)}), bf16[32,8,512]{2,1,0:T(8,128)(2,1)S(1)}, u32[]{:S(2)}, u32[]{:S(2)}) %all-to-all-start.3) | async-done | bytes 262176 | tf_op jit(solution)/shard_map/all_to_all | solution.py:32
  155.1 0.7 broadcast_in_dim.3
  155.7 5.7 %all-to-all-start.4 = ((f32[8,8,512]{2,1,0:T(8,128)}), f32[8,8,512]{2,1,0:T(8,128)S(1)}, u32[]{:S(2)}, u32[]{:S(2)}) async-start(f32[8,8,512]{2,1,0:T(8,128)} %broadcast_in_dim.3), calls=%async_computation.4 | async-start | bytes 262144 | tf_op jit(solution)/shard_map/all_to_all | solution.py:32
  161.4 0.0 copy-done
  161.4 1.4 convolution_convert_fusion
  162.8 3.8 %all-to-all-done.4 = f32[8,8,512]{2,1,0:T(8,128)S(1)} async-done(((f32[8,8,512]{2,1,0:T(8,128)}), f32[8,8,512]{2,1,0:T(8,128)S(1)}, u32[]{:S(2)}, u32[]{:S(2)}) %all-to-all-start.4) | async-done | bytes 131104 | tf_op jit(solution)/shard_map/all_to_all | solution.py:32
  166.7 0.7 copy.10
  (2 shorter events, 0.1 us)
Async XLA Ops:
  0.6 160.8 %copy-start = (bf16[8,4096]{1,0:T(8,128)(2,1)S(1)}, bf16[8,4096]{1,0:T(8,128)(2,1)}, u32[]{:S(2)}) copy-start(bf16[8,4096]{1,0:T(8,128)(2,1)} %param.10) | copy-start | bytes 196612
  0.6 112.1 %copy-start.3 = (bf16[128,4096]{1,0:T(8,128)(2,1)S(1)}, bf16[128,4096]{1,0:T(8,128)(2,1)}, u32[]{:S(2)}) copy-start(bf16[128,4096]{1,0:T(8,128)(2,1)} %own.3) | copy-start | bytes 3145732
  66.5 21.8 %all-to-all-start = ((bf16[8,128,512]{2,1,0:T(8,128)(2,1)}), bf16[8,128,512]{2,1,0:T(8,128)(2,1)S(1)}, u32[]{:S(2)}, u32[]{:S(2)}) async-start(bf16[8,128,512]{2,1,0:T(8,128)(2,1)} %shard_map.86), calls=%async_computation | async-start | bytes 2097152 | tf_op jit(solution)/shard_map/all_to_all | solution.py:32
  73.3 14.8 %collective-permute-start = (bf16[64,4096]{1,0:T(8,128)(2,1)}, bf16[64,4096]{1,0:T(8,128)(2,1)S(1)}, u32[]{:S(2)}, u32[]{:S(2)}) collective-permute-start(bf16[64,4096]{1,0:T(8,128)(2,1)} %get-tuple-element.28), channel_id=1, source_target_pairs={{0,1},{1,2},{2,3},{3,0},{4,5},{5,6},{6,7},{7,4},{8,9},{9,10},{10,1... | collective-permute-start | bytes 1572872 | tf_op jit(solution)/shard_map/ppermute | solution.py:28
  73.7 14.4 %collective-permute-start.1 = (bf16[64,4096]{1,0:T(8,128)(2,1)}, bf16[64,4096]{1,0:T(8,128)(2,1)S(1)}, u32[]{:S(2)}, u32[]{:S(2)}) collective-permute-start(bf16[64,4096]{1,0:T(8,128)(2,1)} %get-tuple-element.27), channel_id=1, source_target_pairs={{0,3},{1,0},{2,1},{3,2},{4,7},{5,4},{6,5},{7,6},{8,11},{9,8},{10,9... | collective-permute-start | bytes 1572872 | tf_op jit(solution)/shard_map/ppermute | solution.py:28
  75.9 23.4 %collective-permute-start.2 = (bf16[64,4096]{1,0:T(8,128)(2,1)}, bf16[64,4096]{1,0:T(8,128)(2,1)}, u32[]{:S(2)}, u32[]{:S(2)}) collective-permute-start(bf16[64,4096]{1,0:T(8,128)(2,1)} %get-tuple-element.27), channel_id=1, source_target_pairs={{0,1},{1,2},{2,3},{3,0},{4,5},{5,6},{6,7},{7,4},{8,9},{9,10},{10,1... | collective-permute-start | bytes 1572872 | tf_op jit(solution)/shard_map/ppermute | solution.py:28
  75.9 23.4 %collective-permute-start.3 = (bf16[64,4096]{1,0:T(8,128)(2,1)}, bf16[64,4096]{1,0:T(8,128)(2,1)}, u32[]{:S(2)}, u32[]{:S(2)}) collective-permute-start(bf16[64,4096]{1,0:T(8,128)(2,1)} %get-tuple-element.28), channel_id=1, source_target_pairs={{0,3},{1,0},{2,1},{3,2},{4,7},{5,4},{6,5},{7,6},{8,11},{9,8},{10,9... | collective-permute-start | bytes 1572872 | tf_op jit(solution)/shard_map/ppermute | solution.py:28
  88.4 30.2 %collective-permute-start.4 = (bf16[64,4096]{1,0:T(8,128)(2,1)S(1)}, bf16[64,4096]{1,0:T(8,128)(2,1)}, u32[]{:S(2)}, u32[]{:S(2)}) collective-permute-start(bf16[64,4096]{1,0:T(8,128)(2,1)S(1)} %collective-permute-done.lu), channel_id=1, source_target_pairs={{0,1},{1,2},{2,3},{3,0},{4,5},{5,6},{6,7},{7,4},{8,9},{9,10},{10,1... | collective-permute-start | bytes 1572872 | tf_op jit(solution)/shard_map/ppermute | solution.py:28
  88.8 29.8 %collective-permute-start.5 = (bf16[64,4096]{1,0:T(8,128)(2,1)S(1)}, bf16[64,4096]{1,0:T(8,128)(2,1)}, u32[]{:S(2)}, u32[]{:S(2)}) collective-permute-start(bf16[64,4096]{1,0:T(8,128)(2,1)S(1)} %collective-permute-done.1.rl), channel_id=1, source_target_pairs={{0,3},{1,0},{2,1},{3,2},{4,7},{5,4},{6,5},{7,6},{8,11},{9,8},{10,9... | collective-permute-start | bytes 1572872 | tf_op jit(solution)/shard_map/ppermute | solution.py:28
  91.1 21.7 %all-to-all-start.1 = ((f32[32,8,128]{2,1,0:T(8,128)}), f32[32,8,128]{2,1,0:T(8,128)S(1)}, u32[]{:S(2)}, u32[]{:S(2)}) async-start(f32[32,8,128]{2,1,0:T(8,128)} %shard_map.87), calls=%async_computation.1 | async-start | bytes 262144 | tf_op jit(solution)/shard_map/all_to_all | solution.py:32
  112.8 2.2 %copy-start.1 = (bf16[512,4096]{1,0:T(8,128)(2,1)S(1)}, bf16[512,4096]{1,0:T(8,128)(2,1)}, u32[]{:S(2)}) copy-start(bf16[512,4096]{1,0:T(8,128)(2,1)} %param.11) | copy-start | bytes 12582916
  114.9 3.6 %copy-start.2 = (bf16[512,4096]{1,0:T(8,128)(2,1)S(1)}, bf16[512,4096]{1,0:T(8,128)(2,1)}, u32[]{:S(2)}) copy-start(bf16[512,4096]{1,0:T(8,128)(2,1)} %param.11) | copy-start | bytes 12582916
  135.0 0.7 copy-start.4
  135.7 19.3 %all-to-all-start.3 = ((bf16[32,8,512]{2,1,0:T(8,128)(2,1)}), bf16[32,8,512]{2,1,0:T(8,128)(2,1)S(1)}, u32[]{:S(2)}, u32[]{:S(2)}) async-start(bf16[32,8,512]{2,1,0:T(8,128)(2,1)} %copy-done.4), calls=%async_computation.3 | async-start | bytes 524288 | tf_op jit(solution)/shard_map/all_to_all | solution.py:32
  155.7 11.0 %all-to-all-start.4 = ((f32[8,8,512]{2,1,0:T(8,128)}), f32[8,8,512]{2,1,0:T(8,128)S(1)}, u32[]{:S(2)}, u32[]{:S(2)}) async-start(f32[8,8,512]{2,1,0:T(8,128)} %broadcast_in_dim.3), calls=%async_computation.4 | async-start | bytes 262144 | tf_op jit(solution)/shard_map/all_to_all | solution.py:32

commit v4 on v3

v4 whole, which is shorter than its diff:
```python
import functools

import jax
import jax.numpy as jnp
from jax import lax
from jax.experimental import pallas as pl
from jax.experimental.pallas import tpu as pltpu
from jax.sharding import Mesh
from jax.sharding import PartitionSpec as P

DP_EXPERT = ("dp_0", "dp_1", "dp_2", "expert")
PLANE = ("dp_1", "dp_2")
HOUSE = ("dp_1", "dp_2", "expert")
REST = ("dp_0", "expert")
BF16 = jnp.bfloat16
F32 = jnp.float32
PIECE = 512
VMEM = pl.BlockSpec(memory_space=pltpu.VMEM)
ANY = pl.BlockSpec(memory_space=pl.ANY)
PARAMS = pltpu.CompilerParams(vmem_limit_bytes=16 * 2**20)


def cost(flops, size):
    return pl.CostEstimate(flops=flops, bytes_accessed=size, transcendentals=0)


def shift(a, step):
    n = lax.axis_size("expert")
    return lax.ppermute(a, "expert", [(i, (i + step) % n) for i in range(n)])


def to_all(a, axes):
    return lax.all_to_all(a, axes, 0, 0, tiled=True)


def wide(v, rows=8):
    return jnp.broadcast_to(v, (rows, v.shape[1]))


def meta_rows(experts_ref, gates_ref):
    lines = [experts_ref[...].astype(F32), gates_ref[...].astype(F32), jnp.zeros((12, 128), F32)]
    return jnp.concatenate(lines, axis=0).astype(BF16)


def split_kernel(experts_ref, gates_ref, grad_ref, upper_ref, lower_ref, sems):
    count = grad_ref.shape[1] // PIECE
    copies = []
    for half, out_ref in enumerate((upper_ref, lower_ref)):
        for j in range(count):
            copies.append(
                pltpu.make_async_copy(
                    grad_ref.at[64 * half : 64 * half + 64, j * PIECE : (j + 1) * PIECE],
                    out_ref.at[64 * j : 64 * j + 64],
                    sems.at[count * half + j],
                )
            )
    for copy in copies:
        copy.start()
    upper_ref[64 * count : 64 * count + 16, :] = jnp.zeros((16, PIECE), BF16)
    upper_ref[64 * count : 64 * count + 16, 0:128] = meta_rows(experts_ref, gates_ref)
    for copy in copies:
        copy.wait()


def split(experts, gates, grad):
    count = grad.shape[1] // PIECE
    return pl.pallas_call(
        split_kernel,
        out_shape=[
            jax.ShapeDtypeStruct((64 * count + 16, PIECE), BF16),
            jax.ShapeDtypeStruct((64 * count, PIECE), BF16),
        ],
        in_specs=[VMEM, VMEM, ANY],
        out_specs=[VMEM, VMEM],
        scratch_shapes=[pltpu.SemaphoreType.DMA((2 * count,))],
        cost_estimate=cost(0, 4 * grad.size),
    )(experts, gates, grad)


def columns_kernel(experts_ref, gates_ref, tokens_ref, out_ref, sems):
    count, _, piece = out_ref.shape
    copies = [
        pltpu.make_async_copy(
            tokens_ref.at[:, j * piece : (j + 1) * piece], out_ref.at[j, 0:128], sems.at[j]
        )
        for j in range(count)
    ]
    for copy in copies:
        copy.start()
    meta = meta_rows(experts_ref, gates_ref)
    for j in range(count):
        out_ref[j, 128:144, :] = jnp.zeros((16, piece), BF16)
        out_ref[j, 128:144, 0:128] = meta
    for copy in copies:
        copy.wait()


def columns(experts, gates, tokens, count):
    return pl.pallas_call(
        columns_kernel,
        out_shape=jax.ShapeDtypeStruct((count, 144, tokens.shape[1] // count), tokens.dtype),
        in_specs=[VMEM, VMEM, ANY],
        out_specs=VMEM,
        scratch_shapes=[pltpu.SemaphoreType.DMA((count,))],
        cost_estimate=cost(0, 4 * tokens.size),
    )(experts, gates, tokens)


def house_index():
    return lax.axis_index("dp_1") * 2 + lax.axis_index("dp_2")


def routing(meta, me):
    meta = meta.astype(F32)
    row = lax.broadcasted_iota(jnp.int32, (8, 128), 0)
    held = (2 * me + row).astype(F32)
    earlier = lax.broadcasted_iota(jnp.int32, (128, 128), 0)
    later = lax.broadcasted_iota(jnp.int32, (128, 128), 1)
    before = jnp.where(earlier < later, 1.0, 0.0).astype(BF16)
    is0 = wide(meta[0:1]) == held
    is1 = wide(meta[1:2]) == held
    named = jnp.logical_or(is0, is1)
    count = jnp.dot(jnp.where(named, 1.0, 0.0).astype(BF16), before, preferred_element_type=F32)
    position = jnp.where(named, count, -1.0)
    gate = jnp.where(is0, wide(meta[2:3]), wide(meta[3:4]))
    return position, gate


def chosen(position, h):
    slot = lax.broadcasted_iota(jnp.int32, (64, 128), 0).astype(F32)
    return slot == wide(position[h : h + 1], 64)


def block(pieces, j):
    if len(pieces) == 1:
        return pieces[0][:, j * PIECE : (j + 1) * PIECE]
    return jnp.concatenate([p[64 * j : 64 * j + 64, :] for p in pieces], axis=0)


def products(position, saved_ref, s, pieces):
    total = jnp.zeros((128, 128), F32)
    for j in range(saved_ref.shape[3] // PIECE):
        at = slice(j * PIECE, (j + 1) * PIECE)
        stored = jnp.concatenate([saved_ref[0, s, :, at], saved_ref[1, s, :, at]], axis=0)
        total = total + lax.dot_general(
            stored, block(pieces, j), (((1,), (1,)), ((), ())), preferred_element_type=F32
        )
    lines = [
        jnp.sum(jnp.where(chosen(position, h), total[64 * h : 64 * h + 64], 0.0), axis=0, keepdims=True)
        for h in range(2)
    ]
    return jnp.concatenate(lines, axis=0)


def scale_rows(routed, pieces, s, held_ref, out_ref, sems):
    position, gate = routed
    pick = jnp.concatenate(
        [jnp.where(chosen(position, h), wide(gate[h : h + 1], 64), 0.0) for h in range(2)], axis=0
    ).astype(BF16)
    for j in range(held_ref.shape[1] // PIECE):
        held_ref[:, j * PIECE : (j + 1) * PIECE] = jnp.dot(
            pick, block(pieces, j), preferred_element_type=F32
        ).astype(BF16)
    copies = [
        pltpu.make_async_copy(held_ref.at[64 * h : 64 * h + 64], out_ref.at[h, s], sems.at[h])
        for h in range(2)
    ]
    for copy in copies:
        copy.start()
    return copies


def near_kernel(experts_ref, gates_ref, saved_ref, own, lu, ll, ru, rl, out_ref, grad_ref, held_ref, sems):
    me = lax.axis_index("expert")
    groups = saved_ref.shape[1]
    own_meta = meta_rows(experts_ref, gates_ref)
    end = ll.shape[0]
    sources = (
        (0, own_meta, (own,)),
        (1, ru[end : end + 16, 0:128], (ru, rl)),
        (3, lu[end : end + 16, 0:128], (lu, ll)),
    )
    routed = [routing(meta, me) for _, meta, _ in sources]
    out_ref[2] = jnp.zeros((2, 128), F32)
    for j, (d, _, pieces) in enumerate(sources):
        out_ref[d] = products(routed[j][0], saved_ref, lax.rem(me + d, groups), pieces)
    copies = []
    for j, (d, _, pieces) in enumerate(sources):
        copies += scale_rows(
            routed[j], pieces, lax.rem(me + d, groups), held_ref.at[j], grad_ref, sems.at[j]
        )
    for copy in copies:
        copy.wait()


def near_sources(experts, gates, saved, pieces):
    groups, width = saved.shape[1], saved.shape[3]
    return pl.pallas_call(
        near_kernel,
        out_shape=[
            jax.ShapeDtypeStruct((groups, 2, 128), F32),
            jax.ShapeDtypeStruct(saved.shape, BF16),
        ],
        in_specs=[VMEM] * 8,
        out_specs=[VMEM, ANY],
        scratch_shapes=[pltpu.VMEM((3, 128, width), BF16), pltpu.SemaphoreType.DMA((3, 2))],
        compiler_params=PARAMS,
        cost_estimate=cost(12 * 128 * 128 * width, 18 * 128 * width),
    )(experts, gates, saved, *pieces)


def far_kernel(saved_ref, up, low, near_ref, out_ref):
    me = lax.axis_index("expert")
    groups = saved_ref.shape[1]
    s = lax.rem(me + 2, groups)
    end = low.shape[0]
    position, _ = routing(up[end : end + 16, 0:128], me)
    lines = {2: products(position, saved_ref, s, (up, low))}
    for d in (0, 1, 3):
        lines[d] = near_ref[d]
    for d in range(groups):
        t = lax.rem(me + d, groups)
        for j in range(out_ref.shape[0]):
            out_ref[j, t] = lines[d]


def far_products(saved, pieces, near, copies):
    groups, width = saved.shape[1], saved.shape[3]
    return pl.pallas_call(
        far_kernel,
        out_shape=jax.ShapeDtypeStruct((copies, groups, 2, 128), F32),
        in_specs=[VMEM] * 4,
        out_specs=VMEM,
        compiler_params=PARAMS,
        cost_estimate=cost(2 * 128 * 128 * width, 4 * 128 * width),
    )(saved, *pieces, near)


def far_rows_kernel(up, low, _, grad_ref, held_ref, sems):
    me = lax.axis_index("expert")
    groups = grad_ref.shape[1]
    end = low.shape[0]
    routed = routing(up[end : end + 16, 0:128], me)
    for copy in scale_rows(routed, (up, low), lax.rem(me + 2, groups), held_ref, grad_ref, sems):
        copy.wait()


def far_rows(pieces, grad):
    width = grad.shape[3]
    return pl.pallas_call(
        far_rows_kernel,
        out_shape=jax.ShapeDtypeStruct(grad.shape, BF16),
        in_specs=[VMEM, VMEM, ANY],
        out_specs=ANY,
        scratch_shapes=[pltpu.VMEM((128, width), BF16), pltpu.SemaphoreType.DMA((2,))],
        input_output_aliases={2: 0},
        compiler_params=PARAMS,
        cost_estimate=cost(2 * 128 * 128 * width, 4 * 128 * width),
    )(*pieces, grad)


def logit_kernel(home_ref, tokens_ref, logit_ref, out_ref):
    house = house_index()
    blocks = tokens_ref.shape[0]
    groups = home_ref.shape[0] // blocks
    row = lax.broadcasted_iota(jnp.int32, (8, 128), 0).astype(F32)
    found = []
    for b in range(blocks):
        meta = tokens_ref[b, 128:144, 0:128].astype(F32)
        e0, e1, g0, g1 = meta[0:1], meta[1:2], meta[2:3], meta[3:4]
        grads = jnp.concatenate([home_ref[b * groups + y] for y in range(groups)], axis=0)
        is0, is1 = wide(e0) == row, wide(e1) == row
        gg0 = jnp.sum(jnp.where(is0, grads, 0.0), axis=0, keepdims=True)
        gg1 = jnp.sum(jnp.where(is1, grads, 0.0), axis=0, keepdims=True)
        blended = g0 * gg0 + g1 * gg1
        s0 = g0 * (gg0 - blended)
        s1 = g1 * (gg1 - blended)
        logit = jnp.where(is0, wide(s0), 0.0) + jnp.where(is1, wide(s1), 0.0)
        found.append(logit.astype(BF16))

        @pl.when(house == b)
        def _():
            logit_ref[...] = logit.astype(BF16)

    every = jnp.concatenate(found, axis=1)
    features = jnp.concatenate([tokens_ref[b, 0:128] for b in range(blocks)], axis=0)
    part = jnp.dot(every, features, preferred_element_type=F32).astype(BF16)
    for j in range(out_ref.shape[0]):
        out_ref[j] = part


def logits(home, tokens, copies):
    piece = tokens.shape[2]
    return pl.pallas_call(
        logit_kernel,
        out_shape=[
            jax.ShapeDtypeStruct((8, 128), BF16),
            jax.ShapeDtypeStruct((copies, 8, piece), BF16),
        ],
        in_specs=[VMEM, VMEM],
        out_specs=[VMEM, VMEM],
        compiler_params=PARAMS,
        cost_estimate=cost(16 * tokens.size, 4 * tokens.size),
    )(home, tokens)


def local(tokens, grad_out, experts, gates, router_weight, saved_outputs):
    width = tokens.shape[1]
    groups = lax.axis_size("expert")
    houses = lax.axis_size(PLANE)
    saved = saved_outputs.reshape(2, groups, 64, width)

    experts, gates = experts.T, gates.T

    upper, lower = split(experts, gates, grad_out)
    left_upper = shift(upper, 1)
    right_lower = shift(lower, -1)
    tokens, upper, lower = lax.optimization_barrier((tokens, upper, lower))
    own_columns = columns(experts, gates, tokens, houses)
    own_columns, upper, lower = lax.optimization_barrier((own_columns, upper, lower))
    left_lower = shift(lower, 1)
    right_upper = shift(upper, -1)
    turned = to_all(own_columns, PLANE)
    far_upper = shift(left_upper, 1)
    far_lower = shift(right_lower, -1)
    near, expert_grad = near_sources(
        experts, gates, saved, (grad_out, left_upper, left_lower, right_upper, right_lower)
    )
    sent = far_products(saved, (far_upper, far_lower), near, houses)
    sent, turned = lax.optimization_barrier((sent, turned))
    home = to_all(sent.reshape(houses * groups, 2, 128), HOUSE)
    expert_grad = far_rows((far_upper, far_lower), expert_grad)

    logit, parts = logits(home, turned, lax.axis_size(REST))
    scale = float(lax.axis_size(DP_EXPERT) * tokens.shape[0]) ** (-0.5)
    total = to_all(parts, REST).astype(F32).sum(axis=0) * scale
    whole = to_all(jnp.broadcast_to(total, (houses, *total.shape)), PLANE)
    router_grad = whole.swapaxes(0, 1).reshape(8, width)
    input_grad = lax.dot_general(
        logit, router_weight, (((0,), (0,)), ((), ())), preferred_element_type=F32
    ).astype(BF16)
    return input_grad, router_grad, expert_grad.reshape(saved_outputs.shape)


def solution(mesh):
    finer = Mesh(
        mesh.devices.reshape(8, 4, 2, mesh.shape["expert"]), ("dp_0", "dp_1", "dp_2", "expert")
    )
    rows = P(DP_EXPERT, None)
    return jax.shard_map(
        local,
        mesh=finer,
        in_specs=(rows, rows, rows, rows, P(), rows),
        out_specs=(rows, P(), rows),
        check_vma=False,
    )
```

time: 168 us -> 91.9 us (0.55)
  Pallas kernels: 77 us -> 13.7 us
  starting transfers between devices: 36.6 us -> 28.8 us
  waiting for transfers between devices: 33 us -> 29.7 us
    pallas_call x5 -> x4, Pallas kernels: 74.9 us -> 12.1 us  [the longest x1 4.36 us: near_sources(): pl.pallas_call(near_kernel, out_shape=[jax.ShapeDtypeStruct((groups, 2, 1...]
    all_to_all x4 -> x3, waiting for transfers between devices: 24.8 us -> 13.6 us  [to_all(): return lax.all_to_all(a, axes, 0, 0, tiled=True)]
    ppermute x6, waiting for transfers between devices: 8.27 us -> 16.1 us  [shift(): return lax.ppermute(a, 'expert', [(i, (i + step) % n) for i in range(n)])]
    all_to_all x4 -> x3, starting transfers between devices: 28.6 us -> 20.9 us  [to_all(): return lax.all_to_all(a, axes, 0, 0, tiled=True)]
    unnamed x11 -> x13, local copies, waits for them, and re-layouts: 3.56 us -> 2.87 us
  transfers between devices with their start and end apart: 10 -> 9, of which waited for: 6 -> 5; matrix products, arithmetic and copies ran while one was open for 1% -> 2% of each run, Pallas kernels for 5% -> 10%
where the time goes in v4:
time: 91.9 us; the launch traced here: 91.4 us
  waiting for transfers between devices  29.7 us (32%)
  starting transfers between devices  28.8 us (31%)
  Pallas kernels  13.7 us (15%)
  blocking collectives  13.5 us (15%)
  local copies, waits for them, and re-layouts  3.53 us (4%)
  matrix products  1.44 us (2%)
    all_to_all x3, starting transfers between devices, to_all(): return lax.all_to_all(a, axes, 0, 0, tiled=True)  20.9 us
    ppermute x6, waiting for transfers between devices, shift(): return lax.ppermute(a, 'expert', [(i, (i + step) % n) for i in range(n)])  16.1 us
    all_to_all x3, waiting for transfers between devices, to_all(): return lax.all_to_all(a, axes, 0, 0, tiled=True)  13.6 us
    all_to_all x1, blocking collectives, to_all(): return lax.all_to_all(a, axes, 0, 0, tiled=True)  13.5 us
    ppermute x6, starting transfers between devices, shift(): return lax.ppermute(a, 'expert', [(i, (i + step) % n) for i in range(n)])  7.88 us
    pallas_call x1, Pallas kernels, near_sources(): pl.pallas_call(near_kernel, out_shape=[jax.ShapeDtypeStruct((groups, 2, 1...  4.36 us
    pallas_call x1, Pallas kernels, split(): pl.pallas_call(split_kernel, out_shape=[jax.ShapeDtypeStruct((64 * count...  3.12 us
    pallas_call x1, Pallas kernels, columns(): pl.pallas_call(columns_kernel, out_shape=jax.ShapeDtypeStruct((count, 144...  3.09 us
  transfers between devices with their start and end apart: 9, of which 5 were waited for; matrix products, arithmetic and copies ran while one was open for 2% of the time, Pallas kernels for 10%

profile of v4, /device:TPU:1, one launch (start us, length us, event | category | flops | bytes accessed | tf_op | source)
XLA Modules:
  0.0 91.4 jit_solution(12621825034491937645)
XLA Ops:
  0.6 0.0 copy-start
  0.6 0.0 copy-start.4
  0.7 0.0 copy-start.5
  0.7 0.0 copy-start.3
  0.7 3.1 %shard_map.85 = (bf16[528,512]{1,0:T(8,128)(2,1)}, bf16[512,512]{1,0:T(8,128)(2,1)}) custom-call(s32[2,128]{1,0:T(2,128)} %bitcast.13, bf16[2,128]{1,0:T(2,128)(2,1)} %bitcast.16, bf16[128,4096]{1,0:T(8,128)(2,1)} %own.1), custom_call_target="tpu_custom_call" | custom-call | bytes 2097152 | tf_op jit(solution)/shard_map/pallas_call | solution.py:67
  3.8 2.2 %collective-permute-start = (bf16[528,512]{1,0:T(8,128)(2,1)}, bf16[528,512]{1,0:T(8,128)(2,1)}, u32[]{:S(2)}, u32[]{:S(2)}) collective-permute-start(bf16[528,512]{1,0:T(8,128)(2,1)} %get-tuple-element.23), channel_id=1, source_target_pairs={{0,1},{1,2},{2,3},{3,0},{4,5},{5,6},{6,7},{7,4},{8,9},{9,10},{10,1... | collective-permute-start | bytes 1622024 | tf_op jit(solution)/shard_map/ppermute | solution.py:29
  6.0 1.5 %collective-permute-start.2 = (bf16[512,512]{1,0:T(8,128)(2,1)}, bf16[512,512]{1,0:T(8,128)(2,1)}, u32[]{:S(2)}, u32[]{:S(2)}) collective-permute-start(bf16[512,512]{1,0:T(8,128)(2,1)} %get-tuple-element.22), channel_id=1, source_target_pairs={{0,3},{1,0},{2,1},{3,2},{4,7},{5,4},{6,5},{7,6},{8,11},{9,8},{10,9... | collective-permute-start | bytes 1572872 | tf_op jit(solution)/shard_map/ppermute | solution.py:29
  7.5 3.1 %shard_map.86 = bf16[8,144,512]{2,1,0:T(8,128)(2,1)} custom-call(s32[2,128]{1,0:T(2,128)} %bitcast.14, bf16[2,128]{1,0:T(2,128)(2,1)} %bitcast.17, bf16[128,4096]{1,0:T(8,128)(2,1)} %tokens_ref), custom_call_target="tpu_custom_call" | custom-call | bytes 2097152 | tf_op jit(solution)/shard_map/pallas_call | solution.py:99
  10.6 6.3 %all-to-all-start = ((bf16[8,144,512]{2,1,0:T(8,128)(2,1)}), bf16[8,144,512]{2,1,0:T(8,128)(2,1)S(1)}, u32[]{:S(2)}, u32[]{:S(2)}) async-start(bf16[8,144,512]{2,1,0:T(8,128)(2,1)} %shard_map.86), calls=%async_computation | async-start | bytes 2359296 | tf_op jit(solution)/shard_map/all_to_all | solution.py:33
  16.9 0.6 collective-permute-start.5
  17.6 0.8 collective-permute-start.4
  18.4 0.0 collective-permute-done.lu
  18.4 0.9 collective-permute-start.1
  19.3 0.0 collective-permute-done.2.rl
  19.3 1.8 %collective-permute-start.3 = (bf16[512,512]{1,0:T(8,128)(2,1)}, bf16[512,512]{1,0:T(8,128)(2,1)S(1)}, u32[]{:S(2)}, u32[]{:S(2)}) collective-permute-start(bf16[512,512]{1,0:T(8,128)(2,1)} %collective-permute-done.2.rl), channel_id=1, source_target_pairs={{0,3},{1,0},{2,1},{3,2},{4,7},{5,4},{6,5},{7,6},{8,11},{9,8},{10,9... | collective-permute-start | bytes 1572872 | tf_op jit(solution)/shard_map/ppermute | solution.py:29
  21.1 11.1 %collective-permute-done.4.ll = bf16[512,512]{1,0:T(8,128)(2,1)S(1)} collective-permute-done((bf16[512,512]{1,0:T(8,128)(2,1)}, bf16[512,512]{1,0:T(8,128)(2,1)S(1)}, u32[]{:S(2)}, u32[]{:S(2)}) %collective-permute-start.4) | collective-permute-done | bytes 524320 | tf_op jit(solution)/shard_map/ppermute | solution.py:29
  32.2 0.0 collective-permute-done.5.ru
  32.2 0.0 copy-done.4
  32.2 0.0 copy-done.5
  32.2 0.0 copy-done.3
  32.2 0.0 copy-start.1
  32.3 2.2 %copy-done.1 = bf16[512,4096]{1,0:T(8,128)(2,1)S(1)} copy-done((bf16[512,4096]{1,0:T(8,128)(2,1)S(1)}, bf16[512,4096]{1,0:T(8,128)(2,1)}, u32[]{:S(2)}) %copy-start.1) | copy-done | bytes 4194328
  34.4 0.0 copy-start.2
  34.4 4.4 %shard_map.87 = (f32[4,2,128]{2,1,0:T(2,128)S(1)}, bf16[2,4,64,4096]{3,2,1,0:T(8,128)(2,1)}) custom-call(s32[2,128]{1,0:T(2,128)S(1)} %bitcast.15, bf16[2,128]{1,0:T(2,128)(2,1)S(1)} %bitcast.18, bf16[2,4,64,4096]{3,2,1,0:T(8,128)(2,1)S(1)} %bitcast.10, bf16[128,4096]{1,0:T(8,128)(2,1)S(1)} %copy-done.3, bf16[528,512]{1,0:T(8,128)(2,1)} %collective-permute-done.lu, ...), custom_call_target="tpu_custom_call" | custom-call | flops 805306368 | bytes 9437184 | tf_op jit(solution)/shard_map/pallas_call | solution.py:198
  38.8 3.9 %collective-permute-done.3.low = bf16[512,512]{1,0:T(8,128)(2,1)S(1)} collective-permute-done((bf16[512,512]{1,0:T(8,128)(2,1)}, bf16[512,512]{1,0:T(8,128)(2,1)S(1)}, u32[]{:S(2)}, u32[]{:S(2)}) %collective-permute-start.3) | collective-permute-done | bytes 524320 | tf_op jit(solution)/shard_map/ppermute | solution.py:29
  42.7 1.2 %collective-permute-done.1.up = bf16[528,512]{1,0:T(8,128)(2,1)S(1)} collective-permute-done((bf16[528,512]{1,0:T(8,128)(2,1)}, bf16[528,512]{1,0:T(8,128)(2,1)S(1)}, u32[]{:S(2)}, u32[]{:S(2)}) %collective-permute-start.1) | collective-permute-done | bytes 540704 | tf_op jit(solution)/shard_map/ppermute | solution.py:29
  43.8 0.0 copy-done.2
  43.8 0.4 shard_map.88
  44.3 0.0 all-to-all-done.tokens_ref
  44.3 13.5 %all_to_all.20.home_ref = f32[32,2,128]{2,1,0:T(2,128)S(1)} all-to-all(f32[32,2,128]{2,1,0:T(2,128)S(1)} %bitcast.12), channel_id=1, replica_groups=mesh['dp_0'=8,'dp_1'=4,'dp_2'=2,'expert'=4] {'dp_1','dp_2','expert'}, dimensions={0} | all-to-all | bytes 65536 | tf_op jit(solution)/shard_map/all_to_all | solution.py:33
  57.8 1.1 %shard_map.89 = (bf16[8,128]{1,0:T(8,128)(2,1)S(1)}, bf16[32,8,512]{2,1,0:T(8,128)(2,1)}) custom-call(f32[32,2,128]{2,1,0:T(2,128)S(1)} %all_to_all.20.home_ref, bf16[8,144,512]{2,1,0:T(8,128)(2,1)S(1)} %all-to-all-done.tokens_ref), custom_call_target="tpu_custom_call" | custom-call | flops 9437184 | bytes 2359296 | tf_op jit(solution)/shard_map/pallas_call | solution.py:294
  58.9 8.9 %all-to-all-start.2 = ((bf16[32,8,512]{2,1,0:T(8,128)(2,1)}), bf16[32,8,512]{2,1,0:T(8,128)(2,1)S(1)}, u32[]{:S(2)}, u32[]{:S(2)}) async-start(bf16[32,8,512]{2,1,0:T(8,128)(2,1)} %get-tuple-element.29), calls=%async_computation.2 | async-start | bytes 524288 | tf_op jit(solution)/shard_map/all_to_all | solution.py:33
  67.8 1.5 %shard_map.90 = bf16[2,4,64,4096]{3,2,1,0:T(8,128)(2,1)} custom-call(bf16[528,512]{1,0:T(8,128)(2,1)S(1)} %collective-permute-done.1.up, bf16[512,512]{1,0:T(8,128)(2,1)S(1)} %collective-permute-done.3.low, bf16[2,4,64,4096]{3,2,1,0:T(8,128)(2,1)} %get-tuple-element.30._), custom_call_target="tpu_custom_call", output_to_operand_aliasing={{}: (2, {})} | custom-call | flops 134217728 | bytes 2097152 | tf_op jit(solution)/shard_map/pallas_call | solution.py:250
  69.4 9.7 %all-to-all-done.2 = bf16[32,8,512]{2,1,0:T(8,128)(2,1)S(1)} async-done(((bf16[32,8,512]{2,1,0:T(8,128)(2,1)}), bf16[32,8,512]{2,1,0:T(8,128)(2,1)S(1)}, u32[]{:S(2)}, u32[]{:S(2)}) %all-to-all-start.2) | async-done | bytes 262176 | tf_op jit(solution)/shard_map/all_to_all | solution.py:33
  79.1 0.7 broadcast_in_dim.3
  79.8 5.7 %all-to-all-start.3 = ((f32[8,8,512]{2,1,0:T(8,128)}), f32[8,8,512]{2,1,0:T(8,128)S(1)}, u32[]{:S(2)}, u32[]{:S(2)}) async-start(f32[8,8,512]{2,1,0:T(8,128)} %broadcast_in_dim.3), calls=%async_computation.3 | async-start | bytes 262144 | tf_op jit(solution)/shard_map/all_to_all | solution.py:33
  85.5 0.0 copy-done
  85.5 1.4 %convolution_convert_fusion = bf16[128,4096]{1,0:T(8,128)(2,1)} fusion(bf16[8,128]{1,0:T(8,128)(2,1)S(1)} %get-tuple-element.28, bf16[8,4096]{1,0:T(8,128)(2,1)S(1)} %copy-done), kind=kOutput, calls=%fused_computation | convolution fusion | flops 8912896 | bytes 1116160 | tf_op jit(solution)/shard_map/dot_general | solution.py:339
  86.9 3.9 %all-to-all-done.3 = f32[8,8,512]{2,1,0:T(8,128)S(1)} async-done(((f32[8,8,512]{2,1,0:T(8,128)}), f32[8,8,512]{2,1,0:T(8,128)S(1)}, u32[]{:S(2)}, u32[]{:S(2)}) %all-to-all-start.3) | async-done | bytes 131104 | tf_op jit(solution)/shard_map/all_to_all | solution.py:33
  90.8 0.7 copy.12
  (2 shorter events, 0.1 us)
Async XLA Ops:
  0.6 84.8 %copy-start = (bf16[8,4096]{1,0:T(8,128)(2,1)S(1)}, bf16[8,4096]{1,0:T(8,128)(2,1)}, u32[]{:S(2)}) copy-start(bf16[8,4096]{1,0:T(8,128)(2,1)} %param.10) | copy-start | bytes 196612
  0.6 31.6 %copy-start.4 = (s32[128,2]{0,1:T(2,128)S(1)}, s32[128,2]{0,1:T(2,128)}, u32[]{:S(2)}) copy-start(s32[128,2]{0,1:T(2,128)} %param.8) | copy-start | bytes 3076
  0.7 31.6 %copy-start.5 = (bf16[128,2]{0,1:T(2,128)(2,1)S(1)}, bf16[128,2]{0,1:T(2,128)(2,1)}, u32[]{:S(2)}) copy-start(bf16[128,2]{0,1:T(2,128)(2,1)} %param.9) | copy-start | bytes 1540
  0.7 31.6 %copy-start.3 = (bf16[128,4096]{1,0:T(8,128)(2,1)S(1)}, bf16[128,4096]{1,0:T(8,128)(2,1)}, u32[]{:S(2)}) copy-start(bf16[128,4096]{1,0:T(8,128)(2,1)} %own.1) | copy-start | bytes 3145732
  3.8 14.6 %collective-permute-start = (bf16[528,512]{1,0:T(8,128)(2,1)}, bf16[528,512]{1,0:T(8,128)(2,1)}, u32[]{:S(2)}, u32[]{:S(2)}) collective-permute-start(bf16[528,512]{1,0:T(8,128)(2,1)} %get-tuple-element.23), channel_id=1, source_target_pairs={{0,1},{1,2},{2,3},{3,0},{4,5},{5,6},{6,7},{7,4},{8,9},{9,10},{10,1... | collective-permute-start | bytes 1622024 | tf_op jit(solution)/shard_map/ppermute | solution.py:29
  6.0 13.3 %collective-permute-start.2 = (bf16[512,512]{1,0:T(8,128)(2,1)}, bf16[512,512]{1,0:T(8,128)(2,1)}, u32[]{:S(2)}, u32[]{:S(2)}) collective-permute-start(bf16[512,512]{1,0:T(8,128)(2,1)} %get-tuple-element.22), channel_id=1, source_target_pairs={{0,3},{1,0},{2,1},{3,2},{4,7},{5,4},{6,5},{7,6},{8,11},{9,8},{10,9... | collective-permute-start | bytes 1572872 | tf_op jit(solution)/shard_map/ppermute | solution.py:29
  10.6 33.6 %all-to-all-start = ((bf16[8,144,512]{2,1,0:T(8,128)(2,1)}), bf16[8,144,512]{2,1,0:T(8,128)(2,1)S(1)}, u32[]{:S(2)}, u32[]{:S(2)}) async-start(bf16[8,144,512]{2,1,0:T(8,128)(2,1)} %shard_map.86), calls=%async_computation | async-start | bytes 2359296 | tf_op jit(solution)/shard_map/all_to_all | solution.py:33
  16.9 15.3 %collective-permute-start.5 = (bf16[528,512]{1,0:T(8,128)(2,1)}, bf16[528,512]{1,0:T(8,128)(2,1)S(1)}, u32[]{:S(2)}, u32[]{:S(2)}) collective-permute-start(bf16[528,512]{1,0:T(8,128)(2,1)} %get-tuple-element.23), channel_id=1, source_target_pairs={{0,3},{1,0},{2,1},{3,2},{4,7},{5,4},{6,5},{7,6},{8,11},{9,8},{10,9... | collective-permute-start | bytes 1622024 | tf_op jit(solution)/shard_map/ppermute | solution.py:29
  17.6 14.7 %collective-permute-start.4 = (bf16[512,512]{1,0:T(8,128)(2,1)}, bf16[512,512]{1,0:T(8,128)(2,1)S(1)}, u32[]{:S(2)}, u32[]{:S(2)}) collective-permute-start(bf16[512,512]{1,0:T(8,128)(2,1)} %get-tuple-element.22), channel_id=1, source_target_pairs={{0,1},{1,2},{2,3},{3,0},{4,5},{5,6},{6,7},{7,4},{8,9},{9,10},{10,1... | collective-permute-start | bytes 1572872 | tf_op jit(solution)/shard_map/ppermute | solution.py:29
  18.4 25.4 %collective-permute-start.1 = (bf16[528,512]{1,0:T(8,128)(2,1)}, bf16[528,512]{1,0:T(8,128)(2,1)S(1)}, u32[]{:S(2)}, u32[]{:S(2)}) collective-permute-start(bf16[528,512]{1,0:T(8,128)(2,1)} %collective-permute-done.lu), channel_id=1, source_target_pairs={{0,1},{1,2},{2,3},{3,0},{4,5},{5,6},{6,7},{7,4},{8,9},{9,10},{10,1... | collective-permute-start | bytes 1622024 | tf_op jit(solution)/shard_map/ppermute | solution.py:29
  19.3 23.4 %collective-permute-start.3 = (bf16[512,512]{1,0:T(8,128)(2,1)}, bf16[512,512]{1,0:T(8,128)(2,1)S(1)}, u32[]{:S(2)}, u32[]{:S(2)}) collective-permute-start(bf16[512,512]{1,0:T(8,128)(2,1)} %collective-permute-done.2.rl), channel_id=1, source_target_pairs={{0,3},{1,0},{2,1},{3,2},{4,7},{5,4},{6,5},{7,6},{8,11},{9,8},{10,9... | collective-permute-start | bytes 1572872 | tf_op jit(solution)/shard_map/ppermute | solution.py:29
  32.2 2.2 %copy-start.1 = (bf16[512,4096]{1,0:T(8,128)(2,1)S(1)}, bf16[512,4096]{1,0:T(8,128)(2,1)}, u32[]{:S(2)}) copy-start(bf16[512,4096]{1,0:T(8,128)(2,1)} %param.11) | copy-start | bytes 12582916
  34.4 9.4 %copy-start.2 = (bf16[512,4096]{1,0:T(8,128)(2,1)S(1)}, bf16[512,4096]{1,0:T(8,128)(2,1)}, u32[]{:S(2)}) copy-start(bf16[512,4096]{1,0:T(8,128)(2,1)} %param.11) | copy-start | bytes 12582916
  58.9 20.2 %all-to-all-start.2 = ((bf16[32,8,512]{2,1,0:T(8,128)(2,1)}), bf16[32,8,512]{2,1,0:T(8,128)(2,1)S(1)}, u32[]{:S(2)}, u32[]{:S(2)}) async-start(bf16[32,8,512]{2,1,0:T(8,128)(2,1)} %get-tuple-element.29), calls=%async_computation.2 | async-start | bytes 524288 | tf_op jit(solution)/shard_map/all_to_all | solution.py:33
  79.8 11.0 %all-to-all-start.3 = ((f32[8,8,512]{2,1,0:T(8,128)}), f32[8,8,512]{2,1,0:T(8,128)S(1)}, u32[]{:S(2)}, u32[]{:S(2)}) async-start(f32[8,8,512]{2,1,0:T(8,128)} %broadcast_in_dim.3), calls=%async_computation.3 | async-start | bytes 262144 | tf_op jit(solution)/shard_map/all_to_all | solution.py:33

commit v5 on v4

--- a/solution.py
+++ b/solution.py
@@ -11,7 +11,7 @@
 DP_EXPERT = ("dp_0", "dp_1", "dp_2", "expert")
 PLANE = ("dp_1", "dp_2")
 HOUSE = ("dp_1", "dp_2", "expert")
-REST = ("dp_0", "expert")
+REST = ("expert", "dp_0")
 BF16 = jnp.bfloat16
 F32 = jnp.float32
 PIECE = 512
@@ -42,23 +42,28 @@
     return jnp.concatenate(lines, axis=0).astype(BF16)
 
 
-def split_kernel(experts_ref, gates_ref, grad_ref, upper_ref, lower_ref, sems):
+def split_kernel(experts_ref, gates_ref, grad_ref, upper_ref, lower_ref, rows_ref, up_ref, low_ref, sems):
     count = grad_ref.shape[1] // PIECE
-    copies = []
-    for half, out_ref in enumerate((upper_ref, lower_ref)):
+    arriving = [
+        pltpu.make_async_copy(grad_ref.at[64 * h : 64 * h + 64], rows_ref.at[h], sems.at[0, h])
+        for h in range(2)
+    ]
+    for copy in arriving:
+        copy.start()
+    halves = (up_ref, low_ref)
+    end = up_ref.shape[0] - 16
+    up_ref[end:, :] = jnp.zeros((16, PIECE), BF16)
+    up_ref[end:, 0:128] = meta_rows(experts_ref, gates_ref)
+    leaving = [
+        pltpu.make_async_copy(up_ref, upper_ref, sems.at[1, 0]),
+        pltpu.make_async_copy(low_ref, lower_ref, sems.at[1, 1]),
+    ]
+    for half in range(2):
+        arriving[half].wait()
         for j in range(count):
-            copies.append(
-                pltpu.make_async_copy(
-                    grad_ref.at[64 * half : 64 * half + 64, j * PIECE : (j + 1) * PIECE],
-                    out_ref.at[64 * j : 64 * j + 64],
-                    sems.at[count * half + j],
-                )
-            )
-    for copy in copies:
-        copy.start()
-    upper_ref[64 * count : 64 * count + 16, :] = jnp.zeros((16, PIECE), BF16)
-    upper_ref[64 * count : 64 * count + 16, 0:128] = meta_rows(experts_ref, gates_ref)
-    for copy in copies:
+            halves[half][64 * j : 64 * j + 64, :] = rows_ref[half, :, j * PIECE : (j + 1) * PIECE]
+        leaving[half].start()
+    for copy in leaving:
         copy.wait()
 
 
@@ -71,37 +76,50 @@
             jax.ShapeDtypeStruct((64 * count, PIECE), BF16),
         ],
         in_specs=[VMEM, VMEM, ANY],
-        out_specs=[VMEM, VMEM],
-        scratch_shapes=[pltpu.SemaphoreType.DMA((2 * count,))],
+        out_specs=[ANY, ANY],
+        scratch_shapes=[
+            pltpu.VMEM((2, 64, grad.shape[1]), BF16),
+            pltpu.VMEM((64 * count + 16, PIECE), BF16),
+            pltpu.VMEM((64 * count, PIECE), BF16),
+            pltpu.SemaphoreType.DMA((2, 2)),
+        ],
         cost_estimate=cost(0, 4 * grad.size),
     )(experts, gates, grad)
 
 
-def columns_kernel(experts_ref, gates_ref, tokens_ref, out_ref, sems):
+def columns_kernel(experts_ref, gates_ref, tokens_ref, out_ref, rows_ref, held_ref, sems):
     count, _, piece = out_ref.shape
-    copies = [
-        pltpu.make_async_copy(
-            tokens_ref.at[:, j * piece : (j + 1) * piece], out_ref.at[j, 0:128], sems.at[j]
-        )
-        for j in range(count)
-    ]
-    for copy in copies:
+    arriving = [
+        pltpu.make_async_copy(tokens_ref.at[64 * h : 64 * h + 64], rows_ref.at[h], sems.at[0, h])
+        for h in range(2)
+    ]
+    for copy in arriving:
         copy.start()
     meta = meta_rows(experts_ref, gates_ref)
     for j in range(count):
-        out_ref[j, 128:144, :] = jnp.zeros((16, piece), BF16)
-        out_ref[j, 128:144, 0:128] = meta
-    for copy in copies:
-        copy.wait()
+        held_ref[j, 128:144, :] = jnp.zeros((16, piece), BF16)
+        held_ref[j, 128:144, 0:128] = meta
+    for half in range(2):
+        arriving[half].wait()
+        for j in range(count):
+            held_ref[j, 64 * half : 64 * half + 64] = rows_ref[half, :, j * piece : (j + 1) * piece]
+    last = pltpu.make_async_copy(held_ref, out_ref, sems.at[1, 0])
+    last.start()
+    last.wait()
 
 
 def columns(experts, gates, tokens, count):
+    piece = tokens.shape[1] // count
     return pl.pallas_call(
         columns_kernel,
-        out_shape=jax.ShapeDtypeStruct((count, 144, tokens.shape[1] // count), tokens.dtype),
+        out_shape=jax.ShapeDtypeStruct((count, 144, piece), tokens.dtype),
         in_specs=[VMEM, VMEM, ANY],
-        out_specs=VMEM,
-        scratch_shapes=[pltpu.SemaphoreType.DMA((count,))],
+        out_specs=ANY,
+        scratch_shapes=[
+            pltpu.VMEM((2, 64, tokens.shape[1]), BF16),
+            pltpu.VMEM((count, 144, piece), BF16),
+            pltpu.SemaphoreType.DMA((2, 2)),
+        ],
         cost_estimate=cost(0, 4 * tokens.size),
     )(experts, gates, tokens)
 
@@ -317,7 +335,6 @@
     right_lower = shift(lower, -1)
     tokens, upper, lower = lax.optimization_barrier((tokens, upper, lower))
     own_columns = columns(experts, gates, tokens, houses)
-    own_columns, upper, lower = lax.optimization_barrier((own_columns, upper, lower))
     left_lower = shift(lower, 1)
     right_upper = shift(upper, -1)
     turned = to_all(own_columns, PLANE)
@@ -331,14 +348,16 @@
     home = to_all(sent.reshape(houses * groups, 2, 128), HOUSE)
     expert_grad = far_rows((far_upper, far_lower), expert_grad)
 
+    home, expert_grad = lax.optimization_barrier((home, expert_grad))
     logit, parts = logits(home, turned, lax.axis_size(REST))
-    scale = float(lax.axis_size(DP_EXPERT) * tokens.shape[0]) ** (-0.5)
-    total = to_all(parts, REST).astype(F32).sum(axis=0) * scale
-    whole = to_all(jnp.broadcast_to(total, (houses, *total.shape)), PLANE)
-    router_grad = whole.swapaxes(0, 1).reshape(8, width)
     input_grad = lax.dot_general(
         logit, router_weight, (((0,), (0,)), ((), ())), preferred_element_type=F32
     ).astype(BF16)
+    scale = float(lax.axis_size(DP_EXPERT) * tokens.shape[0]) ** (-0.5)
+    total = to_all(parts, REST).astype(F32).sum(axis=0) * scale
+    total, input_grad = lax.optimization_barrier((total, input_grad))
+    whole = to_all(jnp.broadcast_to(total.astype(BF16), (houses, *total.shape)), PLANE).astype(F32)
+    router_grad = whole.swapaxes(0, 1).reshape(8, width)
     return input_grad, router_grad, expert_grad.reshape(saved_outputs.shape)
 
 

time: 91.9 us -> 90.1 us (0.980)
  blocking collectives: 13.5 us -> 10.9 us
  local copies, waits for them, and re-layouts: 3.53 us -> 2.22 us
    all_to_all x1, blocking collectives: 13.5 us -> 10.9 us  [to_all(): return lax.all_to_all(a, axes, 0, 0, tiled=True)]
    unnamed x13 -> x12, local copies, waits for them, and re-layouts: 2.87 us -> 2.21 us
  transfers between devices with their start and end apart: 9 -> 9, of which waited for: 5 -> 5; matrix products, arithmetic and copies ran while one was open for 2% -> 2% of each run, Pallas kernels for 10% -> 11%
where the time goes in v5:
time: 90.1 us; the launch traced here: 89.7 us
  waiting for transfers between devices  30 us (33%)
  starting transfers between devices  29.7 us (33%)
  Pallas kernels  14 us (16%)
  blocking collectives  10.9 us (12%)
  local copies, waits for them, and re-layouts  2.22 us (2%)
  matrix products  1.44 us (2%)
    all_to_all x3, starting transfers between devices, to_all(): return lax.all_to_all(a, axes, 0, 0, tiled=True)  21.8 us
    ppermute x6, waiting for transfers between devices, shift(): return lax.ppermute(a, 'expert', [(i, (i + step) % n) for i in range(n)])  16.1 us
    all_to_all x3, waiting for transfers between devices, to_all(): return lax.all_to_all(a, axes, 0, 0, tiled=True)  13.9 us
    all_to_all x1, blocking collectives, to_all(): return lax.all_to_all(a, axes, 0, 0, tiled=True)  10.9 us
    ppermute x6, starting transfers between devices, shift(): return lax.ppermute(a, 'expert', [(i, (i + step) % n) for i in range(n)])  7.88 us
    pallas_call x1, Pallas kernels, near_sources(): pl.pallas_call(near_kernel, out_shape=[jax.ShapeDtypeStruct((groups, 2, 1...  4.36 us
    pallas_call x1, Pallas kernels, columns(): pl.pallas_call(columns_kernel, out_shape=jax.ShapeDtypeStruct((count, 144...  3 us
    pallas_call x1, Pallas kernels, split(): pl.pallas_call(split_kernel, out_shape=[jax.ShapeDtypeStruct((64 * count...  2.85 us
  transfers between devices with their start and end apart: 9, of which 5 were waited for; matrix products, arithmetic and copies ran while one was open for 2% of the time, Pallas kernels for 11%

profile of v5, /device:TPU:1, one launch (start us, length us, event | category | flops | bytes accessed | tf_op | source)
XLA Modules:
  0.0 89.7 jit_solution(2171572383277152529)
XLA Ops:
  0.6 0.0 copy-start
  0.6 0.0 copy-start.3
  0.7 0.0 copy-start.5
  0.7 0.0 copy-start.4
  0.7 2.9 %shard_map.85 = (bf16[528,512]{1,0:T(8,128)(2,1)}, bf16[512,512]{1,0:T(8,128)(2,1)}) custom-call(s32[2,128]{1,0:T(2,128)} %bitcast.12, bf16[2,128]{1,0:T(2,128)(2,1)} %bitcast.15, bf16[128,4096]{1,0:T(8,128)(2,1)} %own.1), custom_call_target="tpu_custom_call" | custom-call | bytes 2097152 | tf_op jit(solution)/shard_map/pallas_call | solution.py:72
  3.5 2.2 %collective-permute-start = (bf16[528,512]{1,0:T(8,128)(2,1)}, bf16[528,512]{1,0:T(8,128)(2,1)}, u32[]{:S(2)}, u32[]{:S(2)}) collective-permute-start(bf16[528,512]{1,0:T(8,128)(2,1)} %get-tuple-element.21), channel_id=1, source_target_pairs={{0,1},{1,2},{2,3},{3,0},{4,5},{5,6},{6,7},{7,4},{8,9},{9,10},{10,1... | collective-permute-start | bytes 1622024 | tf_op jit(solution)/shard_map/ppermute | solution.py:29
  5.7 1.5 %collective-permute-start.2 = (bf16[512,512]{1,0:T(8,128)(2,1)}, bf16[512,512]{1,0:T(8,128)(2,1)}, u32[]{:S(2)}, u32[]{:S(2)}) collective-permute-start(bf16[512,512]{1,0:T(8,128)(2,1)} %get-tuple-element.20), channel_id=1, source_target_pairs={{0,3},{1,0},{2,1},{3,2},{4,7},{5,4},{6,5},{7,6},{8,11},{9,8},{10,9... | collective-permute-start | bytes 1572872 | tf_op jit(solution)/shard_map/ppermute | solution.py:29
  7.3 3.0 %shard_map.88 = bf16[8,144,512]{2,1,0:T(8,128)(2,1)} custom-call(s32[2,128]{1,0:T(2,128)} %bitcast.13, bf16[2,128]{1,0:T(2,128)(2,1)} %bitcast.16, bf16[128,4096]{1,0:T(8,128)(2,1)} %tokens_ref), custom_call_target="tpu_custom_call" | custom-call | bytes 2097152 | tf_op jit(solution)/shard_map/pallas_call | solution.py:113
  10.3 6.3 %all-to-all-start = ((bf16[8,144,512]{2,1,0:T(8,128)(2,1)}), bf16[8,144,512]{2,1,0:T(8,128)(2,1)S(1)}, u32[]{:S(2)}, u32[]{:S(2)}) async-start(bf16[8,144,512]{2,1,0:T(8,128)(2,1)} %shard_map.88), calls=%async_computation | async-start | bytes 2359296 | tf_op jit(solution)/shard_map/all_to_all | solution.py:33
  16.6 0.6 collective-permute-start.5
  17.2 0.8 collective-permute-start.4
  18.0 0.0 collective-permute-done.lu
  18.1 1.0 %collective-permute-start.1 = (bf16[528,512]{1,0:T(8,128)(2,1)}, bf16[528,512]{1,0:T(8,128)(2,1)S(1)}, u32[]{:S(2)}, u32[]{:S(2)}) collective-permute-start(bf16[528,512]{1,0:T(8,128)(2,1)} %collective-permute-done.lu), channel_id=1, source_target_pairs={{0,1},{1,2},{2,3},{3,0},{4,5},{5,6},{6,7},{7,4},{8,9},{9,10},{10,1... | collective-permute-start | bytes 1622024 | tf_op jit(solution)/shard_map/ppermute | solution.py:29
  19.0 0.0 collective-permute-done.2.rl
  19.0 1.7 %collective-permute-start.3 = (bf16[512,512]{1,0:T(8,128)(2,1)}, bf16[512,512]{1,0:T(8,128)(2,1)S(1)}, u32[]{:S(2)}, u32[]{:S(2)}) collective-permute-start(bf16[512,512]{1,0:T(8,128)(2,1)} %collective-permute-done.2.rl), channel_id=1, source_target_pairs={{0,3},{1,0},{2,1},{3,2},{4,7},{5,4},{6,5},{7,6},{8,11},{9,8},{10,9... | collective-permute-start | bytes 1572872 | tf_op jit(solution)/shard_map/ppermute | solution.py:29
  20.7 11.1 %collective-permute-done.4.ll = bf16[512,512]{1,0:T(8,128)(2,1)S(1)} collective-permute-done((bf16[512,512]{1,0:T(8,128)(2,1)}, bf16[512,512]{1,0:T(8,128)(2,1)S(1)}, u32[]{:S(2)}, u32[]{:S(2)}) %collective-permute-start.4) | collective-permute-done | bytes 524320 | tf_op jit(solution)/shard_map/ppermute | solution.py:29
  31.9 0.0 collective-permute-done.5.ru
  31.9 0.0 copy-done.3
  31.9 0.0 copy-done.5
  31.9 0.0 copy-done.4
  31.9 0.0 copy-start.1
  31.9 2.2 %copy-done.1 = bf16[512,4096]{1,0:T(8,128)(2,1)S(1)} copy-done((bf16[512,4096]{1,0:T(8,128)(2,1)S(1)}, bf16[512,4096]{1,0:T(8,128)(2,1)}, u32[]{:S(2)}) %copy-start.1) | copy-done | bytes 4194328
  34.1 0.0 copy-start.2
  34.1 4.4 %shard_map.86 = (f32[4,2,128]{2,1,0:T(2,128)S(1)}, bf16[2,4,64,4096]{3,2,1,0:T(8,128)(2,1)}) custom-call(s32[2,128]{1,0:T(2,128)S(1)} %bitcast.14, bf16[2,128]{1,0:T(2,128)(2,1)S(1)} %bitcast.17, bf16[2,4,64,4096]{3,2,1,0:T(8,128)(2,1)S(1)} %bitcast.10, bf16[128,4096]{1,0:T(8,128)(2,1)S(1)} %copy-done.3, bf16[528,512]{1,0:T(8,128)(2,1)} %collective-permute-done.lu, ...), custom_call_target="tpu_custom_call" | custom-call | flops 805306368 | bytes 9437184 | tf_op jit(solution)/shard_map/pallas_call | solution.py:216
  38.4 3.9 %collective-permute-done.3.low = bf16[512,512]{1,0:T(8,128)(2,1)S(1)} collective-permute-done((bf16[512,512]{1,0:T(8,128)(2,1)}, bf16[512,512]{1,0:T(8,128)(2,1)S(1)}, u32[]{:S(2)}, u32[]{:S(2)}) %collective-permute-start.3) | collective-permute-done | bytes 524320 | tf_op jit(solution)/shard_map/ppermute | solution.py:29
  42.4 1.1 %collective-permute-done.1.up = bf16[528,512]{1,0:T(8,128)(2,1)S(1)} collective-permute-done((bf16[528,512]{1,0:T(8,128)(2,1)}, bf16[528,512]{1,0:T(8,128)(2,1)S(1)}, u32[]{:S(2)}, u32[]{:S(2)}) %collective-permute-start.1) | collective-permute-done | bytes 540704 | tf_op jit(solution)/shard_map/ppermute | solution.py:29
  43.4 0.0 copy-done.2
  43.4 1.1 %shard_map.87 = f32[8,4,2,128]{3,2,1,0:T(2,128)} custom-call(bf16[2,4,64,4096]{3,2,1,0:T(8,128)(2,1)S(1)} %bitcast.11, bf16[528,512]{1,0:T(8,128)(2,1)S(1)} %collective-permute-done.1.up, bf16[512,512]{1,0:T(8,128)(2,1)S(1)} %collective-permute-done.3.low, f32[4,2,128]{2,1,0:T(2,128)S(1)} %get-tuple-element.22.near_ref), custom_call_target="tpu_custom_call" | custom-call | flops 134217728 | bytes 2097152 | tf_op jit(solution)/shard_map/pallas_call | solution.py:247
  44.5 0.0 all-to-all-done.tokens_ref
  44.5 6.6 %all-to-all-start.1 = ((f32[32,2,128]{2,1,0:T(2,128)}), f32[32,2,128]{2,1,0:T(2,128)S(1)}, u32[]{:S(2)}, u32[]{:S(2)}) async-start(f32[32,2,128]{2,1,0:T(2,128)} %bitcast.3), calls=%async_computation.1 | async-start | bytes 65536 | tf_op jit(solution)/shard_map/all_to_all | solution.py:33
  51.1 1.5 %shard_map.89 = bf16[2,4,64,4096]{3,2,1,0:T(8,128)(2,1)} custom-call(bf16[528,512]{1,0:T(8,128)(2,1)S(1)} %collective-permute-done.1.up, bf16[512,512]{1,0:T(8,128)(2,1)S(1)} %collective-permute-done.3.low, bf16[2,4,64,4096]{3,2,1,0:T(8,128)(2,1)} %get-tuple-element.25._), custom_call_target="tpu_custom_call", output_to_operand_aliasing={{}: (2, {})} | custom-call | flops 134217728 | bytes 2097152 | tf_op jit(solution)/shard_map/pallas_call | solution.py:268
  52.7 5.7 %all-to-all-done.1.home_ref = f32[32,2,128]{2,1,0:T(2,128)S(1)} async-done(((f32[32,2,128]{2,1,0:T(2,128)}), f32[32,2,128]{2,1,0:T(2,128)S(1)}, u32[]{:S(2)}, u32[]{:S(2)}) %all-to-all-start.1) | async-done | bytes 32800 | tf_op jit(solution)/shard_map/all_to_all | solution.py:33
  58.3 1.1 %shard_map.90 = (bf16[8,128]{1,0:T(8,128)(2,1)S(1)}, bf16[32,8,512]{2,1,0:T(8,128)(2,1)}) custom-call(f32[32,2,128]{2,1,0:T(2,128)S(1)} %all-to-all-done.1.home_ref, bf16[8,144,512]{2,1,0:T(8,128)(2,1)S(1)} %all-to-all-done.tokens_ref), custom_call_target="tpu_custom_call" | custom-call | flops 9437184 | bytes 2359296 | tf_op jit(solution)/shard_map/pallas_call | solution.py:312
  59.5 8.9 %all-to-all-start.2 = ((bf16[32,8,512]{2,1,0:T(8,128)(2,1)}), bf16[32,8,512]{2,1,0:T(8,128)(2,1)S(1)}, u32[]{:S(2)}, u32[]{:S(2)}) async-start(bf16[32,8,512]{2,1,0:T(8,128)(2,1)} %get-tuple-element.28), calls=%async_computation.2 | async-start | bytes 524288 | tf_op jit(solution)/shard_map/all_to_all | solution.py:33
  68.4 0.0 copy-done
  68.4 1.4 %convolution_convert_fusion = bf16[128,4096]{1,0:T(8,128)(2,1)} fusion(bf16[8,128]{1,0:T(8,128)(2,1)S(1)} %get-tuple-element.29, bf16[8,4096]{1,0:T(8,128)(2,1)S(1)} %copy-done), kind=kOutput, calls=%fused_computation | convolution fusion | flops 8912896 | bytes 1116160 | tf_op jit(solution)/shard_map/dot_general | solution.py:353
  69.8 8.2 %all-to-all-done.2 = bf16[32,8,512]{2,1,0:T(8,128)(2,1)S(1)} async-done(((bf16[32,8,512]{2,1,0:T(8,128)(2,1)}), bf16[32,8,512]{2,1,0:T(8,128)(2,1)S(1)}, u32[]{:S(2)}, u32[]{:S(2)}) %all-to-all-start.2) | async-done | bytes 262176 | tf_op jit(solution)/shard_map/all_to_all | solution.py:33
  78.1 10.9 %all_to_all.20 = bf16[8,8,512]{2,1,0:T(8,128)(2,1)S(1)} all-to-all(bf16[8,8,512]{2,1,0:T(8,128)(2,1)S(1)} %broadcast_in_dim.3), channel_id=1, replica_groups=mesh['dp_0'=8,'dp_1'=4,'dp_2'=2,'expert'=4] {'dp_1','dp_2'}, dimensions={0} | all-to-all | bytes 131072 | tf_op jit(solution)/shard_map/all_to_all | solution.py:33
  89.0 0.7 reshape.28
  (3 shorter events, 0.1 us)
Async XLA Ops:
  0.6 67.8 %copy-start = (bf16[8,4096]{1,0:T(8,128)(2,1)S(1)}, bf16[8,4096]{1,0:T(8,128)(2,1)}, u32[]{:S(2)}) copy-start(bf16[8,4096]{1,0:T(8,128)(2,1)} %param.10) | copy-start | bytes 196612
  0.6 31.2 %copy-start.3 = (bf16[128,4096]{1,0:T(8,128)(2,1)S(1)}, bf16[128,4096]{1,0:T(8,128)(2,1)}, u32[]{:S(2)}) copy-start(bf16[128,4096]{1,0:T(8,128)(2,1)} %own.1) | copy-start | bytes 3145732
  0.7 31.2 %copy-start.5 = (bf16[128,2]{0,1:T(2,128)(2,1)S(1)}, bf16[128,2]{0,1:T(2,128)(2,1)}, u32[]{:S(2)}) copy-start(bf16[128,2]{0,1:T(2,128)(2,1)} %param.9) | copy-start | bytes 1540
  0.7 31.2 %copy-start.4 = (s32[128,2]{0,1:T(2,128)S(1)}, s32[128,2]{0,1:T(2,128)}, u32[]{:S(2)}) copy-start(s32[128,2]{0,1:T(2,128)} %param.8) | copy-start | bytes 3076
  3.5 14.5 %collective-permute-start = (bf16[528,512]{1,0:T(8,128)(2,1)}, bf16[528,512]{1,0:T(8,128)(2,1)}, u32[]{:S(2)}, u32[]{:S(2)}) collective-permute-start(bf16[528,512]{1,0:T(8,128)(2,1)} %get-tuple-element.21), channel_id=1, source_target_pairs={{0,1},{1,2},{2,3},{3,0},{4,5},{5,6},{6,7},{7,4},{8,9},{9,10},{10,1... | collective-permute-start | bytes 1622024 | tf_op jit(solution)/shard_map/ppermute | solution.py:29
  5.7 13.3 %collective-permute-start.2 = (bf16[512,512]{1,0:T(8,128)(2,1)}, bf16[512,512]{1,0:T(8,128)(2,1)}, u32[]{:S(2)}, u32[]{:S(2)}) collective-permute-start(bf16[512,512]{1,0:T(8,128)(2,1)} %get-tuple-element.20), channel_id=1, source_target_pairs={{0,3},{1,0},{2,1},{3,2},{4,7},{5,4},{6,5},{7,6},{8,11},{9,8},{10,9... | collective-permute-start | bytes 1572872 | tf_op jit(solution)/shard_map/ppermute | solution.py:29
  10.3 34.2 %all-to-all-start = ((bf16[8,144,512]{2,1,0:T(8,128)(2,1)}), bf16[8,144,512]{2,1,0:T(8,128)(2,1)S(1)}, u32[]{:S(2)}, u32[]{:S(2)}) async-start(bf16[8,144,512]{2,1,0:T(8,128)(2,1)} %shard_map.88), calls=%async_computation | async-start | bytes 2359296 | tf_op jit(solution)/shard_map/all_to_all | solution.py:33
  16.6 15.3 %collective-permute-start.5 = (bf16[528,512]{1,0:T(8,128)(2,1)}, bf16[528,512]{1,0:T(8,128)(2,1)S(1)}, u32[]{:S(2)}, u32[]{:S(2)}) collective-permute-start(bf16[528,512]{1,0:T(8,128)(2,1)} %get-tuple-element.21), channel_id=1, source_target_pairs={{0,3},{1,0},{2,1},{3,2},{4,7},{5,4},{6,5},{7,6},{8,11},{9,8},{10,9... | collective-permute-start | bytes 1622024 | tf_op jit(solution)/shard_map/ppermute | solution.py:29
  17.2 14.7 %collective-permute-start.4 = (bf16[512,512]{1,0:T(8,128)(2,1)}, bf16[512,512]{1,0:T(8,128)(2,1)S(1)}, u32[]{:S(2)}, u32[]{:S(2)}) collective-permute-start(bf16[512,512]{1,0:T(8,128)(2,1)} %get-tuple-element.20), channel_id=1, source_target_pairs={{0,1},{1,2},{2,3},{3,0},{4,5},{5,6},{6,7},{7,4},{8,9},{9,10},{10,1... | collective-permute-start | bytes 1572872 | tf_op jit(solution)/shard_map/ppermute | solution.py:29
  18.1 25.4 %collective-permute-start.1 = (bf16[528,512]{1,0:T(8,128)(2,1)}, bf16[528,512]{1,0:T(8,128)(2,1)S(1)}, u32[]{:S(2)}, u32[]{:S(2)}) collective-permute-start(bf16[528,512]{1,0:T(8,128)(2,1)} %collective-permute-done.lu), channel_id=1, source_target_pairs={{0,1},{1,2},{2,3},{3,0},{4,5},{5,6},{6,7},{7,4},{8,9},{9,10},{10,1... | collective-permute-start | bytes 1622024 | tf_op jit(solution)/shard_map/ppermute | solution.py:29
  19.0 23.4 %collective-permute-start.3 = (bf16[512,512]{1,0:T(8,128)(2,1)}, bf16[512,512]{1,0:T(8,128)(2,1)S(1)}, u32[]{:S(2)}, u32[]{:S(2)}) collective-permute-start(bf16[512,512]{1,0:T(8,128)(2,1)} %collective-permute-done.2.rl), channel_id=1, source_target_pairs={{0,3},{1,0},{2,1},{3,2},{4,7},{5,4},{6,5},{7,6},{8,11},{9,8},{10,9... | collective-permute-start | bytes 1572872 | tf_op jit(solution)/shard_map/ppermute | solution.py:29
  31.9 2.2 %copy-start.1 = (bf16[512,4096]{1,0:T(8,128)(2,1)S(1)}, bf16[512,4096]{1,0:T(8,128)(2,1)}, u32[]{:S(2)}) copy-start(bf16[512,4096]{1,0:T(8,128)(2,1)} %param.11) | copy-start | bytes 12582916
  34.1 9.4 %copy-start.2 = (bf16[512,4096]{1,0:T(8,128)(2,1)S(1)}, bf16[512,4096]{1,0:T(8,128)(2,1)}, u32[]{:S(2)}) copy-start(bf16[512,4096]{1,0:T(8,128)(2,1)} %param.11) | copy-start | bytes 12582916
  44.5 13.8 %all-to-all-start.1 = ((f32[32,2,128]{2,1,0:T(2,128)}), f32[32,2,128]{2,1,0:T(2,128)S(1)}, u32[]{:S(2)}, u32[]{:S(2)}) async-start(f32[32,2,128]{2,1,0:T(2,128)} %bitcast.3), calls=%async_computation.1 | async-start | bytes 65536 | tf_op jit(solution)/shard_map/all_to_all | solution.py:33
  59.5 18.6 %all-to-all-start.2 = ((bf16[32,8,512]{2,1,0:T(8,128)(2,1)}), bf16[32,8,512]{2,1,0:T(8,128)(2,1)S(1)}, u32[]{:S(2)}, u32[]{:S(2)}) async-start(bf16[32,8,512]{2,1,0:T(8,128)(2,1)} %get-tuple-element.28), calls=%async_computation.2 | async-start | bytes 524288 | tf_op jit(solution)/shard_map/all_to_all | solution.py:33

commit v6 on v5

--- a/solution.py
+++ b/solution.py
@@ -8,10 +8,11 @@
 from jax.sharding import Mesh
 from jax.sharding import PartitionSpec as P
 
-DP_EXPERT = ("dp_0", "dp_1", "dp_2", "expert")
+DP_EXPERT = ("far_z", "near_z", "dp_1", "dp_2", "expert")
 PLANE = ("dp_1", "dp_2")
 HOUSE = ("dp_1", "dp_2", "expert")
-REST = ("expert", "dp_0")
+REST = ("expert", "far_z", "near_z")
+SLICES = ("dp_1", "dp_2", "near_z")
 BF16 = jnp.bfloat16
 F32 = jnp.float32
 PIECE = 512
@@ -37,26 +38,32 @@
     return jnp.broadcast_to(v, (rows, v.shape[1]))
 
 
-def meta_rows(experts_ref, gates_ref):
-    lines = [experts_ref[...].astype(F32), gates_ref[...].astype(F32), jnp.zeros((12, 128), F32)]
+def meta_rows(experts, gates):
+    lines = [experts.astype(F32), gates.astype(F32), jnp.zeros((12, 128), F32)]
     return jnp.concatenate(lines, axis=0).astype(BF16)
 
 
-def split_kernel(experts_ref, gates_ref, grad_ref, upper_ref, lower_ref, rows_ref, up_ref, low_ref, sems):
+def fetch(pairs, sems):
+    copies = [pltpu.make_async_copy(a, b, sems.at[i]) for i, (a, b) in enumerate(pairs)]
+    for copy in copies:
+        copy.start()
+    return copies
+
+
+def split_kernel(experts_hbm, gates_hbm, grad_ref, upper_ref, lower_ref, rows_ref, up_ref, low_ref, experts_ref, gates_ref, in_sems, out_sems):
     count = grad_ref.shape[1] // PIECE
-    arriving = [
-        pltpu.make_async_copy(grad_ref.at[64 * h : 64 * h + 64], rows_ref.at[h], sems.at[0, h])
-        for h in range(2)
-    ]
-    for copy in arriving:
-        copy.start()
+    pairs = [(grad_ref.at[64 * h : 64 * h + 64], rows_ref.at[h]) for h in range(2)]
+    pairs += [(experts_hbm, experts_ref), (gates_hbm, gates_ref)]
+    arriving = fetch(pairs, in_sems)
     halves = (up_ref, low_ref)
     end = up_ref.shape[0] - 16
     up_ref[end:, :] = jnp.zeros((16, PIECE), BF16)
-    up_ref[end:, 0:128] = meta_rows(experts_ref, gates_ref)
+    arriving[2].wait()
+    arriving[3].wait()
+    up_ref[end:, 0:128] = meta_rows(experts_ref[...], gates_ref[...])
     leaving = [
-        pltpu.make_async_copy(up_ref, upper_ref, sems.at[1, 0]),
-        pltpu.make_async_copy(low_ref, lower_ref, sems.at[1, 1]),
+        pltpu.make_async_copy(up_ref, upper_ref, out_sems.at[0]),
+        pltpu.make_async_copy(low_ref, lower_ref, out_sems.at[1]),
     ]
     for half in range(2):
         arriving[half].wait()
@@ -75,27 +82,25 @@
             jax.ShapeDtypeStruct((64 * count + 16, PIECE), BF16),
             jax.ShapeDtypeStruct((64 * count, PIECE), BF16),
         ],
-        in_specs=[VMEM, VMEM, ANY],
+        in_specs=[ANY, ANY, ANY],
         out_specs=[ANY, ANY],
         scratch_shapes=[
             pltpu.VMEM((2, 64, grad.shape[1]), BF16),
             pltpu.VMEM((64 * count + 16, PIECE), BF16),
             pltpu.VMEM((64 * count, PIECE), BF16),
-            pltpu.SemaphoreType.DMA((2, 2)),
+            pltpu.VMEM(experts.shape, experts.dtype),
+            pltpu.VMEM(gates.shape, gates.dtype),
+            pltpu.SemaphoreType.DMA((4,)),
+            pltpu.SemaphoreType.DMA((2,)),
         ],
         cost_estimate=cost(0, 4 * grad.size),
     )(experts, gates, grad)
 
 
-def columns_kernel(experts_ref, gates_ref, tokens_ref, out_ref, rows_ref, held_ref, sems):
+def columns_kernel(experts_ref, gates_ref, tokens_ref, out_ref, rows_ref, held_ref, in_sems, out_sem):
     count, _, piece = out_ref.shape
-    arriving = [
-        pltpu.make_async_copy(tokens_ref.at[64 * h : 64 * h + 64], rows_ref.at[h], sems.at[0, h])
-        for h in range(2)
-    ]
-    for copy in arriving:
-        copy.start()
-    meta = meta_rows(experts_ref, gates_ref)
+    arriving = fetch([(tokens_ref.at[64 * h : 64 * h + 64], rows_ref.at[h]) for h in range(2)], in_sems)
+    meta = meta_rows(experts_ref[...], gates_ref[...])
     for j in range(count):
         held_ref[j, 128:144, :] = jnp.zeros((16, piece), BF16)
         held_ref[j, 128:144, 0:128] = meta
@@ -103,7 +108,7 @@
         arriving[half].wait()
         for j in range(count):
             held_ref[j, 64 * half : 64 * half + 64] = rows_ref[half, :, j * piece : (j + 1) * piece]
-    last = pltpu.make_async_copy(held_ref, out_ref, sems.at[1, 0])
+    last = pltpu.make_async_copy(held_ref, out_ref, out_sem)
     last.start()
     last.wait()
 
@@ -118,7 +123,8 @@
         scratch_shapes=[
             pltpu.VMEM((2, 64, tokens.shape[1]), BF16),
             pltpu.VMEM((count, 144, piece), BF16),
-            pltpu.SemaphoreType.DMA((2, 2)),
+            pltpu.SemaphoreType.DMA((2,)),
+            pltpu.SemaphoreType.DMA,
         ],
         cost_estimate=cost(0, 4 * tokens.size),
     )(experts, gates, tokens)
@@ -191,7 +197,7 @@
 def near_kernel(experts_ref, gates_ref, saved_ref, own, lu, ll, ru, rl, out_ref, grad_ref, held_ref, sems):
     me = lax.axis_index("expert")
     groups = saved_ref.shape[1]
-    own_meta = meta_rows(experts_ref, gates_ref)
+    own_meta = meta_rows(experts_ref[...], gates_ref[...])
     end = ll.shape[0]
     sources = (
         (0, own_meta, (own,)),
@@ -303,12 +309,14 @@
     every = jnp.concatenate(found, axis=1)
     features = jnp.concatenate([tokens_ref[b, 0:128] for b in range(blocks)], axis=0)
     part = jnp.dot(every, features, preferred_element_type=F32).astype(BF16)
+    piece = out_ref.shape[2]
     for j in range(out_ref.shape[0]):
-        out_ref[j] = part
-
-
-def logits(home, tokens, copies):
-    piece = tokens.shape[2]
+        at = j % (part.shape[1] // piece) * piece
+        out_ref[j] = part[:, at : at + piece]
+
+
+def logits(home, tokens, copies, slices):
+    piece = tokens.shape[2] // slices
     return pl.pallas_call(
         logit_kernel,
         out_shape=[
@@ -348,22 +356,22 @@
     home = to_all(sent.reshape(houses * groups, 2, 128), HOUSE)
     expert_grad = far_rows((far_upper, far_lower), expert_grad)
 
-    home, expert_grad = lax.optimization_barrier((home, expert_grad))
-    logit, parts = logits(home, turned, lax.axis_size(REST))
+    logit, parts = logits(home, turned, lax.axis_size(REST), lax.axis_size("near_z"))
     input_grad = lax.dot_general(
         logit, router_weight, (((0,), (0,)), ((), ())), preferred_element_type=F32
     ).astype(BF16)
     scale = float(lax.axis_size(DP_EXPERT) * tokens.shape[0]) ** (-0.5)
     total = to_all(parts, REST).astype(F32).sum(axis=0) * scale
-    total, input_grad = lax.optimization_barrier((total, input_grad))
-    whole = to_all(jnp.broadcast_to(total.astype(BF16), (houses, *total.shape)), PLANE).astype(F32)
+    total, input_grad, expert_grad = lax.optimization_barrier((total, input_grad, expert_grad))
+    copies = jnp.broadcast_to(total.astype(BF16), (lax.axis_size(SLICES), *total.shape))
+    whole = to_all(copies, SLICES).astype(F32)
     router_grad = whole.swapaxes(0, 1).reshape(8, width)
     return input_grad, router_grad, expert_grad.reshape(saved_outputs.shape)
 
 
 def solution(mesh):
     finer = Mesh(
-        mesh.devices.reshape(8, 4, 2, mesh.shape["expert"]), ("dp_0", "dp_1", "dp_2", "expert")
+        mesh.devices.reshape(4, 2, 4, 2, mesh.shape["expert"]), DP_EXPERT
     )
     rows = P(DP_EXPERT, None)
     return jax.shard_map(

time: 90.1 us -> 88.2 us (0.979)
  blocking collectives: 10.9 us -> 24.8 us
  waiting for transfers between devices: 30 us -> 22.3 us
  starting transfers between devices: 29.7 us -> 23.1 us
  Pallas kernels: 14 us -> 12.6 us
    all_to_all x1 -> x2, blocking collectives: 10.9 us -> 24.8 us  [to_all(): return lax.all_to_all(a, axes, 0, 0, tiled=True)]
    all_to_all x3 -> x2, waiting for transfers between devices: 13.9 us -> 6.16 us  [to_all(): return lax.all_to_all(a, axes, 0, 0, tiled=True)]
    all_to_all x3 -> x2, starting transfers between devices: 21.8 us -> 15.2 us  [to_all(): return lax.all_to_all(a, axes, 0, 0, tiled=True)]
  transfers between devices with their start and end apart: 9 -> 8, of which waited for: 5 -> 4; matrix products, arithmetic and copies ran while one was open for 2% -> 2% of each run, Pallas kernels for 11% -> 11%
where the time goes in v6:
time: 88.2 us; the launch traced here: 87.9 us
  blocking collectives  24.8 us (28%)
  starting transfers between devices  23.1 us (26%)
  waiting for transfers between devices  22.3 us (25%)
  Pallas kernels  12.6 us (14%)
  local copies, waits for them, and re-layouts  2.22 us (3%)
  matrix products  1.44 us (2%)
    all_to_all x2, blocking collectives, to_all(): return lax.all_to_all(a, axes, 0, 0, tiled=True)  24.8 us
    ppermute x6, waiting for transfers between devices, shift(): return lax.ppermute(a, 'expert', [(i, (i + step) % n) for i in range(n)])  16.1 us
    all_to_all x2, starting transfers between devices, to_all(): return lax.all_to_all(a, axes, 0, 0, tiled=True)  15.2 us
    ppermute x6, starting transfers between devices, shift(): return lax.ppermute(a, 'expert', [(i, (i + step) % n) for i in range(n)])  7.88 us
    all_to_all x2, waiting for transfers between devices, to_all(): return lax.all_to_all(a, axes, 0, 0, tiled=True)  6.16 us
    pallas_call x1, Pallas kernels, near_sources(): pl.pallas_call(near_kernel, out_shape=[jax.ShapeDtypeStruct((groups, 2, 1...  4.36 us
    pallas_call x1, Pallas kernels, columns(): pl.pallas_call(columns_kernel, out_shape=jax.ShapeDtypeStruct((count, 144...  2.97 us
    unnamed x12, local copies, waits for them, and re-layouts  2.21 us
  transfers between devices with their start and end apart: 8, of which 4 were waited for; matrix products, arithmetic and copies ran while one was open for 2% of the time, Pallas kernels for 11%

profile of v6, /device:TPU:1, one launch (start us, length us, event | category | flops | bytes accessed | tf_op | source)
XLA Modules:
  0.0 87.9 jit_solution(13875769256418204721)
XLA Ops:
  0.6 0.0 copy-start
  0.6 0.0 copy-start.4
  0.7 0.0 copy-start.5
  0.7 0.0 copy-start.3
  0.7 2.2 %shard_map.85 = (bf16[528,512]{1,0:T(8,128)(2,1)}, bf16[512,512]{1,0:T(8,128)(2,1)}) custom-call(s32[2,128]{1,0:T(2,128)} %bitcast.13, bf16[2,128]{1,0:T(2,128)(2,1)} %bitcast.16, bf16[128,4096]{1,0:T(8,128)(2,1)} %own.1), custom_call_target="tpu_custom_call" | custom-call | bytes 2097152 | tf_op jit(solution)/shard_map/pallas_call | solution.py:79
  2.9 2.2 %collective-permute-start = (bf16[528,512]{1,0:T(8,128)(2,1)}, bf16[528,512]{1,0:T(8,128)(2,1)}, u32[]{:S(2)}, u32[]{:S(2)}) collective-permute-start(bf16[528,512]{1,0:T(8,128)(2,1)} %get-tuple-element.20), channel_id=1, source_target_pairs={{0,1},{1,2},{2,3},{3,0},{4,5},{5,6},{6,7},{7,4},{8,9},{9,10},{10,1... | collective-permute-start | bytes 1622024 | tf_op jit(solution)/shard_map/ppermute | solution.py:30
  5.1 1.5 %collective-permute-start.2 = (bf16[512,512]{1,0:T(8,128)(2,1)}, bf16[512,512]{1,0:T(8,128)(2,1)}, u32[]{:S(2)}, u32[]{:S(2)}) collective-permute-start(bf16[512,512]{1,0:T(8,128)(2,1)} %get-tuple-element.19), channel_id=1, source_target_pairs={{0,3},{1,0},{2,1},{3,2},{4,7},{5,4},{6,5},{7,6},{8,11},{9,8},{10,9... | collective-permute-start | bytes 1572872 | tf_op jit(solution)/shard_map/ppermute | solution.py:30
  6.6 3.0 %shard_map.88 = bf16[8,144,512]{2,1,0:T(8,128)(2,1)} custom-call(s32[2,128]{1,0:T(2,128)} %bitcast.14, bf16[2,128]{1,0:T(2,128)(2,1)} %bitcast.17, bf16[128,4096]{1,0:T(8,128)(2,1)} %tokens_ref), custom_call_target="tpu_custom_call" | custom-call | bytes 2097152 | tf_op jit(solution)/shard_map/pallas_call | solution.py:118
  9.6 6.3 %all-to-all-start = ((bf16[8,144,512]{2,1,0:T(8,128)(2,1)}), bf16[8,144,512]{2,1,0:T(8,128)(2,1)S(1)}, u32[]{:S(2)}, u32[]{:S(2)}) async-start(bf16[8,144,512]{2,1,0:T(8,128)(2,1)} %shard_map.88), calls=%async_computation | async-start | bytes 2359296 | tf_op jit(solution)/shard_map/all_to_all | solution.py:34
  15.9 0.6 collective-permute-start.5
  16.5 0.8 collective-permute-start.4
  17.4 0.0 collective-permute-done.lu
  17.4 1.0 %collective-permute-start.1 = (bf16[528,512]{1,0:T(8,128)(2,1)}, bf16[528,512]{1,0:T(8,128)(2,1)S(1)}, u32[]{:S(2)}, u32[]{:S(2)}) collective-permute-start(bf16[528,512]{1,0:T(8,128)(2,1)} %collective-permute-done.lu), channel_id=1, source_target_pairs={{0,1},{1,2},{2,3},{3,0},{4,5},{5,6},{6,7},{7,4},{8,9},{9,10},{10,1... | collective-permute-start | bytes 1622024 | tf_op jit(solution)/shard_map/ppermute | solution.py:30
  18.4 0.0 collective-permute-done.2.rl
  18.4 1.7 %collective-permute-start.3 = (bf16[512,512]{1,0:T(8,128)(2,1)}, bf16[512,512]{1,0:T(8,128)(2,1)S(1)}, u32[]{:S(2)}, u32[]{:S(2)}) collective-permute-start(bf16[512,512]{1,0:T(8,128)(2,1)} %collective-permute-done.2.rl), channel_id=1, source_target_pairs={{0,3},{1,0},{2,1},{3,2},{4,7},{5,4},{6,5},{7,6},{8,11},{9,8},{10,9... | collective-permute-start | bytes 1572872 | tf_op jit(solution)/shard_map/ppermute | solution.py:30
  20.0 11.1 %collective-permute-done.4.ll = bf16[512,512]{1,0:T(8,128)(2,1)S(1)} collective-permute-done((bf16[512,512]{1,0:T(8,128)(2,1)}, bf16[512,512]{1,0:T(8,128)(2,1)S(1)}, u32[]{:S(2)}, u32[]{:S(2)}) %collective-permute-start.4) | collective-permute-done | bytes 524320 | tf_op jit(solution)/shard_map/ppermute | solution.py:30
  31.2 0.0 collective-permute-done.5.ru
  31.2 0.0 copy-done.4
  31.2 0.0 copy-done.5
  31.2 0.0 copy-done.3
  31.2 0.0 copy-start.1
  31.2 2.2 %copy-done.1 = bf16[512,4096]{1,0:T(8,128)(2,1)S(1)} copy-done((bf16[512,4096]{1,0:T(8,128)(2,1)S(1)}, bf16[512,4096]{1,0:T(8,128)(2,1)}, u32[]{:S(2)}) %copy-start.1) | copy-done | bytes 4194328
  33.4 0.0 copy-start.2
  33.4 4.4 %shard_map.86 = (f32[4,2,128]{2,1,0:T(2,128)S(1)}, bf16[2,4,64,4096]{3,2,1,0:T(8,128)(2,1)}) custom-call(s32[2,128]{1,0:T(2,128)S(1)} %bitcast.15, bf16[2,128]{1,0:T(2,128)(2,1)S(1)} %bitcast.18, bf16[2,4,64,4096]{3,2,1,0:T(8,128)(2,1)S(1)} %bitcast.10, bf16[128,4096]{1,0:T(8,128)(2,1)S(1)} %copy-done.3, bf16[528,512]{1,0:T(8,128)(2,1)} %collective-permute-done.lu, ...), custom_call_target="tpu_custom_call" | custom-call | flops 805306368 | bytes 9437184 | tf_op jit(solution)/shard_map/pallas_call | solution.py:222
  37.8 3.9 %collective-permute-done.3.low = bf16[512,512]{1,0:T(8,128)(2,1)S(1)} collective-permute-done((bf16[512,512]{1,0:T(8,128)(2,1)}, bf16[512,512]{1,0:T(8,128)(2,1)S(1)}, u32[]{:S(2)}, u32[]{:S(2)}) %collective-permute-start.3) | collective-permute-done | bytes 524320 | tf_op jit(solution)/shard_map/ppermute | solution.py:30
  41.7 1.1 %collective-permute-done.1.up = bf16[528,512]{1,0:T(8,128)(2,1)S(1)} collective-permute-done((bf16[528,512]{1,0:T(8,128)(2,1)}, bf16[528,512]{1,0:T(8,128)(2,1)S(1)}, u32[]{:S(2)}, u32[]{:S(2)}) %collective-permute-start.1) | collective-permute-done | bytes 540704 | tf_op jit(solution)/shard_map/ppermute | solution.py:30
  42.8 0.0 copy-done.2
  42.8 0.4 shard_map.87
  43.2 0.0 all-to-all-done.tokens_ref
  43.2 13.6 %all_to_all.20.home_ref = f32[32,2,128]{2,1,0:T(2,128)S(1)} all-to-all(f32[32,2,128]{2,1,0:T(2,128)S(1)} %bitcast.12), channel_id=1, replica_groups=mesh['far_z'=4,'near_z'=2,'dp_1'=4,'dp_2'=2,'expert'=4] {'dp_1','dp_2','..., dimensions={0} | all-to-all | bytes 65536 | tf_op jit(solution)/shard_map/all_to_all | solution.py:34
  56.9 1.1 %shard_map.89 = (bf16[8,128]{1,0:T(8,128)(2,1)S(1)}, bf16[32,8,256]{2,1,0:T(8,128)(2,1)}) custom-call(f32[32,2,128]{2,1,0:T(2,128)S(1)} %all_to_all.20.home_ref, bf16[8,144,512]{2,1,0:T(8,128)(2,1)S(1)} %all-to-all-done.tokens_ref), custom_call_target="tpu_custom_call" | custom-call | flops 9437184 | bytes 2359296 | tf_op jit(solution)/shard_map/pallas_call | solution.py:320
  57.9 8.9 %all-to-all-start.2 = ((bf16[32,8,256]{2,1,0:T(8,128)(2,1)}), bf16[32,8,256]{2,1,0:T(8,128)(2,1)S(1)}, u32[]{:S(2)}, u32[]{:S(2)}) async-start(bf16[32,8,256]{2,1,0:T(8,128)(2,1)} %get-tuple-element.25), calls=%async_computation.2 | async-start | bytes 262144 | tf_op jit(solution)/shard_map/all_to_all | solution.py:34
  66.8 1.5 %shard_map.90 = bf16[2,4,64,4096]{3,2,1,0:T(8,128)(2,1)} custom-call(bf16[528,512]{1,0:T(8,128)(2,1)S(1)} %collective-permute-done.1.up, bf16[512,512]{1,0:T(8,128)(2,1)S(1)} %collective-permute-done.3.low, bf16[2,4,64,4096]{3,2,1,0:T(8,128)(2,1)} %get-tuple-element.27._), custom_call_target="tpu_custom_call", output_to_operand_aliasing={{}: (2, {})} | custom-call | flops 134217728 | bytes 2097152 | tf_op jit(solution)/shard_map/pallas_call | solution.py:274
  68.4 0.0 copy-done
  68.4 1.4 %convolution_convert_fusion = bf16[128,4096]{1,0:T(8,128)(2,1)} fusion(bf16[8,128]{1,0:T(8,128)(2,1)S(1)} %get-tuple-element.26, bf16[8,4096]{1,0:T(8,128)(2,1)S(1)} %copy-done), kind=kOutput, calls=%fused_computation | convolution fusion | flops 8912896 | bytes 1116160 | tf_op jit(solution)/shard_map/dot_general | solution.py:360
  69.8 6.2 %all-to-all-done.2 = bf16[32,8,256]{2,1,0:T(8,128)(2,1)S(1)} async-done(((bf16[32,8,256]{2,1,0:T(8,128)(2,1)}), bf16[32,8,256]{2,1,0:T(8,128)(2,1)S(1)}, u32[]{:S(2)}, u32[]{:S(2)}) %all-to-all-start.2) | async-done | bytes 131104 | tf_op jit(solution)/shard_map/all_to_all | solution.py:34
  76.1 11.1 %all_to_all.21 = bf16[16,8,256]{2,1,0:T(8,128)(2,1)S(1)} all-to-all(bf16[16,8,256]{2,1,0:T(8,128)(2,1)S(1)} %broadcast_in_dim.3), channel_id=1, replica_groups=mesh['far_z'=4,'near_z'=2,'dp_1'=4,'dp_2'=2,'expert'=4] {'dp_1','dp_2','..., dimensions={0} | all-to-all | bytes 131072 | tf_op jit(solution)/shard_map/all_to_all | solution.py:34
  87.2 0.7 reshape.28
  (3 shorter events, 0.0 us)
Async XLA Ops:
  0.6 67.8 %copy-start = (bf16[8,4096]{1,0:T(8,128)(2,1)S(1)}, bf16[8,4096]{1,0:T(8,128)(2,1)}, u32[]{:S(2)}) copy-start(bf16[8,4096]{1,0:T(8,128)(2,1)} %param.10) | copy-start | bytes 196612
  0.6 30.5 %copy-start.4 = (s32[128,2]{0,1:T(2,128)S(1)}, s32[128,2]{0,1:T(2,128)}, u32[]{:S(2)}) copy-start(s32[128,2]{0,1:T(2,128)} %param.8) | copy-start | bytes 3076
  0.7 30.5 %copy-start.5 = (bf16[128,2]{0,1:T(2,128)(2,1)S(1)}, bf16[128,2]{0,1:T(2,128)(2,1)}, u32[]{:S(2)}) copy-start(bf16[128,2]{0,1:T(2,128)(2,1)} %param.9) | copy-start | bytes 1540
  0.7 30.5 %copy-start.3 = (bf16[128,4096]{1,0:T(8,128)(2,1)S(1)}, bf16[128,4096]{1,0:T(8,128)(2,1)}, u32[]{:S(2)}) copy-start(bf16[128,4096]{1,0:T(8,128)(2,1)} %own.1) | copy-start | bytes 3145732
  2.9 14.5 %collective-permute-start = (bf16[528,512]{1,0:T(8,128)(2,1)}, bf16[528,512]{1,0:T(8,128)(2,1)}, u32[]{:S(2)}, u32[]{:S(2)}) collective-permute-start(bf16[528,512]{1,0:T(8,128)(2,1)} %get-tuple-element.20), channel_id=1, source_target_pairs={{0,1},{1,2},{2,3},{3,0},{4,5},{5,6},{6,7},{7,4},{8,9},{9,10},{10,1... | collective-permute-start | bytes 1622024 | tf_op jit(solution)/shard_map/ppermute | solution.py:30
  5.1 13.3 %collective-permute-start.2 = (bf16[512,512]{1,0:T(8,128)(2,1)}, bf16[512,512]{1,0:T(8,128)(2,1)}, u32[]{:S(2)}, u32[]{:S(2)}) collective-permute-start(bf16[512,512]{1,0:T(8,128)(2,1)} %get-tuple-element.19), channel_id=1, source_target_pairs={{0,3},{1,0},{2,1},{3,2},{4,7},{5,4},{6,5},{7,6},{8,11},{9,8},{10,9... | collective-permute-start | bytes 1572872 | tf_op jit(solution)/shard_map/ppermute | solution.py:30
  9.6 33.6 %all-to-all-start = ((bf16[8,144,512]{2,1,0:T(8,128)(2,1)}), bf16[8,144,512]{2,1,0:T(8,128)(2,1)S(1)}, u32[]{:S(2)}, u32[]{:S(2)}) async-start(bf16[8,144,512]{2,1,0:T(8,128)(2,1)} %shard_map.88), calls=%async_computation | async-start | bytes 2359296 | tf_op jit(solution)/shard_map/all_to_all | solution.py:34
  15.9 15.3 %collective-permute-start.5 = (bf16[528,512]{1,0:T(8,128)(2,1)}, bf16[528,512]{1,0:T(8,128)(2,1)S(1)}, u32[]{:S(2)}, u32[]{:S(2)}) collective-permute-start(bf16[528,512]{1,0:T(8,128)(2,1)} %get-tuple-element.20), channel_id=1, source_target_pairs={{0,3},{1,0},{2,1},{3,2},{4,7},{5,4},{6,5},{7,6},{8,11},{9,8},{10,9... | collective-permute-start | bytes 1622024 | tf_op jit(solution)/shard_map/ppermute | solution.py:30
  16.5 14.7 %collective-permute-start.4 = (bf16[512,512]{1,0:T(8,128)(2,1)}, bf16[512,512]{1,0:T(8,128)(2,1)S(1)}, u32[]{:S(2)}, u32[]{:S(2)}) collective-permute-start(bf16[512,512]{1,0:T(8,128)(2,1)} %get-tuple-element.19), channel_id=1, source_target_pairs={{0,1},{1,2},{2,3},{3,0},{4,5},{5,6},{6,7},{7,4},{8,9},{9,10},{10,1... | collective-permute-start | bytes 1572872 | tf_op jit(solution)/shard_map/ppermute | solution.py:30
  17.4 25.4 %collective-permute-start.1 = (bf16[528,512]{1,0:T(8,128)(2,1)}, bf16[528,512]{1,0:T(8,128)(2,1)S(1)}, u32[]{:S(2)}, u32[]{:S(2)}) collective-permute-start(bf16[528,512]{1,0:T(8,128)(2,1)} %collective-permute-done.lu), channel_id=1, source_target_pairs={{0,1},{1,2},{2,3},{3,0},{4,5},{5,6},{6,7},{7,4},{8,9},{9,10},{10,1... | collective-permute-start | bytes 1622024 | tf_op jit(solution)/shard_map/ppermute | solution.py:30
  18.4 23.3 %collective-permute-start.3 = (bf16[512,512]{1,0:T(8,128)(2,1)}, bf16[512,512]{1,0:T(8,128)(2,1)S(1)}, u32[]{:S(2)}, u32[]{:S(2)}) collective-permute-start(bf16[512,512]{1,0:T(8,128)(2,1)} %collective-permute-done.2.rl), channel_id=1, source_target_pairs={{0,3},{1,0},{2,1},{3,2},{4,7},{5,4},{6,5},{7,6},{8,11},{9,8},{10,9... | collective-permute-start | bytes 1572872 | tf_op jit(solution)/shard_map/ppermute | solution.py:30
  31.2 2.2 %copy-start.1 = (bf16[512,4096]{1,0:T(8,128)(2,1)S(1)}, bf16[512,4096]{1,0:T(8,128)(2,1)}, u32[]{:S(2)}) copy-start(bf16[512,4096]{1,0:T(8,128)(2,1)} %param.11) | copy-start | bytes 12582916
  33.4 9.4 %copy-start.2 = (bf16[512,4096]{1,0:T(8,128)(2,1)S(1)}, bf16[512,4096]{1,0:T(8,128)(2,1)}, u32[]{:S(2)}) copy-start(bf16[512,4096]{1,0:T(8,128)(2,1)} %param.11) | copy-start | bytes 12582916
  57.9 18.1 %all-to-all-start.2 = ((bf16[32,8,256]{2,1,0:T(8,128)(2,1)}), bf16[32,8,256]{2,1,0:T(8,128)(2,1)S(1)}, u32[]{:S(2)}, u32[]{:S(2)}) async-start(bf16[32,8,256]{2,1,0:T(8,128)(2,1)} %get-tuple-element.25), calls=%async_computation.2 | async-start | bytes 262144 | tf_op jit(solution)/shard_map/all_to_all | solution.py:34

commit v7 on v6

--- a/solution.py
+++ b/solution.py
@@ -52,24 +52,33 @@
 
 def split_kernel(experts_hbm, gates_hbm, grad_ref, upper_ref, lower_ref, rows_ref, up_ref, low_ref, experts_ref, gates_ref, in_sems, out_sems):
     count = grad_ref.shape[1] // PIECE
-    pairs = [(grad_ref.at[64 * h : 64 * h + 64], rows_ref.at[h]) for h in range(2)]
+    part = grad_ref.shape[1] // 2
+    parts = [(h, q) for h in range(2) for q in range(2)]
+    pairs = [
+        (
+            grad_ref.at[64 * h : 64 * h + 64, q * part : (q + 1) * part],
+            rows_ref.at[h, :, q * part : (q + 1) * part],
+        )
+        for h, q in parts
+    ]
     pairs += [(experts_hbm, experts_ref), (gates_hbm, gates_ref)]
     arriving = fetch(pairs, in_sems)
-    halves = (up_ref, low_ref)
+    halves, targets = (up_ref, low_ref), (upper_ref, lower_ref)
     end = up_ref.shape[0] - 16
     up_ref[end:, :] = jnp.zeros((16, PIECE), BF16)
-    arriving[2].wait()
-    arriving[3].wait()
+    arriving[4].wait()
+    arriving[5].wait()
     up_ref[end:, 0:128] = meta_rows(experts_ref[...], gates_ref[...])
-    leaving = [
-        pltpu.make_async_copy(up_ref, upper_ref, out_sems.at[0]),
-        pltpu.make_async_copy(low_ref, lower_ref, out_sems.at[1]),
-    ]
-    for half in range(2):
-        arriving[half].wait()
-        for j in range(count):
-            halves[half][64 * j : 64 * j + 64, :] = rows_ref[half, :, j * PIECE : (j + 1) * PIECE]
-        leaving[half].start()
+    leaving = []
+    for i, (h, q) in enumerate(parts):
+        arriving[i].wait()
+        for j in range(q * count // 2, (q + 1) * count // 2):
+            halves[h][64 * j : 64 * j + 64, :] = rows_ref[h, :, j * PIECE : (j + 1) * PIECE]
+        last = halves[h].shape[0] if q else 32 * count
+        at = slice(32 * count * q, last)
+        copy = pltpu.make_async_copy(halves[h].at[at], targets[h].at[at], out_sems.at[i])
+        copy.start()
+        leaving.append(copy)
     for copy in leaving:
         copy.wait()
 
@@ -90,8 +99,8 @@
             pltpu.VMEM((64 * count, PIECE), BF16),
             pltpu.VMEM(experts.shape, experts.dtype),
             pltpu.VMEM(gates.shape, gates.dtype),
+            pltpu.SemaphoreType.DMA((6,)),
             pltpu.SemaphoreType.DMA((4,)),
-            pltpu.SemaphoreType.DMA((2,)),
         ],
         cost_estimate=cost(0, 4 * grad.size),
     )(experts, gates, grad)
@@ -306,9 +315,13 @@
         def _():
             logit_ref[...] = logit.astype(BF16)
 
-    every = jnp.concatenate(found, axis=1)
-    features = jnp.concatenate([tokens_ref[b, 0:128] for b in range(blocks)], axis=0)
-    part = jnp.dot(every, features, preferred_element_type=F32).astype(BF16)
+    part = jnp.zeros((8, tokens_ref.shape[2]), F32)
+    for b in range(0, blocks, 2):
+        pair = jnp.concatenate([tokens_ref[b, 0:128], tokens_ref[b + 1, 0:128]], axis=0)
+        part = part + jnp.dot(
+            jnp.concatenate(found[b : b + 2], axis=1), pair, preferred_element_type=F32
+        )
+    part = part.astype(BF16)
     piece = out_ref.shape[2]
     for j in range(out_ref.shape[0]):
         at = j % (part.shape[1] // piece) * piece

time: 88.2 us -> 88.3 us (level)
  no operation moved by 1% of the time
where the time goes in v7:
time: 88.3 us; the launch traced here: 87.9 us
  blocking collectives  24.8 us (28%)
  starting transfers between devices  23.1 us (26%)
  waiting for transfers between devices  22.3 us (25%)
  Pallas kernels  12.6 us (14%)
  local copies, waits for them, and re-layouts  2.22 us (3%)
  matrix products  1.44 us (2%)
    all_to_all x2, blocking collectives, to_all(): return lax.all_to_all(a, axes, 0, 0, tiled=True)  24.8 us
    ppermute x6, waiting for transfers between devices, shift(): return lax.ppermute(a, 'expert', [(i, (i + step) % n) for i in range(n)])  16.1 us
    all_to_all x2, starting transfers between devices, to_all(): return lax.all_to_all(a, axes, 0, 0, tiled=True)  15.2 us
    ppermute x6, starting transfers between devices, shift(): return lax.ppermute(a, 'expert', [(i, (i + step) % n) for i in range(n)])  7.88 us
    all_to_all x2, waiting for transfers between devices, to_all(): return lax.all_to_all(a, axes, 0, 0, tiled=True)  6.16 us
    pallas_call x1, Pallas kernels, near_sources(): pl.pallas_call(near_kernel, out_shape=[jax.ShapeDtypeStruct((groups, 2, 1...  4.36 us
    pallas_call x1, Pallas kernels, columns(): pl.pallas_call(columns_kernel, out_shape=jax.ShapeDtypeStruct((count, 144...  2.97 us
    unnamed x12, local copies, waits for them, and re-layouts  2.21 us
  transfers between devices with their start and end apart: 8, of which 4 were waited for; matrix products, arithmetic and copies ran while one was open for 2% of the time, Pallas kernels for 11%

profile of v7, /device:TPU:1, one launch (start us, length us, event | category | flops | bytes accessed | tf_op | source)
XLA Modules:
  0.0 87.9 jit_solution(16418808334618999192)
XLA Ops:
  0.6 0.0 copy-start
  0.6 0.0 copy-start.4
  0.7 0.0 copy-start.5
  0.7 0.0 copy-start.3
  0.7 2.2 %shard_map.85 = (bf16[528,512]{1,0:T(8,128)(2,1)}, bf16[512,512]{1,0:T(8,128)(2,1)}) custom-call(s32[2,128]{1,0:T(2,128)} %bitcast.13, bf16[2,128]{1,0:T(2,128)(2,1)} %bitcast.16, bf16[128,4096]{1,0:T(8,128)(2,1)} %own.1), custom_call_target="tpu_custom_call" | custom-call | bytes 2097152 | tf_op jit(solution)/shard_map/pallas_call | solution.py:88
  2.9 2.2 %collective-permute-start = (bf16[528,512]{1,0:T(8,128)(2,1)}, bf16[528,512]{1,0:T(8,128)(2,1)}, u32[]{:S(2)}, u32[]{:S(2)}) collective-permute-start(bf16[528,512]{1,0:T(8,128)(2,1)} %get-tuple-element.20), channel_id=1, source_target_pairs={{0,1},{1,2},{2,3},{3,0},{4,5},{5,6},{6,7},{7,4},{8,9},{9,10},{10,1... | collective-permute-start | bytes 1622024 | tf_op jit(solution)/shard_map/ppermute | solution.py:30
  5.1 1.5 %collective-permute-start.2 = (bf16[512,512]{1,0:T(8,128)(2,1)}, bf16[512,512]{1,0:T(8,128)(2,1)}, u32[]{:S(2)}, u32[]{:S(2)}) collective-permute-start(bf16[512,512]{1,0:T(8,128)(2,1)} %get-tuple-element.19), channel_id=1, source_target_pairs={{0,3},{1,0},{2,1},{3,2},{4,7},{5,4},{6,5},{7,6},{8,11},{9,8},{10,9... | collective-permute-start | bytes 1572872 | tf_op jit(solution)/shard_map/ppermute | solution.py:30
  6.6 3.0 %shard_map.88 = bf16[8,144,512]{2,1,0:T(8,128)(2,1)} custom-call(s32[2,128]{1,0:T(2,128)} %bitcast.14, bf16[2,128]{1,0:T(2,128)(2,1)} %bitcast.17, bf16[128,4096]{1,0:T(8,128)(2,1)} %tokens_ref), custom_call_target="tpu_custom_call" | custom-call | bytes 2097152 | tf_op jit(solution)/shard_map/pallas_call | solution.py:127
  9.6 6.3 %all-to-all-start = ((bf16[8,144,512]{2,1,0:T(8,128)(2,1)}), bf16[8,144,512]{2,1,0:T(8,128)(2,1)S(1)}, u32[]{:S(2)}, u32[]{:S(2)}) async-start(bf16[8,144,512]{2,1,0:T(8,128)(2,1)} %shard_map.88), calls=%async_computation | async-start | bytes 2359296 | tf_op jit(solution)/shard_map/all_to_all | solution.py:34
  15.9 0.6 collective-permute-start.5
  16.5 0.8 collective-permute-start.4
  17.4 0.0 collective-permute-done.lu
  17.4 1.0 %collective-permute-start.1 = (bf16[528,512]{1,0:T(8,128)(2,1)}, bf16[528,512]{1,0:T(8,128)(2,1)S(1)}, u32[]{:S(2)}, u32[]{:S(2)}) collective-permute-start(bf16[528,512]{1,0:T(8,128)(2,1)} %collective-permute-done.lu), channel_id=1, source_target_pairs={{0,1},{1,2},{2,3},{3,0},{4,5},{5,6},{6,7},{7,4},{8,9},{9,10},{10,1... | collective-permute-start | bytes 1622024 | tf_op jit(solution)/shard_map/ppermute | solution.py:30
  18.4 0.0 collective-permute-done.2.rl
  18.4 1.7 %collective-permute-start.3 = (bf16[512,512]{1,0:T(8,128)(2,1)}, bf16[512,512]{1,0:T(8,128)(2,1)S(1)}, u32[]{:S(2)}, u32[]{:S(2)}) collective-permute-start(bf16[512,512]{1,0:T(8,128)(2,1)} %collective-permute-done.2.rl), channel_id=1, source_target_pairs={{0,3},{1,0},{2,1},{3,2},{4,7},{5,4},{6,5},{7,6},{8,11},{9,8},{10,9... | collective-permute-start | bytes 1572872 | tf_op jit(solution)/shard_map/ppermute | solution.py:30
  20.1 11.1 %collective-permute-done.4.ll = bf16[512,512]{1,0:T(8,128)(2,1)S(1)} collective-permute-done((bf16[512,512]{1,0:T(8,128)(2,1)}, bf16[512,512]{1,0:T(8,128)(2,1)S(1)}, u32[]{:S(2)}, u32[]{:S(2)}) %collective-permute-start.4) | collective-permute-done | bytes 524320 | tf_op jit(solution)/shard_map/ppermute | solution.py:30
  31.2 0.0 collective-permute-done.5.ru
  31.2 0.0 copy-done.4
  31.2 0.0 copy-done.5
  31.2 0.0 copy-done.3
  31.2 0.0 copy-start.1
  31.2 2.2 %copy-done.1 = bf16[512,4096]{1,0:T(8,128)(2,1)S(1)} copy-done((bf16[512,4096]{1,0:T(8,128)(2,1)S(1)}, bf16[512,4096]{1,0:T(8,128)(2,1)}, u32[]{:S(2)}) %copy-start.1) | copy-done | bytes 4194328
  33.4 0.0 copy-start.2
  33.4 4.4 %shard_map.86 = (f32[4,2,128]{2,1,0:T(2,128)S(1)}, bf16[2,4,64,4096]{3,2,1,0:T(8,128)(2,1)}) custom-call(s32[2,128]{1,0:T(2,128)S(1)} %bitcast.15, bf16[2,128]{1,0:T(2,128)(2,1)S(1)} %bitcast.18, bf16[2,4,64,4096]{3,2,1,0:T(8,128)(2,1)S(1)} %bitcast.10, bf16[128,4096]{1,0:T(8,128)(2,1)S(1)} %copy-done.3, bf16[528,512]{1,0:T(8,128)(2,1)} %collective-permute-done.lu, ...), custom_call_target="tpu_custom_call" | custom-call | flops 805306368 | bytes 9437184 | tf_op jit(solution)/shard_map/pallas_call | solution.py:231
  37.8 3.9 %collective-permute-done.3.low = bf16[512,512]{1,0:T(8,128)(2,1)S(1)} collective-permute-done((bf16[512,512]{1,0:T(8,128)(2,1)}, bf16[512,512]{1,0:T(8,128)(2,1)S(1)}, u32[]{:S(2)}, u32[]{:S(2)}) %collective-permute-start.3) | collective-permute-done | bytes 524320 | tf_op jit(solution)/shard_map/ppermute | solution.py:30
  41.7 1.1 %collective-permute-done.1.up = bf16[528,512]{1,0:T(8,128)(2,1)S(1)} collective-permute-done((bf16[528,512]{1,0:T(8,128)(2,1)}, bf16[528,512]{1,0:T(8,128)(2,1)S(1)}, u32[]{:S(2)}, u32[]{:S(2)}) %collective-permute-start.1) | collective-permute-done | bytes 540704 | tf_op jit(solution)/shard_map/ppermute | solution.py:30
  42.8 0.0 copy-done.2
  42.8 0.4 shard_map.87
  43.2 0.0 all-to-all-done.tokens_ref
  43.2 13.6 %all_to_all.20.home_ref = f32[32,2,128]{2,1,0:T(2,128)S(1)} all-to-all(f32[32,2,128]{2,1,0:T(2,128)S(1)} %bitcast.12), channel_id=1, replica_groups=mesh['far_z'=4,'near_z'=2,'dp_1'=4,'dp_2'=2,'expert'=4] {'dp_1','dp_2','..., dimensions={0} | all-to-all | bytes 65536 | tf_op jit(solution)/shard_map/all_to_all | solution.py:34
  56.9 1.1 %shard_map.89 = (bf16[8,128]{1,0:T(8,128)(2,1)S(1)}, bf16[32,8,256]{2,1,0:T(8,128)(2,1)}) custom-call(f32[32,2,128]{2,1,0:T(2,128)S(1)} %all_to_all.20.home_ref, bf16[8,144,512]{2,1,0:T(8,128)(2,1)S(1)} %all-to-all-done.tokens_ref), custom_call_target="tpu_custom_call" | custom-call | flops 9437184 | bytes 2359296 | tf_op jit(solution)/shard_map/pallas_call | solution.py:333
  57.9 8.9 %all-to-all-start.2 = ((bf16[32,8,256]{2,1,0:T(8,128)(2,1)}), bf16[32,8,256]{2,1,0:T(8,128)(2,1)S(1)}, u32[]{:S(2)}, u32[]{:S(2)}) async-start(bf16[32,8,256]{2,1,0:T(8,128)(2,1)} %get-tuple-element.25), calls=%async_computation.2 | async-start | bytes 262144 | tf_op jit(solution)/shard_map/all_to_all | solution.py:34
  66.9 1.5 %shard_map.90 = bf16[2,4,64,4096]{3,2,1,0:T(8,128)(2,1)} custom-call(bf16[528,512]{1,0:T(8,128)(2,1)S(1)} %collective-permute-done.1.up, bf16[512,512]{1,0:T(8,128)(2,1)S(1)} %collective-permute-done.3.low, bf16[2,4,64,4096]{3,2,1,0:T(8,128)(2,1)} %get-tuple-element.27._), custom_call_target="tpu_custom_call", output_to_operand_aliasing={{}: (2, {})} | custom-call | flops 134217728 | bytes 2097152 | tf_op jit(solution)/shard_map/pallas_call | solution.py:283
  68.4 0.0 copy-done
  68.4 1.4 %convolution_convert_fusion = bf16[128,4096]{1,0:T(8,128)(2,1)} fusion(bf16[8,128]{1,0:T(8,128)(2,1)S(1)} %get-tuple-element.26, bf16[8,4096]{1,0:T(8,128)(2,1)S(1)} %copy-done), kind=kOutput, calls=%fused_computation | convolution fusion | flops 8912896 | bytes 1116160 | tf_op jit(solution)/shard_map/dot_general | solution.py:373
  69.9 6.2 %all-to-all-done.2 = bf16[32,8,256]{2,1,0:T(8,128)(2,1)S(1)} async-done(((bf16[32,8,256]{2,1,0:T(8,128)(2,1)}), bf16[32,8,256]{2,1,0:T(8,128)(2,1)S(1)}, u32[]{:S(2)}, u32[]{:S(2)}) %all-to-all-start.2) | async-done | bytes 131104 | tf_op jit(solution)/shard_map/all_to_all | solution.py:34
  76.1 11.1 %all_to_all.21 = bf16[16,8,256]{2,1,0:T(8,128)(2,1)S(1)} all-to-all(bf16[16,8,256]{2,1,0:T(8,128)(2,1)S(1)} %broadcast_in_dim.3), channel_id=1, replica_groups=mesh['far_z'=4,'near_z'=2,'dp_1'=4,'dp_2'=2,'expert'=4] {'dp_1','dp_2','..., dimensions={0} | all-to-all | bytes 131072 | tf_op jit(solution)/shard_map/all_to_all | solution.py:34
  87.2 0.7 reshape.28
  (3 shorter events, 0.0 us)
Async XLA Ops:
  0.6 67.8 %copy-start = (bf16[8,4096]{1,0:T(8,128)(2,1)S(1)}, bf16[8,4096]{1,0:T(8,128)(2,1)}, u32[]{:S(2)}) copy-start(bf16[8,4096]{1,0:T(8,128)(2,1)} %param.10) | copy-start | bytes 196612
  0.6 30.5 %copy-start.4 = (s32[128,2]{0,1:T(2,128)S(1)}, s32[128,2]{0,1:T(2,128)}, u32[]{:S(2)}) copy-start(s32[128,2]{0,1:T(2,128)} %param.8) | copy-start | bytes 3076
  0.7 30.5 %copy-start.5 = (bf16[128,2]{0,1:T(2,128)(2,1)S(1)}, bf16[128,2]{0,1:T(2,128)(2,1)}, u32[]{:S(2)}) copy-start(bf16[128,2]{0,1:T(2,128)(2,1)} %param.9) | copy-start | bytes 1540
  0.7 30.5 %copy-start.3 = (bf16[128,4096]{1,0:T(8,128)(2,1)S(1)}, bf16[128,4096]{1,0:T(8,128)(2,1)}, u32[]{:S(2)}) copy-start(bf16[128,4096]{1,0:T(8,128)(2,1)} %own.1) | copy-start | bytes 3145732
  2.9 14.5 %collective-permute-start = (bf16[528,512]{1,0:T(8,128)(2,1)}, bf16[528,512]{1,0:T(8,128)(2,1)}, u32[]{:S(2)}, u32[]{:S(2)}) collective-permute-start(bf16[528,512]{1,0:T(8,128)(2,1)} %get-tuple-element.20), channel_id=1, source_target_pairs={{0,1},{1,2},{2,3},{3,0},{4,5},{5,6},{6,7},{7,4},{8,9},{9,10},{10,1... | collective-permute-start | bytes 1622024 | tf_op jit(solution)/shard_map/ppermute | solution.py:30
  5.1 13.3 %collective-permute-start.2 = (bf16[512,512]{1,0:T(8,128)(2,1)}, bf16[512,512]{1,0:T(8,128)(2,1)}, u32[]{:S(2)}, u32[]{:S(2)}) collective-permute-start(bf16[512,512]{1,0:T(8,128)(2,1)} %get-tuple-element.19), channel_id=1, source_target_pairs={{0,3},{1,0},{2,1},{3,2},{4,7},{5,4},{6,5},{7,6},{8,11},{9,8},{10,9... | collective-permute-start | bytes 1572872 | tf_op jit(solution)/shard_map/ppermute | solution.py:30
  9.6 33.6 %all-to-all-start = ((bf16[8,144,512]{2,1,0:T(8,128)(2,1)}), bf16[8,144,512]{2,1,0:T(8,128)(2,1)S(1)}, u32[]{:S(2)}, u32[]{:S(2)}) async-start(bf16[8,144,512]{2,1,0:T(8,128)(2,1)} %shard_map.88), calls=%async_computation | async-start | bytes 2359296 | tf_op jit(solution)/shard_map/all_to_all | solution.py:34
  15.9 15.3 %collective-permute-start.5 = (bf16[528,512]{1,0:T(8,128)(2,1)}, bf16[528,512]{1,0:T(8,128)(2,1)S(1)}, u32[]{:S(2)}, u32[]{:S(2)}) collective-permute-start(bf16[528,512]{1,0:T(8,128)(2,1)} %get-tuple-element.20), channel_id=1, source_target_pairs={{0,3},{1,0},{2,1},{3,2},{4,7},{5,4},{6,5},{7,6},{8,11},{9,8},{10,9... | collective-permute-start | bytes 1622024 | tf_op jit(solution)/shard_map/ppermute | solution.py:30
  16.5 14.7 %collective-permute-start.4 = (bf16[512,512]{1,0:T(8,128)(2,1)}, bf16[512,512]{1,0:T(8,128)(2,1)S(1)}, u32[]{:S(2)}, u32[]{:S(2)}) collective-permute-start(bf16[512,512]{1,0:T(8,128)(2,1)} %get-tuple-element.19), channel_id=1, source_target_pairs={{0,1},{1,2},{2,3},{3,0},{4,5},{5,6},{6,7},{7,4},{8,9},{9,10},{10,1... | collective-permute-start | bytes 1572872 | tf_op jit(solution)/shard_map/ppermute | solution.py:30
  17.4 25.4 %collective-permute-start.1 = (bf16[528,512]{1,0:T(8,128)(2,1)}, bf16[528,512]{1,0:T(8,128)(2,1)S(1)}, u32[]{:S(2)}, u32[]{:S(2)}) collective-permute-start(bf16[528,512]{1,0:T(8,128)(2,1)} %collective-permute-done.lu), channel_id=1, source_target_pairs={{0,1},{1,2},{2,3},{3,0},{4,5},{5,6},{6,7},{7,4},{8,9},{9,10},{10,1... | collective-permute-start | bytes 1622024 | tf_op jit(solution)/shard_map/ppermute | solution.py:30
  18.4 23.3 %collective-permute-start.3 = (bf16[512,512]{1,0:T(8,128)(2,1)}, bf16[512,512]{1,0:T(8,128)(2,1)S(1)}, u32[]{:S(2)}, u32[]{:S(2)}) collective-permute-start(bf16[512,512]{1,0:T(8,128)(2,1)} %collective-permute-done.2.rl), channel_id=1, source_target_pairs={{0,3},{1,0},{2,1},{3,2},{4,7},{5,4},{6,5},{7,6},{8,11},{9,8},{10,9... | collective-permute-start | bytes 1572872 | tf_op jit(solution)/shard_map/ppermute | solution.py:30
  31.2 2.2 %copy-start.1 = (bf16[512,4096]{1,0:T(8,128)(2,1)S(1)}, bf16[512,4096]{1,0:T(8,128)(2,1)}, u32[]{:S(2)}) copy-start(bf16[512,4096]{1,0:T(8,128)(2,1)} %param.11) | copy-start | bytes 12582916
  33.4 9.4 %copy-start.2 = (bf16[512,4096]{1,0:T(8,128)(2,1)S(1)}, bf16[512,4096]{1,0:T(8,128)(2,1)}, u32[]{:S(2)}) copy-start(bf16[512,4096]{1,0:T(8,128)(2,1)} %param.11) | copy-start | bytes 12582916
  57.9 18.1 %all-to-all-start.2 = ((bf16[32,8,256]{2,1,0:T(8,128)(2,1)}), bf16[32,8,256]{2,1,0:T(8,128)(2,1)S(1)}, u32[]{:S(2)}, u32[]{:S(2)}) async-start(bf16[32,8,256]{2,1,0:T(8,128)(2,1)} %get-tuple-element.25), calls=%async_computation.2 | async-start | bytes 262144 | tf_op jit(solution)/shard_map/all_to_all | solution.py:34
